TPU v7x, 32 devices: a whole 2x2x4 slice. The times are simulated.
32 devices in a mesh: row: 4 (over z), rep: 8 (over y, x, core).
Axes of the slice: x: 2, y: 2, z: 4, core: 2. Of those that a mesh axis runs over, the one named last changes fastest.
Arguments:
- features: bfloat16 [8192, 256], P('row'), may hold values from 0 to 2
- self_weight: bfloat16 [256, 256], replicated, may hold values from -0.375 to 0.375
- neigh_weight: bfloat16 [256, 256], replicated, may hold values from -0.375 to 0.375
- out_bias: float32 [256], replicated, may hold values from -4 to 4
- tile_masks: int32 [8192, 32, 128], P('row', 'rep'), may hold values 0 or 1
- tile_live: int32 [64, 32], P('row', 'rep'), may hold values from 0 to 1, as said below
- tile_columns: int32 [64, 32], P('row', 'rep'), may hold values from 0 to 1
- node_degree: int32 [8192], P(('row', 'rep')), may hold values from 32 to 127
- cotangent: bfloat16 [8192, 256], P(('row', 'rep')), may hold values from -6 to 6
Outputs:
- hidden_out: bfloat16 [8192, 256], P(('row', 'rep'))
- grad_features: bfloat16 [8192, 256], P(('row', 'rep'))
- grad_self: float32 [256, 256], replicated
- grad_neigh: float32 [256, 256], replicated
- grad_bias: float32 [256], replicated
Inputs may be any that keep to these rules, and one draw needn't show every extreme that they name: `tile_masks`: an edge bit; bits of slots without a tile are not read. `tile_live`: 1 where the slot holds a tile. `tile_columns`: the covered block among the 2 blocks of that column set and panel.
All inputs are finite; a program needn't handle non-finite values. No bound on the sum of `tile_masks` on one device may be relied on, other than what follows from the above.
Results may differ from a plain program's by a relative error of at most 0.0053.
Values may be sent and summed in bfloat16 or wider, within the bound.
No kernel may reach another device: no remote copies, remote signals or barrier semaphores. Data moves between devices by JAX's collectives and lax.ppermute only.
A program may use at most 128 MiB of HBM per device.

v0:
```python
import math

import jax
import jax.numpy as jnp
from jax import lax
from jax.sharding import PartitionSpec as P


def activation(values):
    return jax.nn.gelu(values, approximate=True)


def per_device(
    features,
    self_weight,
    neigh_weight,
    out_bias,
    tile_masks,
    tile_live,
    tile_columns,
    node_degree,
    cotangent,
):
    row_devices = lax.axis_size("row")
    rep_devices = lax.axis_size("rep")
    panel_rows, width = features.shape
    share_rows = node_degree.shape[0]
    panel_count = tile_masks.shape[1]
    tile_size = tile_masks.shape[2]
    block_rows = panel_rows // tile_size
    set_blocks = share_rows // tile_size
    column_rows = panel_count * share_rows
    contract_first = (((0,), (0,)), ((), ()))
    contract_second = (((1,), (1,)), ((), ()))
    block_ids = jnp.arange(set_blocks, dtype=jnp.int32)
    selected = (tile_columns[:, :, None] == block_ids[None, None, :]) & (tile_live[:, :, None] != 0)
    keeper = selected.astype(jnp.bfloat16)
    dense = tile_masks.reshape(block_rows, tile_size, panel_count, 1, tile_size).astype(
        jnp.bfloat16
    )
    dense = (dense * keeper[:, None, :, :, None]).reshape(panel_rows, column_rows)
    own = lax.dynamic_slice_in_dim(features, lax.axis_index("rep") * share_rows, share_rows, 0)
    strip = dense
    partial_sums = jnp.dot(
        strip, lax.all_gather(own, "row", axis=0, tiled=True), preferred_element_type=jnp.float32
    )
    agg_sum = lax.psum_scatter(partial_sums, "rep", scatter_dimension=0, tiled=True)
    degree = node_degree.astype(jnp.float32)[:, None]
    mean = (agg_sum / degree).astype(jnp.bfloat16)
    pre = (
        jnp.dot(own, self_weight, preferred_element_type=jnp.float32)
        + jnp.dot(mean, neigh_weight, preferred_element_type=jnp.float32)
        + out_bias
    )
    result, pull = jax.vjp(activation, pre)
    hidden_out = result.astype(jnp.bfloat16)
    dpre = pull(cotangent.astype(jnp.float32))[0]
    dpre_b = dpre.astype(jnp.bfloat16)
    scale = 1.0 / math.sqrt(share_rows * row_devices * rep_devices)
    self_term = (
        lax.dot_general(own, dpre_b, contract_first, preferred_element_type=jnp.float32) * scale
    )
    neigh_term = (
        lax.dot_general(mean, dpre_b, contract_first, preferred_element_type=jnp.float32) * scale
    )
    bias_term = jnp.sum(dpre, axis=0) * scale
    grad_self, grad_neigh, grad_bias = lax.psum((self_term, neigh_term, bias_term), ("row", "rep"))
    message = (
        lax.dot_general(dpre_b, neigh_weight, contract_second, preferred_element_type=jnp.float32)
        / degree
    ).astype(jnp.bfloat16)
    direct = lax.dot_general(
        dpre_b, self_weight, contract_second, preferred_element_type=jnp.float32
    )
    strip = dense
    partial_back = lax.dot_general(
        strip,
        lax.all_gather(message, "rep", axis=0, tiled=True),
        contract_first,
        preferred_element_type=jnp.float32,
    )
    spread = lax.psum_scatter(
        partial_back.astype(jnp.bfloat16), "row", scatter_dimension=0, tiled=True
    ).astype(jnp.float32)
    grad_features = (direct + spread).astype(jnp.bfloat16)
    return (hidden_out, grad_features, grad_self, grad_neigh, grad_bias)


def solution(mesh):
    return jax.shard_map(
        per_device,
        mesh=mesh,
        in_specs=(
            P("row", None),
            P(),
            P(),
            P(),
            P("row", "rep", None),
            P("row", "rep"),
            P("row", "rep"),
            P(("row", "rep")),
            P(("row", "rep"), None),
        ),
        out_specs=(P(("row", "rep"), None), P(("row", "rep"), None), P(), P(), P()),
        check_vma=False,
    )
```

profile of v0, /device:TPU:0, one launch (start us, length us, event | category | flops | bytes accessed | tf_op | source)
XLA Modules:
  0.0 286.2 jit_solution(14548331133038136443)
XLA Ops:
  7.2 0.0 copy-start
  7.2 0.0 reduce-scatter.3.cloned.1.call-start
  7.2 0.8 copy.14
  8.1 0.7 broadcast_compare_fusion
  8.8 0.1 copy.15
  8.9 2.6 convert_element_type.45
  11.5 0.1 fusion.13
  11.6 5.6 %broadcast_multiply_fusion = bf16[16,128,4,2,128]{4,3,2,1,0:T(2,128)(2,1)} fusion(bf16[16,4,2]{2,1,0:T(4,128)(2,1)S(1)} %fusion.13, bf16[16,128,4,128]{3,2,1,0:T(4,128)(2,1)S(1)} %bitcast.15), kind=kLoop, calls=%fused_computation | loop fusion | flops 2097152 | bytes 6291712 | tf_op jit(solution)/shard_map/mul | solution.py:41
  17.2 7.7 %mul.80 = bf16[2048,1024]{1,0:T(8,128)(2,1)} reshape(bf16[16,128,4,2,128]{4,3,2,1,0:T(2,128)(2,1)} %broadcast_multiply_fusion) | data formatting | bytes 8388608 | tf_op jit(solution)/shard_map/mul | solution.py:41
  24.8 0.0 copy-done
  24.9 17.4 %all_gather.6 = bf16[1024,256]{1,0:T(8,128)(2,1)S(1)} all-gather(bf16[256,256]{1,0:T(8,128)(2,1)S(1)} %constant_dynamic-slice_fusion), channel_id=1, replica_groups=mesh['row'=4,'rep'=8] {'row'}, dimensions={0}, use_global_device_ids=true | all-gather | bytes 655360 | tf_op jit(solution)/shard_map/all_gather | solution.py:45
  42.2 0.0 copy-start.2
  42.2 0.0 copy-start.1
  42.2 0.0 copy-start.4
  42.2 0.0 copy-start.5
  42.2 0.0 copy-start.6
  42.2 4.8 %fusion.17 = f32[2048,256]{1,0:T(8,128)} fusion(bf16[2048,1024]{1,0:T(8,128)(2,1)} %mul.80, bf16[1024,256]{1,0:T(8,128)(2,1)S(1)} %all_gather.6), kind=kOutput, calls=%fused_computation.33 | convolution fusion | flops 1073741824 | bytes 6815744 | tf_op jit(solution)/shard_map/dot_general | solution.py:44
  47.1 0.0 reduce-scatter.3.cloned.1.call-update
  47.1 0.0 all-gather.2.cloned.1.call-start
  47.1 0.0 copy-done.2
  47.1 0.0 copy-done.1
  47.2 0.2 fusion.16
  47.3 42.9 %reduce-scatter.3.cloned.1.call-done = f32[256,256]{1,0:T(8,128)} async-done(((f32[2048,256]{1,0:T(8,128)}), f32[256,256]{1,0:T(8,128)}) %reduce-scatter.3.cloned.1.call-update) | async-done | bytes 262160 | tf_op jit(solution)/shard_map/reduce_scatter | solution.py:47
  90.2 0.0 copy-done.4
  90.2 0.0 copy-done.5
  90.2 0.0 copy-done.6
  90.2 2.0 fusion.14
  92.3 0.9 fusion.2
  93.1 0.0 all-gather.2.cloned.1.call-update
  93.2 0.0 copy-start.3
  93.2 0.0 reduce-scatter.5.cloned.1.call-start
  93.2 23.6 %all-gather.2.cloned.1.call-done = bf16[2048,256]{1,0:T(8,128)(2,1)} async-done(((bf16[256,256]{1,0:T(8,128)(2,1)}), bf16[2048,256]{1,0:T(8,128)(2,1)}) %all-gather.2.cloned.1.call-update) | async-done | bytes 1048592 | tf_op jit(solution)/shard_map/all_gather | solution.py:78
  116.8 4.6 %convolution_convert_fusion = bf16[1024,256]{1,0:T(8,128)(2,1)} fusion(bf16[2048,1024]{1,0:T(8,128)(2,1)} %mul.80, bf16[2048,256]{1,0:T(8,128)(2,1)} %all-gather.2.cloned.1.call-done), kind=kOutput, calls=%fused_computation.1 | convolution fusion | flops 1074003968 | bytes 5767168 | tf_op jit(solution)/shard_map/dot_general | solution.py:76
  121.4 0.0 reduce-scatter.5.cloned.1.call-update
  121.4 0.0 all-reduce.3.cloned.1.call-start
  121.5 0.9 convolution_multiply_fusion.1
  122.4 0.0 copy-done.3
  122.4 1.0 convolution_multiply_fusion
  123.4 0.0 all-reduce.3.cloned.1.call-update
  123.5 39.4 %psum.23 = f32[256]{0:T(256)} all-reduce(f32[256]{0:T(256)S(1)} %broadcast_multiply_fusion.1), channel_id=1, replica_groups=mesh['row'=4,'rep'=8] {'row','rep'}, use_global_device_ids=true, to_apply=%region_5.0 | all-reduce | flops 256 | bytes 2048 | tf_op jit(solution)/shard_map/psum | solution.py:67
  162.9 0.0 reduce-scatter.5.cloned.1.call-done
  162.9 1.8 fusion.1
  164.7 111.7 %all-reduce.3.cloned.1.call-done = (f32[256,256]{1,0:T(8,128)}, f32[256,256]{1,0:T(8,128)}) async-done(((f32[256,256]{1,0:T(8,128)}, f32[256,256]{1,0:T(8,128)}), (f32[256,256]{1,0:T(8,128)}, f32[256,256]{1,0:T(8,128)})) %all-reduce.3.cloned.1.call-update) | async-done | bytes 524304 | tf_op jit(solution)/shard_map/psum | solution.py:67
  276.4 1.7 copy.18
  278.0 1.7 copy.19
  (3 shorter events, 0.0 us)
Async XLA Ops:
  7.2 17.7 %copy-start = (bf16[2048,256]{1,0:T(8,128)(2,1)S(1)}, bf16[2048,256]{1,0:T(8,128)(2,1)}, u32[]{:S(2)}) copy-start(bf16[2048,256]{1,0:T(8,128)(2,1)} %param.9) | copy-start | bytes 3145732
  7.2 83.0 %reduce-scatter.3.cloned.1.call-start = ((), (), s32[]{:S(2)}) async-start(), calls=%async_computation.2 | async-start | bytes 2359296 | tf_op jit(solution)/shard_map/reduce_scatter | solution.py:47
  42.2 4.9 %copy-start.2 = (s32[256]{0:T(256)S(1)}, s32[256]{0:T(256)}, u32[]{:S(2)}) copy-start(s32[256]{0:T(256)} %param.16) | copy-start | bytes 3076
  42.2 4.9 %copy-start.1 = (bf16[256,256]{1,0:T(8,128)(2,1)S(1)}, bf16[256,256]{1,0:T(8,128)(2,1)}, u32[]{:S(2)}) copy-start(bf16[256,256]{1,0:T(8,128)(2,1)} %param.10) | copy-start | bytes 393220
  42.2 48.0 %copy-start.4 = (bf16[256,256]{1,0:T(8,128)(2,1)S(1)}, bf16[256,256]{1,0:T(8,128)(2,1)}, u32[]{:S(2)}) copy-start(bf16[256,256]{1,0:T(8,128)(2,1)} %param.17) | copy-start | bytes 393220
  42.2 48.0 %copy-start.5 = (bf16[256,256]{1,0:T(8,128)(2,1)S(1)}, bf16[256,256]{1,0:T(8,128)(2,1)}, u32[]{:S(2)}) copy-start(bf16[256,256]{1,0:T(8,128)(2,1)} %param.11) | copy-start | bytes 393220
  42.2 48.0 %copy-start.6 = (f32[256]{0:T(256)S(1)}, f32[256]{0:T(256)}, u32[]{:S(2)}) copy-start(f32[256]{0:T(256)} %param.12) | copy-start | bytes 3076
  47.1 69.7 %all-gather.2.cloned.1.call-start = ((), (), s32[]{:S(2)}) async-start(), calls=%async_computation.3 | async-start | bytes 1179648 | tf_op jit(solution)/shard_map/all_gather | solution.py:78
  93.2 29.3 %copy-start.3 = (f32[256,256]{1,0:T(8,128)S(1)}, f32[256,256]{1,0:T(8,128)}, u32[]{:S(2)}) copy-start(f32[256,256]{1,0:T(8,128)} %reduce-scatter.3.cloned.1.call-done) | copy-start | bytes 786436
  93.2 69.8 %reduce-scatter.5.cloned.1.call-start = ((), (), s32[]{:S(2)}) async-start(), calls=%async_computation.4 | async-start | bytes 655360 | tf_op jit(solution)/shard_map/reduce_scatter | solution.py:82
  121.4 154.9 %all-reduce.3.cloned.1.call-start = ((), (), s32[]{:S(2)}) async-start(), calls=%async_computation.5 | async-start | bytes 1048576 | tf_op jit(solution)/shard_map/psum | solution.py:67
Sparse Core Ops, SparseCore 0:
  47.2 42.9 reduce-scatter.2
  93.3 23.4 all-gather.1
  121.6 21.6 reduce-scatter.4
  150.0 126.2 all-reduce.2
where the time goes:
time: 287 us; the launch traced here: 286 us
  waiting for transfers between devices  178 us (62%)
  blocking collectives  56.8 us (20%)
  matrix products  16.3 us (6%)
  between operations  13.9 us (5%)
  local copies, waits for them, and re-layouts  12 us (4%)
  other arithmetic  8.98 us (3%)
    psum x1, waiting for transfers between devices, per_device(): lax.psum((self_term, neigh_term, bias_term), ('row', 'rep'))  112 us
    reduce_scatter x1, waiting for transfers between devices, per_device(): lax.psum_scatter(partial_sums, 'rep', scatter_dimension=0, tiled=True)  42.9 us
    psum x1, blocking collectives, per_device(): lax.psum((self_term, neigh_term, bias_term), ('row', 'rep'))  39.4 us
    all_gather x1, waiting for transfers between devices, per_device(): lax.all_gather(message, 'rep', axis=0, tiled=True)  23.6 us
    all_gather x1, blocking collectives, per_device(): lax.all_gather(own, 'row', axis=0, tiled=True)  17.4 us
    mul x1, local copies, waits for them, and re-layouts, per_device(): dense * keeper[:, None, :, :, None]  7.68 us
  transfers between devices with their start and end apart: 4, of which 3 were waited for; matrix products, arithmetic and copies ran while one was open for 1% of the time, Pallas kernels for 0%

commit v1 on v0

v1 whole, which is shorter than its diff:
```python
import functools
import math

import jax
import jax.numpy as jnp
from jax import lax
from jax.experimental import pallas as pl
from jax.experimental.pallas import tpu as pltpu
from jax.sharding import PartitionSpec as P

BF16 = jnp.bfloat16
F32 = jnp.float32
BIAS_ROWS = 16
VMEM_LIMIT = 40 * 1024 * 1024
CONTRACT_FIRST = (((0,), (0,)), ((), ()))
CONTRACT_SECOND = (((1,), (1,)), ((), ()))
GELU_A = math.sqrt(2.0 / math.pi)
GELU_B = 0.044715


def dot(a, b, dims=(((1,), (0,)), ((), ()))):
    return lax.dot_general(a, b, dims, preferred_element_type=F32)


def params():
    return pltpu.CompilerParams(vmem_limit_bytes=VMEM_LIMIT)


def cost(flops, bytes_accessed):
    return pl.CostEstimate(flops=flops, bytes_accessed=bytes_accessed, transcendentals=0)


def whole(n):
    return [pl.BlockSpec(memory_space=pltpu.VMEM)] * n


def xor_permute(value, axis, k):
    return lax.ppermute(value, axis, [(i, i ^ k) for i in range(lax.axis_size(axis))])


def strip_kernel(panels, blocks, tile, live_ref, cols_ref, mask_ref, dense_ref, flip_ref):
    step = pl.program_id(0)
    for j in range(blocks):
        i = step * blocks + j
        for s in range(panels):
            bits = mask_ref[pl.ds(j * tile * panels + s, tile, stride=panels), :].astype(F32)
            turned = bits.T
            live = live_ref[s, i] != 0
            col = cols_ref[s, i]
            for b in range(blocks):
                keep = jnp.where(live & (col == b), 1.0, 0.0).astype(F32)
                at = (s * blocks + b) * tile
                dense_ref[j * tile : (j + 1) * tile, at : at + tile] = (bits * keep).astype(BF16)
                flip_ref[0, at : at + tile, j * tile : (j + 1) * tile] = (turned * keep).astype(BF16)


def build_strip(masks, live, cols, panels, blocks, tile, steps):
    share = blocks * tile
    width = panels * share
    return pl.pallas_call(
        functools.partial(strip_kernel, panels, blocks, tile),
        grid=(steps,),
        in_specs=[
            pl.BlockSpec(memory_space=pltpu.SMEM),
            pl.BlockSpec(memory_space=pltpu.SMEM),
            pl.BlockSpec((share * panels, tile), lambda c: (c, 0)),
        ],
        out_specs=[
            pl.BlockSpec((share, width), lambda c: (c, 0)),
            pl.BlockSpec((1, width, share), lambda c: (c, 0, 0)),
        ],
        out_shape=[
            jax.ShapeDtypeStruct((steps * share, width), BF16),
            jax.ShapeDtypeStruct((steps, width, share), BF16),
        ],
        compiler_params=params(),
        name="build_strip",
    )(live, cols, masks)


def stack_features(ids_ref, feature_refs, held):
    share = feature_refs[0].shape[0]
    for k, ref in enumerate(feature_refs):
        at = pl.multiple_of((ids_ref[1] ^ k) * share, share)
        held[pl.ds(at, share), :] = ref[...]


def sibling_sums_kernel(n, ids_ref, dense_ref, *refs):
    feature_refs, out_ref, held = refs[:n], refs[n], refs[n + 1]

    @pl.when(pl.program_id(0) == 0)
    def _():
        stack_features(ids_ref, feature_refs, held)

    out_ref[...] = dot(dense_ref[...], held[...]).astype(BF16)


def chip_sums_kernel(n, m, ids_ref, dense_ref, recv_ref, *refs):
    feature_refs, own_ref, out_refs, held = refs[:n], refs[n], refs[n + 1 : n + m], refs[n + m]
    step = pl.program_id(0)

    @pl.when(step == 0)
    def _():
        stack_features(ids_ref, feature_refs, held)

    total = dot(dense_ref[...], held[...]) + recv_ref[...].astype(F32)

    @pl.when(step == 0)
    def _():
        own_ref[...] = total

    for q in range(1, m):

        @pl.when(step == q)
        def _(q=q):
            out_refs[q - 1][...] = total.astype(BF16)


def sibling_sums(ids, dense, features, chips):
    share, width = features[0].shape
    n = len(features)
    return pl.pallas_call(
        functools.partial(sibling_sums_kernel, n),
        grid_spec=pltpu.PrefetchScalarGridSpec(
            num_scalar_prefetch=1,
            grid=(chips,),
            in_specs=[pl.BlockSpec((share, n * share), lambda q, ids: ((ids[0] ^ 1) ^ (2 * q), 0))]
            + [pl.BlockSpec((share, width), lambda q, ids: (0, 0))] * n,
            out_specs=pl.BlockSpec((share, width), lambda q, ids: (q, 0)),
            scratch_shapes=[pltpu.VMEM((n * share, width), BF16)],
        ),
        out_shape=jax.ShapeDtypeStruct((chips * share, width), BF16),
        compiler_params=params(),
        name="sibling_sums",
    )(ids, dense, *features)


def chip_sums(ids, dense, recv, features, chips):
    share, width = features[0].shape
    n = len(features)
    block = jax.ShapeDtypeStruct((share, width), BF16)
    fixed = pl.BlockSpec((share, width), lambda q, ids: (0, 0))
    return pl.pallas_call(
        functools.partial(chip_sums_kernel, n, chips),
        grid_spec=pltpu.PrefetchScalarGridSpec(
            num_scalar_prefetch=1,
            grid=(chips,),
            in_specs=[
                pl.BlockSpec((share, n * share), lambda q, ids: (ids[0] ^ (2 * q), 0)),
                pl.BlockSpec((share, width), lambda q, ids: (q, 0)),
            ]
            + [fixed] * n,
            out_specs=[fixed] * chips,
            scratch_shapes=[pltpu.VMEM((n * share, width), BF16)],
        ),
        out_shape=[jax.ShapeDtypeStruct((share, width), F32)] + [block] * (chips - 1),
        compiler_params=params(),
        name="chip_sums",
    )(ids, dense, recv, *features)


def rows_kernel(m, own_ref, ws_ref, wn_ref, bias_ref, deg_ref, cot_ref, agg_ref, *refs):
    recv_refs = refs[: m - 1]
    hidden_ref, dpre_ref, mean_ref, msg_ref, dbias_ref = refs[m - 1 :]
    agg = agg_ref[...]
    for ref in recv_refs:
        agg = agg + ref[...].astype(F32)
    deg = deg_ref[...]
    mean = (agg / deg).astype(BF16)
    mean_ref[...] = mean
    v = dot(own_ref[...], ws_ref[...]) + dot(mean, wn_ref[...]) + bias_ref[...]
    t = jnp.tanh(GELU_A * (v + GELU_B * (v * v * v)))
    hidden_ref[...] = (0.5 * v * (1.0 + t)).astype(BF16)
    slope = 0.5 * (1.0 + t) + 0.5 * v * (1.0 - t * t) * (GELU_A * (1.0 + 3.0 * GELU_B * v * v))
    dpre = cot_ref[...].astype(F32) * slope
    dpre_b = dpre.astype(BF16)
    dpre_ref[...] = dpre_b
    msg_ref[...] = (dot(dpre_b, wn_ref[...], CONTRACT_SECOND) / deg).astype(BF16)
    dbias_ref[...] = jnp.sum(dpre, axis=0, keepdims=True)


def rows_step(own, ws, wn, bias, deg, cot, agg, recvs):
    share, width = own.shape
    block = jax.ShapeDtypeStruct((share, width), BF16)
    m = len(recvs) + 1
    return pl.pallas_call(
        functools.partial(rows_kernel, m),
        in_specs=whole(7 + m - 1),
        out_specs=whole(5),
        out_shape=[block, block, block, block, jax.ShapeDtypeStruct((1, width), F32)],
        compiler_params=params(),
        name="rows_step",
    )(own, ws, wn, bias, deg, cot, agg, *recvs)


def local_grads_kernel(chips, scale, ids_ref, own_ref, mean_ref, dpre_ref, dbias_ref, away_ref, keep_ref, held):
    width = own_ref.shape[1]
    piece = width // (2 * chips)
    rows = 2 * piece + BIAS_ROWS
    dpre = dpre_ref[...]
    held[0:width, :] = dot(own_ref[...], dpre, CONTRACT_FIRST) * scale
    held[width : 2 * width, :] = dot(mean_ref[...], dpre, CONTRACT_FIRST) * scale
    dbias = jnp.broadcast_to(dbias_ref[...] * scale, (BIAS_ROWS, dbias_ref.shape[1]))
    for out_ref, base in ((away_ref, ids_ref[0] ^ 1), (keep_ref, ids_ref[0])):
        for q in range(chips):
            at = pl.multiple_of((base ^ (2 * q)) * piece, piece)
            out_ref[q * rows : q * rows + piece, :] = held[pl.ds(at, piece), :]
            out_ref[q * rows + piece : q * rows + 2 * piece, :] = held[pl.ds(width + at, piece), :]
            out_ref[q * rows + 2 * piece : (q + 1) * rows, :] = dbias


def local_grads(ids, own, mean, dpre, dbias, chips, scale):
    width = own.shape[1]
    rows = 2 * (width // (2 * chips)) + BIAS_ROWS
    out = jax.ShapeDtypeStruct((chips * rows, width), F32)
    return pl.pallas_call(
        functools.partial(local_grads_kernel, chips, scale),
        in_specs=[pl.BlockSpec(memory_space=pltpu.SMEM)] + whole(4),
        out_specs=whole(2),
        out_shape=[out, out],
        scratch_shapes=[pltpu.VMEM((2 * width, width), F32)],
        compiler_params=params(),
        name="local_grads",
    )(ids, own, mean, dpre, dbias)


def store_shard(out_ref, total):
    rows = total.shape[0]
    half = BIAS_ROWS // 2
    high = total.astype(BF16)
    tail = total[rows - BIAS_ROWS :, :]
    tail_high = tail.astype(BF16).astype(F32)
    index = lax.broadcasted_iota(jnp.int32, tail.shape, 0)
    mixed = jnp.where(index < half, tail_high, tail - tail_high)
    out_ref[0 : rows - BIAS_ROWS, :] = high[0 : rows - BIAS_ROWS, :]
    out_ref[rows - BIAS_ROWS :, :] = mixed.astype(BF16)


def load_shard(ref):
    value = ref[...].astype(F32)
    rows = value.shape[0]
    half = BIAS_ROWS // 2
    line = value[rows - BIAS_ROWS : rows - BIAS_ROWS + 1, :] + value[rows - half : rows - half + 1, :]
    return jnp.concatenate(
        [value[: rows - BIAS_ROWS, :], jnp.broadcast_to(line, (BIAS_ROWS, value.shape[1]))], axis=0
    )


def pair_grads_kernel(chips, keep_ref, recv_ref, own_ref, *out_refs):
    rows = own_ref.shape[0]
    own_ref[...] = keep_ref[0:rows, :] + recv_ref[0:rows, :]
    for q in range(1, chips):
        at = slice(q * rows, (q + 1) * rows)
        store_shard(out_refs[q - 1], keep_ref[at, :] + recv_ref[at, :])


def pair_grads(keep, recv, chips):
    rows, width = keep.shape[0] // chips, keep.shape[1]
    block = jax.ShapeDtypeStruct((rows, width), BF16)
    return pl.pallas_call(
        functools.partial(pair_grads_kernel, chips),
        in_specs=whole(2),
        out_specs=whole(chips),
        out_shape=[jax.ShapeDtypeStruct((rows, width), F32)] + [block] * (chips - 1),
        compiler_params=params(),
        name="pair_grads",
    )(keep, recv)


def panel_grads_kernel(n, own_ref, *refs):
    total = own_ref[...]
    for ref in refs[:n]:
        total = total + load_shard(ref)
    refs[n][...] = total
    store_shard(refs[n + 1], total)


def panel_grads(own, recvs):
    rows, width = own.shape
    return pl.pallas_call(
        functools.partial(panel_grads_kernel, len(recvs)),
        in_specs=whole(1 + len(recvs)),
        out_specs=whole(2),
        out_shape=[
            jax.ShapeDtypeStruct((rows, width), F32),
            jax.ShapeDtypeStruct((rows, width), BF16),
        ],
        compiler_params=params(),
        name="panel_grads",
    )(own, *recvs)


def all_grads_kernel(n, own_ref, *refs):
    total = own_ref[...]
    for ref in refs[:n]:
        total = total + load_shard(ref)
    rows = total.shape[0] - BIAS_ROWS
    refs[n][...] = total[:rows, :]
    refs[n + 1][...] = total[rows : rows + 1, :]


def all_grads(own, recvs):
    rows, width = own.shape
    return pl.pallas_call(
        functools.partial(all_grads_kernel, len(recvs)),
        in_specs=whole(1 + len(recvs)),
        out_specs=whole(2),
        out_shape=[
            jax.ShapeDtypeStruct((rows - BIAS_ROWS, width), F32),
            jax.ShapeDtypeStruct((1, width), F32),
        ],
        compiler_params=params(),
        name="all_grads",
    )(own, *recvs)


def place_grads_kernel(n, ids_ref, *refs):
    shard_refs, self_ref, neigh_ref = refs[:n], refs[n], refs[n + 1]
    piece = shard_refs[0].shape[0] // 2
    for k, ref in enumerate(shard_refs):
        at = pl.multiple_of((ids_ref[0] ^ k) * piece, piece)
        self_ref[pl.ds(at, piece), :] = ref[0:piece, :]
        neigh_ref[pl.ds(at, piece), :] = ref[piece : 2 * piece, :]


def place_grads(ids, shards):
    width = shards[0].shape[1]
    out = jax.ShapeDtypeStruct((width, width), F32)
    n = len(shards)
    return pl.pallas_call(
        functools.partial(place_grads_kernel, n),
        in_specs=[pl.BlockSpec(memory_space=pltpu.SMEM)] + whole(n),
        out_specs=whole(2),
        out_shape=[out, out],
        compiler_params=params(),
        name="place_grads",
    )(ids, *shards)


def back_kernel(n, first, offset, ids_ref, flip_ref, *refs):
    msg_refs = refs[:n]
    step = pl.program_id(0)
    if first:
        prior, total_ref = None, refs[n]
    else:
        prior, total_ref = refs[n], refs[-1]

    @pl.when(step == 0)
    def _():
        if first:
            total_ref[...] = jnp.zeros_like(total_ref)
        else:
            total_ref[...] = prior[...]

    for k in range(n):

        @pl.when(step == k)
        def _(k=k):
            total_ref[...] += dot(flip_ref[0], msg_refs[k][...])

    if not first:
        own_ref, out_refs = refs[n + 1], refs[n + 2 : -1]
        share = own_ref.shape[0]

        @pl.when(step == n - 1)
        def _():
            own_ref[...] = total_ref[pl.ds(pl.multiple_of(ids_ref[1] * share, share), share), :]
            for k, ref in enumerate(out_refs):
                at = pl.multiple_of((ids_ref[1] ^ (k + 1)) * share, share)
                ref[...] = total_ref[pl.ds(at, share), :].astype(BF16)


def back_sums(ids, flip, messages, offset, prior, panels):
    share, width = messages[0].shape
    n = len(messages)
    rows = panels * share
    fixed = pl.BlockSpec((share, width), lambda q, ids: (0, 0))
    total_spec = pl.BlockSpec((rows, width), lambda q, ids: (0, 0))
    first = prior is None
    total = jax.ShapeDtypeStruct((rows, width), F32)
    own = jax.ShapeDtypeStruct((share, width), F32)
    block = jax.ShapeDtypeStruct((share, width), BF16)
    return pl.pallas_call(
        functools.partial(back_kernel, n, first, offset),
        grid_spec=pltpu.PrefetchScalarGridSpec(
            num_scalar_prefetch=1,
            grid=(n,),
            in_specs=[
                pl.BlockSpec((1, rows, share), lambda q, ids: ((ids[0] ^ offset) ^ (2 * q), 0, 0))
            ]
            + [fixed] * n
            + ([] if first else [total_spec]),
            out_specs=total_spec if first else [fixed] * panels,
            scratch_shapes=[] if first else [pltpu.VMEM((rows, width), F32)],
        ),
        out_shape=total if first else [own] + [block] * (panels - 1),
        compiler_params=params(),
        name="back_sums_even" if first else "back_sums_odd",
    )(ids, flip, *messages, *([] if first else [prior]))


def feature_grads_kernel(n, dpre_ref, ws_ref, own_ref, *refs):
    total = own_ref[...]
    for ref in refs[:n]:
        total = total + ref[...].astype(F32)
    refs[n][...] = (total + dot(dpre_ref[...], ws_ref[...], CONTRACT_SECOND)).astype(BF16)


def feature_grads(dpre, ws, own, recvs):
    return pl.pallas_call(
        functools.partial(feature_grads_kernel, len(recvs)),
        in_specs=whole(3 + len(recvs)),
        out_specs=pl.BlockSpec(memory_space=pltpu.VMEM),
        out_shape=jax.ShapeDtypeStruct(dpre.shape, BF16),
        compiler_params=params(),
        name="feature_grads",
    )(dpre, ws, own, *recvs)


def per_device(
    features,
    self_weight,
    neigh_weight,
    out_bias,
    tile_masks,
    tile_live,
    tile_columns,
    node_degree,
    cotangent,
):
    row_devices = lax.axis_size("row")
    rep_devices = lax.axis_size("rep")
    chips = rep_devices // 2
    panel_rows, width = features.shape
    share = node_degree.shape[0]
    panels = tile_masks.shape[1]
    tile = tile_masks.shape[2]
    blocks = share // tile
    scale = 1.0 / math.sqrt(share * row_devices * rep_devices)
    rep, row = lax.axis_index("rep"), lax.axis_index("row")
    ids = jnp.stack([rep, row]).astype(jnp.int32)

    own = lax.dynamic_slice_in_dim(features, rep * share, share, 0)
    gathered = [own] + [xor_permute(own, "row", k) for k in range(1, row_devices)]
    dense, flip = build_strip(
        tile_masks.reshape(panel_rows * panels, tile), tile_live.T, tile_columns.T,
        panels, blocks, tile, rep_devices,
    )
    deg = jnp.broadcast_to(node_degree.astype(F32)[:, None], (share, width))

    away = sibling_sums(ids, dense, gathered, chips)
    sums = chip_sums(ids, dense, xor_permute(away, "rep", 1), gathered, chips)
    recvs = [xor_permute(sums[q], "rep", 2 * q) for q in range(1, chips)]
    hidden_out, dpre, mean, message, dbias = rows_step(
        own, self_weight, neigh_weight, out_bias[None, :], deg, cotangent, sums[0], recvs
    )

    even = [message] + [xor_permute(message, "rep", 2 * q) for q in range(1, chips)]
    odd = [xor_permute(value, "rep", 1) for value in even]
    half = back_sums(ids, flip, even, 0, None, panels)
    spread = back_sums(ids, flip, odd, 1, half, panels)

    grad_away, grad_keep = local_grads(ids, own, mean, dpre, dbias, chips, scale)
    pair = pair_grads(grad_keep, xor_permute(grad_away, "rep", 1), chips)
    panel, panel_b = panel_grads(
        pair[0], [xor_permute(pair[q], "rep", 2 * q) for q in range(1, chips)]
    )
    shard, grad_bias = all_grads(
        panel, [xor_permute(panel_b, "row", k) for k in range(1, row_devices)]
    )
    shards = [shard] + [xor_permute(shard, "rep", 2 * q) for q in range(1, chips)]
    others = [xor_permute(value, "rep", 1) for value in shards]
    ordered = [value for both in zip(shards, others) for value in both]
    grad_self, grad_neigh = place_grads(ids, ordered)

    arrived = [xor_permute(spread[k], "row", k) for k in range(1, row_devices)]
    grad_features = feature_grads(dpre, self_weight, spread[0], arrived)
    return (hidden_out, grad_features, grad_self, grad_neigh, grad_bias[0])


def solution(mesh):
    return jax.shard_map(
        per_device,
        mesh=mesh,
        in_specs=(
            P("row", None),
            P(),
            P(),
            P(),
            P("row", "rep", None),
            P("row", "rep"),
            P("row", "rep"),
            P(("row", "rep")),
            P(("row", "rep"), None),
        ),
        out_specs=(P(("row", "rep"), None), P(("row", "rep"), None), P(), P(), P()),
        check_vma=False,
    )
```

time: 287 us -> 78.2 us (0.27)
  waiting for transfers between devices: 178 us -> 27 us
  blocking collectives: 56.8 us -> 0 us
  starting transfers between devices: 0.16 us -> 30.2 us
  matrix products: 16.3 us -> 0 us
  Pallas kernels: 0 us -> 14.9 us
  between operations: 13.9 us -> 0.85 us
  other arithmetic: 8.98 us -> 0.08 us
  local copies, waits for them, and re-layouts: 12 us -> 4.9 us
    psum x1 -> x0, waiting for transfers between devices: 112 us -> none  [per_device(): lax.psum((self_term, neigh_term, bias_term), ('row', 'rep'))]
    reduce_scatter x2 -> x0, waiting for transfers between devices: 42.9 us -> none  [the longest x1 42.9 us: per_device(): lax.psum_scatter(partial_sums, 'rep', scatter_dimension=0, tiled=True)]
    psum x1 -> x0, blocking collectives: 39.4 us -> none  [per_device(): lax.psum((self_term, neigh_term, bias_term), ('row', 'rep'))]
    ppermute x0 -> x31, starting transfers between devices: none -> 30.2 us  [xor_permute(): lax.ppermute(value, axis, [(i, i ^ k) for i in range(lax.axis_size(axis))])]
    ppermute x0 -> x31, waiting for transfers between devices: none -> 27 us  [xor_permute(): lax.ppermute(value, axis, [(i, i ^ k) for i in range(lax.axis_size(axis))])]
    all_gather x1 -> x0, waiting for transfers between devices: 23.6 us -> none  [per_device(): lax.all_gather(message, 'rep', axis=0, tiled=True)]
    all_gather x1 -> x0, blocking collectives: 17.4 us -> none  [per_device(): lax.all_gather(own, 'row', axis=0, tiled=True)]
    dot_general x8 -> x0, matrix products: 16.3 us -> none  [the longest x1 4.82 us: per_device(): jnp.dot(strip, lax.all_gather(own, 'row', axis=0, tiled=True), preferred_...]
  transfers between devices with their start and end apart: 4 -> 31, of which waited for: 3 -> 15; matrix products, arithmetic and copies ran while one was open for 1% -> 0% of each run, Pallas kernels for 0% -> 10%
where the time goes in v1:
time: 78.2 us; the launch traced here: 77.9 us
  starting transfers between devices  30.2 us (39%)
  waiting for transfers between devices  27 us (35%)
  Pallas kernels  14.9 us (19%)
  local copies, waits for them, and re-layouts  4.9 us (6%)
  between operations  0.85 us (1%)
    ppermute x31, starting transfers between devices, xor_permute(): lax.ppermute(value, axis, [(i, i ^ k) for i in range(lax.axis_size(axis))])  30.2 us
    ppermute x31, waiting for transfers between devices, xor_permute(): lax.ppermute(value, axis, [(i, i ^ k) for i in range(lax.axis_size(axis))])  27 us
    unnamed x18, local copies, waits for them, and re-layouts  4.79 us
    pallas_call x2, Pallas kernels, back_sums(): pl.pallas_call(functools.partial(back_kernel, n, first, offset), grid_spe...  3.75 us
    pallas_call x1, Pallas kernels, build_strip(): pl.pallas_call(functools.partial(strip_kernel, panels, blocks, tile), gri...  2.5 us
    pallas_call x1, Pallas kernels, chip_sums(): pl.pallas_call(functools.partial(chip_sums_kernel, n, chips), grid_spec=p...  1.95 us
    pallas_call x1, Pallas kernels, sibling_sums(): pl.pallas_call(functools.partial(sibling_sums_kernel, n), grid_spec=pltpu...  1.88 us
  transfers between devices with their start and end apart: 31, of which 15 were waited for; matrix products, arithmetic and copies ran while one was open for 0% of the time, Pallas kernels for 10%

profile of v1, /device:TPU:0, one launch (start us, length us, event | category | flops | bytes accessed | tf_op | source)
XLA Modules:
  0.0 77.9 jit_solution(1903099645718030100)
XLA Ops:
  0.6 0.0 copy-start
  0.7 1.2 %copy-done = bf16[2048,256]{1,0:T(8,128)(2,1)S(1)} copy-done((bf16[2048,256]{1,0:T(8,128)(2,1)S(1)}, bf16[2048,256]{1,0:T(8,128)(2,1)}, u32[]{:S(2)}) %copy-start) | copy-done | bytes 1048600
  1.9 3.1 %collective-permute-start = (bf16[256,256]{1,0:T(8,128)(2,1)S(1)}, bf16[256,256]{1,0:T(8,128)(2,1)S(1)}, u32[]{:S(2)}, u32[]{:S(2)}) collective-permute-start(bf16[256,256]{1,0:T(8,128)(2,1)S(1)} %constant_dynamic-slice_fusion.refs_0_.own_ref), channel_id=1, source_target_pairs={{0,8},{8,0},{16,24},{24,16},{1,9},{9,1},{17,25},{25,17},{2,10},{10... | collective-permute-start | bytes 393224 | tf_op jit(solution)/shard_map/ppermute | solution.py:38
  5.0 2.6 %collective-permute-start.1 = (bf16[256,256]{1,0:T(8,128)(2,1)S(1)}, bf16[256,256]{1,0:T(8,128)(2,1)S(1)}, u32[]{:S(2)}, u32[]{:S(2)}) collective-permute-start(bf16[256,256]{1,0:T(8,128)(2,1)S(1)} %constant_dynamic-slice_fusion.refs_0_.own_ref), channel_id=1, source_target_pairs={{0,16},{8,24},{16,0},{24,8},{1,17},{9,25},{17,1},{25,9},{2,18},{10... | collective-permute-start | bytes 393224 | tf_op jit(solution)/shard_map/ppermute | solution.py:38
  7.6 2.2 %copy-done.1 = s32[2048,4,128]{2,1,0:T(4,128)S(1)} copy-done((s32[2048,4,128]{2,1,0:T(4,128)S(1)}, s32[2048,4,128]{2,1,0:T(4,128)}, u32[]{:S(2)}) %copy-start.1) | copy-done | bytes 4194328
  9.7 0.7 copy-done.5
  10.4 0.7 copy-done.6
  11.1 2.5 %build_strip.1 = (bf16[2048,1024]{1,0:T(8,128)(2,1)S(1)}, bf16[8,1024,256]{2,1,0:T(8,128)(2,1)S(1)}) custom-call(s32[4,16]{1,0:T(4,128)S(1)} %bitcast.8, s32[4,16]{1,0:T(4,128)S(1)} %bitcast.9, s32[8192,128]{1,0:T(8,128)S(1)} %bitcast.7), custom_call_target="tpu_custom_call" | custom-call | tf_op jit(solution)/shard_map/build_strip/pallas_call | solution.py:60
  13.6 0.1 pad_add_fusion.ids_ref
  13.7 0.0 collective-permute-done.refs_1_
  13.7 4.2 %collective-permute-done.1.refs_2_ = bf16[256,256]{1,0:T(8,128)(2,1)S(1)} collective-permute-done((bf16[256,256]{1,0:T(8,128)(2,1)S(1)}, bf16[256,256]{1,0:T(8,128)(2,1)S(1)}, u32[]{:S(2)}, u32[]{:S(2)}) %collective-permute-start.1) | collective-permute-done | bytes 131104 | tf_op jit(solution)/shard_map/ppermute | solution.py:38
  17.9 0.0 collective-permute-done.2.refs_3_
  17.9 0.0 copy-start.4
  17.9 0.0 copy-start.7
  17.9 1.9 %sibling_sums.1 = bf16[1024,256]{1,0:T(8,128)(2,1)S(1)} custom-call(s32[2]{0:T(128)S(1)} %pad_add_fusion.ids_ref, bf16[2048,1024]{1,0:T(8,128)(2,1)S(1)} %get-tuple-element.32.dense_ref, bf16[256,256]{1,0:T(8,128)(2,1)S(1)} %constant_dynamic-slice_fusion.refs_0_.own_ref, bf16[256,256]{1,0:T(8,128)(2,1)S(1)} %collective-permute-done.refs_1_, ...), custom_call_target="tpu_custom_call" | custom-call | tf_op jit(solution)/shard_map/sibling_sums/pallas_call | solution.py:122
  19.8 0.1 collective-permute-start.3
  19.9 1.9 %collective-permute-done.3.recv_ref = bf16[1024,256]{1,0:T(8,128)(2,1)S(1)} collective-permute-done((bf16[1024,256]{1,0:T(8,128)(2,1)S(1)}, bf16[1024,256]{1,0:T(8,128)(2,1)S(1)}, u32[]{:S(2)}, u32[]{:S(2)}) %collective-permute-start.3) | collective-permute-done | bytes 524320 | tf_op jit(solution)/shard_map/ppermute | solution.py:38
  21.8 2.0 %chip_sums.1 = (f32[256,256]{1,0:T(8,128)S(1)}, bf16[256,256]{1,0:T(8,128)(2,1)S(1)}, bf16[256,256]{1,0:T(8,128)(2,1)S(1)}, bf16[256,256]{1,0:T(8,128)(2,1)S(1)}) custom-call(s32[2]{0:T(128)S(1)} %pad_add_fusion.ids_ref, bf16[2048,1024]{1,0:T(8,128)(2,1)S(1)} %get-tuple-element.32.dense_ref, bf16[1024,256]{1,0:T(8,128)(2,1)S(1)} %collective-permute-done.3.recv_ref, ...), custom_call_target="tpu_custom_call" | custom-call | tf_op jit(solution)/shard_map/chip_sums/pallas_call | solution.py:143
  23.8 1.6 %collective-permute-start.4 = (bf16[256,256]{1,0:T(8,128)(2,1)S(1)}, bf16[256,256]{1,0:T(8,128)(2,1)S(1)}, u32[]{:S(2)}, u32[]{:S(2)}) collective-permute-start(bf16[256,256]{1,0:T(8,128)(2,1)S(1)} %get-tuple-element.34), channel_id=1, source_target_pairs={{0,2},{1,3},{2,0},{3,1},{4,6},{5,7},{6,4},{7,5},{8,10},{9,11},{10,... | collective-permute-start | bytes 393224 | tf_op jit(solution)/shard_map/ppermute | solution.py:38
  25.3 1.5 %collective-permute-start.5 = (bf16[256,256]{1,0:T(8,128)(2,1)S(1)}, bf16[256,256]{1,0:T(8,128)(2,1)S(1)}, u32[]{:S(2)}, u32[]{:S(2)}) collective-permute-start(bf16[256,256]{1,0:T(8,128)(2,1)S(1)} %get-tuple-element.35), channel_id=1, source_target_pairs={{0,4},{1,5},{2,6},{3,7},{4,0},{5,1},{6,2},{7,3},{8,12},{9,13},{10,... | collective-permute-start | bytes 393224 | tf_op jit(solution)/shard_map/ppermute | solution.py:38
  26.8 0.5 collective-permute-start.6
  27.3 2.4 %collective-permute-done.4.refs_0_ = bf16[256,256]{1,0:T(8,128)(2,1)S(1)} collective-permute-done((bf16[256,256]{1,0:T(8,128)(2,1)S(1)}, bf16[256,256]{1,0:T(8,128)(2,1)S(1)}, u32[]{:S(2)}, u32[]{:S(2)}) %collective-permute-start.4) | collective-permute-done | bytes 131104 | tf_op jit(solution)/shard_map/ppermute | solution.py:38
  29.7 3.7 %collective-permute-done.5.refs_1_ = bf16[256,256]{1,0:T(8,128)(2,1)S(1)} collective-permute-done((bf16[256,256]{1,0:T(8,128)(2,1)S(1)}, bf16[256,256]{1,0:T(8,128)(2,1)S(1)}, u32[]{:S(2)}, u32[]{:S(2)}) %collective-permute-start.5) | collective-permute-done | bytes 131104 | tf_op jit(solution)/shard_map/ppermute | solution.py:38
  33.4 0.1 broadcast_in_dim.10.deg_ref
  33.5 1.1 %rows_step.1 = (bf16[256,256]{1,0:T(8,128)(2,1)}, bf16[256,256]{1,0:T(8,128)(2,1)S(1)}, bf16[256,256]{1,0:T(8,128)(2,1)S(1)}, bf16[256,256]{1,0:T(8,128)(2,1)S(1)}, f32[1,256]{1,0:T(1,128)S(1)}) custom-call(bf16[256,256]{1,0:T(8,128)(2,1)S(1)} %constant_dynamic-slice_fusion.refs_0_.own_ref, bf16[256,256]{1,0:T(8,128)(2,1)S(1)} %copy-done.2, ...), custom_call_target="tpu_custom_call" | custom-call | tf_op jit(solution)/shard_map/rows_step/pallas_call | solution.py:186
  34.6 0.8 %local_grads.1 = (f32[320,256]{1,0:T(8,128)S(1)}, f32[320,256]{1,0:T(8,128)S(1)}) custom-call(s32[2]{0:T(128)S(1)} %pad_add_fusion.ids_ref, bf16[256,256]{1,0:T(8,128)(2,1)S(1)} %constant_dynamic-slice_fusion.refs_0_.own_ref, bf16[256,256]{1,0:T(8,128)(2,1)S(1)} %get-tuple-element.45.mean_ref, bf16[256,256]{1,0:T(8,128)(2,1)S(1)} %get-tuple-element.38.dpre_ref, ...), custom_call_target="tpu_custom_call" | custom-call | tf_op jit(solution)/shard_map/local_grads/pallas_call | solution.py:216
  35.5 0.1 collective-permute-start.17
  35.6 1.6 %collective-permute-start.10 = (bf16[256,256]{1,0:T(8,128)(2,1)S(1)}, bf16[256,256]{1,0:T(8,128)(2,1)S(1)}, u32[]{:S(2)}, u32[]{:S(2)}) collective-permute-start(bf16[256,256]{1,0:T(8,128)(2,1)S(1)} %get-tuple-element.40.refs_0_), channel_id=1, source_target_pairs={{0,4},{1,5},{2,6},{3,7},{4,0},{5,1},{6,2},{7,3},{8,12},{9,13},{10,... | collective-permute-start | bytes 393224 | tf_op jit(solution)/shard_map/ppermute | solution.py:38
  37.1 1.2 %collective-permute-start.12 = (bf16[256,256]{1,0:T(8,128)(2,1)S(1)}, bf16[256,256]{1,0:T(8,128)(2,1)S(1)}, u32[]{:S(2)}, u32[]{:S(2)}) collective-permute-start(bf16[256,256]{1,0:T(8,128)(2,1)S(1)} %get-tuple-element.40.refs_0_), channel_id=1, source_target_pairs={{0,6},{1,7},{2,4},{3,5},{4,2},{5,3},{6,0},{7,1},{8,14},{9,15},{10,... | collective-permute-start | bytes 393224 | tf_op jit(solution)/shard_map/ppermute | solution.py:38
  38.3 0.8 %collective-permute-start.8 = (bf16[256,256]{1,0:T(8,128)(2,1)S(1)}, bf16[256,256]{1,0:T(8,128)(2,1)S(1)}, u32[]{:S(2)}, u32[]{:S(2)}) collective-permute-start(bf16[256,256]{1,0:T(8,128)(2,1)S(1)} %get-tuple-element.40.refs_0_), channel_id=1, source_target_pairs={{0,2},{1,3},{2,0},{3,1},{4,6},{5,7},{6,4},{7,5},{8,10},{9,11},{10,... | collective-permute-start | bytes 393224 | tf_op jit(solution)/shard_map/ppermute | solution.py:38
  39.1 0.0 collective-permute-start.7
  39.1 5.0 %collective-permute-done.10.refs_2_ = bf16[256,256]{1,0:T(8,128)(2,1)S(1)} collective-permute-done((bf16[256,256]{1,0:T(8,128)(2,1)S(1)}, bf16[256,256]{1,0:T(8,128)(2,1)S(1)}, u32[]{:S(2)}, u32[]{:S(2)}) %collective-permute-start.10) | collective-permute-done | bytes 131104 | tf_op jit(solution)/shard_map/ppermute | solution.py:38
  44.1 0.0 collective-permute-start.11
  44.1 0.3 collective-permute-done.12.refs_3_
  44.4 0.2 collective-permute-start.13
  44.6 0.9 %collective-permute-done.8.refs_1_ = bf16[256,256]{1,0:T(8,128)(2,1)S(1)} collective-permute-done((bf16[256,256]{1,0:T(8,128)(2,1)S(1)}, bf16[256,256]{1,0:T(8,128)(2,1)S(1)}, u32[]{:S(2)}, u32[]{:S(2)}) %collective-permute-start.8) | collective-permute-done | bytes 131104 | tf_op jit(solution)/shard_map/ppermute | solution.py:38
  45.5 1.8 %back_sums_even.1.refs_4_ = f32[1024,256]{1,0:T(8,128)S(1)} custom-call(s32[2]{0:T(128)S(1)} %pad_add_fusion.ids_ref, bf16[8,1024,256]{2,1,0:T(8,128)(2,1)S(1)} %get-tuple-element.39.flip_ref, bf16[256,256]{1,0:T(8,128)(2,1)S(1)} %get-tuple-element.40.refs_0_, bf16[256,256]{1,0:T(8,128)(2,1)S(1)} %collective-permute-done.8.refs_1_, ...), custom_call_target="tpu_custom_call" | custom-call | tf_op jit(solution)/shard_map/back_sums_even/pallas_call | solution.py:383
  47.4 0.0 collective-permute-done.7.refs_0_
  47.4 0.0 collective-permute-done.11.refs_2_
  47.4 0.0 collective-permute-done.9.refs_1_
  47.4 1.9 %back_sums_odd.1 = (f32[256,256]{1,0:T(8,128)S(1)}, bf16[256,256]{1,0:T(8,128)(2,1)S(1)}, bf16[256,256]{1,0:T(8,128)(2,1)S(1)}, bf16[256,256]{1,0:T(8,128)(2,1)S(1)}) custom-call(s32[2]{0:T(128)S(1)} %pad_add_fusion.ids_ref, bf16[8,1024,256]{2,1,0:T(8,128)(2,1)S(1)} %get-tuple-element.39.flip_ref, bf16[256,256]{1,0:T(8,128)(2,1)S(1)} %collective-permute-done.7.refs_0_, ...), custom_call_target="tpu_custom_call" | custom-call | tf_op jit(solution)/shard_map/back_sums_odd/pallas_call | solution.py:383
  49.3 2.0 %collective-permute-start.14 = (bf16[256,256]{1,0:T(8,128)(2,1)S(1)}, bf16[256,256]{1,0:T(8,128)(2,1)S(1)}, u32[]{:S(2)}, u32[]{:S(2)}) collective-permute-start(bf16[256,256]{1,0:T(8,128)(2,1)S(1)} %get-tuple-element.42), channel_id=1, source_target_pairs={{0,8},{8,0},{16,24},{24,16},{1,9},{9,1},{17,25},{25,17},{2,10},{10... | collective-permute-start | bytes 393224 | tf_op jit(solution)/shard_map/ppermute | solution.py:38
  51.4 1.3 %collective-permute-start.18 = (bf16[80,256]{1,0:T(8,128)(2,1)S(1)}, bf16[80,256]{1,0:T(8,128)(2,1)S(1)}, u32[]{:S(2)}, u32[]{:S(2)}) collective-permute-start(bf16[80,256]{1,0:T(8,128)(2,1)S(1)} %get-tuple-element.50), channel_id=1, source_target_pairs={{0,2},{1,3},{2,0},{3,1},{4,6},{5,7},{6,4},{7,5},{8,10},{9,11},{10,... | collective-permute-start | bytes 122888 | tf_op jit(solution)/shard_map/ppermute | solution.py:38
  52.7 0.8 %collective-permute-start.19 = (bf16[80,256]{1,0:T(8,128)(2,1)S(1)}, bf16[80,256]{1,0:T(8,128)(2,1)S(1)}, u32[]{:S(2)}, u32[]{:S(2)}) collective-permute-start(bf16[80,256]{1,0:T(8,128)(2,1)S(1)} %get-tuple-element.51), channel_id=1, source_target_pairs={{0,4},{1,5},{2,6},{3,7},{4,0},{5,1},{6,2},{7,3},{8,12},{9,13},{10,... | collective-permute-start | bytes 122888 | tf_op jit(solution)/shard_map/ppermute | solution.py:38
  53.5 1.4 %collective-permute-start.20 = (bf16[80,256]{1,0:T(8,128)(2,1)S(1)}, bf16[80,256]{1,0:T(8,128)(2,1)S(1)}, u32[]{:S(2)}, u32[]{:S(2)}) collective-permute-start(bf16[80,256]{1,0:T(8,128)(2,1)S(1)} %get-tuple-element.52), channel_id=1, source_target_pairs={{0,6},{1,7},{2,4},{3,5},{4,2},{5,3},{6,0},{7,1},{8,14},{9,15},{10,... | collective-permute-start | bytes 122888 | tf_op jit(solution)/shard_map/ppermute | solution.py:38
  54.9 1.0 %collective-permute-start.15 = (bf16[256,256]{1,0:T(8,128)(2,1)S(1)}, bf16[256,256]{1,0:T(8,128)(2,1)S(1)}, u32[]{:S(2)}, u32[]{:S(2)}) collective-permute-start(bf16[256,256]{1,0:T(8,128)(2,1)S(1)} %get-tuple-element.43), channel_id=1, source_target_pairs={{0,16},{8,24},{16,0},{24,8},{1,17},{9,25},{17,1},{25,9},{2,18},{10... | collective-permute-start | bytes 393224 | tf_op jit(solution)/shard_map/ppermute | solution.py:38
  56.0 0.7 collective-permute-done.19.refs_1_
  56.7 1.7 %collective-permute-done.20.refs_2_ = bf16[80,256]{1,0:T(8,128)(2,1)S(1)} collective-permute-done((bf16[80,256]{1,0:T(8,128)(2,1)S(1)}, bf16[80,256]{1,0:T(8,128)(2,1)S(1)}, u32[]{:S(2)}, u32[]{:S(2)}) %collective-permute-start.20) | collective-permute-done | bytes 40992 | tf_op jit(solution)/shard_map/ppermute | solution.py:38
  58.5 0.1 collective-permute-start.21
  58.6 2.9 %collective-permute-start.22 = (bf16[80,256]{1,0:T(8,128)(2,1)S(1)}, bf16[80,256]{1,0:T(8,128)(2,1)S(1)}, u32[]{:S(2)}, u32[]{:S(2)}) collective-permute-start(bf16[80,256]{1,0:T(8,128)(2,1)S(1)} %get-tuple-element.54), channel_id=1, source_target_pairs={{0,16},{8,24},{16,0},{24,8},{1,17},{9,25},{17,1},{25,9},{2,18},{10... | collective-permute-start | bytes 122888 | tf_op jit(solution)/shard_map/ppermute | solution.py:38
  61.5 1.4 %collective-permute-start.23 = (bf16[80,256]{1,0:T(8,128)(2,1)S(1)}, bf16[80,256]{1,0:T(8,128)(2,1)S(1)}, u32[]{:S(2)}, u32[]{:S(2)}) collective-permute-start(bf16[80,256]{1,0:T(8,128)(2,1)S(1)} %get-tuple-element.54), channel_id=1, source_target_pairs={{0,24},{8,16},{16,8},{24,0},{1,25},{9,17},{17,9},{25,1},{2,26},{10... | collective-permute-start | bytes 122888 | tf_op jit(solution)/shard_map/ppermute | solution.py:38
  62.9 1.8 %collective-permute-done.21.refs_0_ = bf16[80,256]{1,0:T(8,128)(2,1)S(1)} collective-permute-done((bf16[80,256]{1,0:T(8,128)(2,1)S(1)}, bf16[80,256]{1,0:T(8,128)(2,1)S(1)}, u32[]{:S(2)}, u32[]{:S(2)}) %collective-permute-start.21) | collective-permute-done | bytes 40992 | tf_op jit(solution)/shard_map/ppermute | solution.py:38
  64.7 2.5 %collective-permute-start.16 = (bf16[256,256]{1,0:T(8,128)(2,1)S(1)}, bf16[256,256]{1,0:T(8,128)(2,1)S(1)}, u32[]{:S(2)}, u32[]{:S(2)}) collective-permute-start(bf16[256,256]{1,0:T(8,128)(2,1)S(1)} %get-tuple-element.44), channel_id=1, source_target_pairs={{0,24},{8,16},{16,8},{24,0},{1,25},{9,17},{17,9},{25,1},{2,26},{10... | collective-permute-start | bytes 393224 | tf_op jit(solution)/shard_map/ppermute | solution.py:38
  67.2 0.3 collective-permute-done.22.refs_1_
  67.5 0.6 all_grads.1
  68.1 1.4 %collective-permute-start.25 = (f32[64,256]{1,0:T(8,128)S(1)}, f32[64,256]{1,0:T(8,128)S(1)}, u32[]{:S(2)}, u32[]{:S(2)}) collective-permute-start(f32[64,256]{1,0:T(8,128)S(1)} %get-tuple-element.55.refs_0_), channel_id=1, source_target_pairs={{0,2},{1,3},{2,0},{3,1},{4,6},{5,7},{6,4},{7,5},{8,10},{9,11},{10,... | collective-permute-start | bytes 196616 | tf_op jit(solution)/shard_map/ppermute | solution.py:38
  69.5 0.6 collective-permute-start.27
  70.1 1.4 %collective-permute-start.29 = (f32[64,256]{1,0:T(8,128)S(1)}, f32[64,256]{1,0:T(8,128)S(1)}, u32[]{:S(2)}, u32[]{:S(2)}) collective-permute-start(f32[64,256]{1,0:T(8,128)S(1)} %get-tuple-element.55.refs_0_), channel_id=1, source_target_pairs={{0,6},{1,7},{2,4},{3,5},{4,2},{5,3},{6,0},{7,1},{8,14},{9,15},{10,... | collective-permute-start | bytes 196616 | tf_op jit(solution)/shard_map/ppermute | solution.py:38
  71.6 0.9 %collective-permute-done.25.refs_2_ = f32[64,256]{1,0:T(8,128)S(1)} collective-permute-done((f32[64,256]{1,0:T(8,128)S(1)}, f32[64,256]{1,0:T(8,128)S(1)}, u32[]{:S(2)}, u32[]{:S(2)}) %collective-permute-start.25) | collective-permute-done | bytes 65568 | tf_op jit(solution)/shard_map/ppermute | solution.py:38
  72.5 1.9 %collective-permute-done.27.refs_4_ = f32[64,256]{1,0:T(8,128)S(1)} collective-permute-done((f32[64,256]{1,0:T(8,128)S(1)}, f32[64,256]{1,0:T(8,128)S(1)}, u32[]{:S(2)}, u32[]{:S(2)}) %collective-permute-start.27) | collective-permute-done | bytes 65568 | tf_op jit(solution)/shard_map/ppermute | solution.py:38
  74.4 0.9 %collective-permute-done.29.refs_6_ = f32[64,256]{1,0:T(8,128)S(1)} collective-permute-done((f32[64,256]{1,0:T(8,128)S(1)}, f32[64,256]{1,0:T(8,128)S(1)}, u32[]{:S(2)}, u32[]{:S(2)}) %collective-permute-start.29) | collective-permute-done | bytes 65568 | tf_op jit(solution)/shard_map/ppermute | solution.py:38
  75.3 0.9 %feature_grads.1 = bf16[256,256]{1,0:T(8,128)(2,1)} custom-call(bf16[256,256]{1,0:T(8,128)(2,1)S(1)} %get-tuple-element.38.dpre_ref, bf16[256,256]{1,0:T(8,128)(2,1)S(1)} %copy-done.2, f32[256,256]{1,0:T(8,128)S(1)} %get-tuple-element.41.own_ref, bf16[256,256]{1,0:T(8,128)(2,1)S(1)} %collective-permute-done.14.refs_0_, ...), custom_call_target="tpu_custom_call" | custom-call | tf_op jit(solution)/shard_map/feature_grads/pallas_call | solution.py:410
  76.2 0.4 collective-permute-done.30.refs_7_
  76.6 1.4 %place_grads.1 = (f32[256,256]{1,0:T(8,128)}, f32[256,256]{1,0:T(8,128)}) custom-call(s32[2]{0:T(128)S(1)} %pad_add_fusion.ids_ref, f32[64,256]{1,0:T(8,128)S(1)} %get-tuple-element.55.refs_0_, f32[64,256]{1,0:T(8,128)S(1)} %collective-permute-done.24.refs_1_, f32[64,256]{1,0:T(8,128)S(1)} %collective-permute-done.25.refs_2_, ...), custom_call_target="tpu_custom_call" | custom-call | tf_op jit(solution)/shard_map/place_grads/pallas_call | solution.py:330
  (32 shorter events, 0.1 us)
Async XLA Ops:
  0.6 1.2 %copy-start = (bf16[2048,256]{1,0:T(8,128)(2,1)S(1)}, bf16[2048,256]{1,0:T(8,128)(2,1)}, u32[]{:S(2)}) copy-start(bf16[2048,256]{1,0:T(8,128)(2,1)} %param.9) | copy-start | bytes 3145732
  1.9 11.8 %collective-permute-start = (bf16[256,256]{1,0:T(8,128)(2,1)S(1)}, bf16[256,256]{1,0:T(8,128)(2,1)S(1)}, u32[]{:S(2)}, u32[]{:S(2)}) collective-permute-start(bf16[256,256]{1,0:T(8,128)(2,1)S(1)} %constant_dynamic-slice_fusion.refs_0_.own_ref), channel_id=1, source_target_pairs={{0,8},{8,0},{16,24},{24,16},{1,9},{9,1},{17,25},{25,17},{2,10},{10... | collective-permute-start | bytes 393224 | tf_op jit(solution)/shard_map/ppermute | solution.py:38
  5.0 12.9 %collective-permute-start.1 = (bf16[256,256]{1,0:T(8,128)(2,1)S(1)}, bf16[256,256]{1,0:T(8,128)(2,1)S(1)}, u32[]{:S(2)}, u32[]{:S(2)}) collective-permute-start(bf16[256,256]{1,0:T(8,128)(2,1)S(1)} %constant_dynamic-slice_fusion.refs_0_.own_ref), channel_id=1, source_target_pairs={{0,16},{8,24},{16,0},{24,8},{1,17},{9,25},{17,1},{25,9},{2,18},{10... | collective-permute-start | bytes 393224 | tf_op jit(solution)/shard_map/ppermute | solution.py:38
  7.6 10.3 %collective-permute-start.2 = (bf16[256,256]{1,0:T(8,128)(2,1)S(1)}, bf16[256,256]{1,0:T(8,128)(2,1)S(1)}, u32[]{:S(2)}, u32[]{:S(2)}) collective-permute-start(bf16[256,256]{1,0:T(8,128)(2,1)S(1)} %constant_dynamic-slice_fusion.refs_0_.own_ref), channel_id=1, source_target_pairs={{0,24},{8,16},{16,8},{24,0},{1,25},{9,17},{17,9},{25,1},{2,26},{10... | collective-permute-start | bytes 393224 | tf_op jit(solution)/shard_map/ppermute | solution.py:38
  7.6 2.2 %copy-start.1 = (s32[2048,4,128]{2,1,0:T(4,128)S(1)}, s32[2048,4,128]{2,1,0:T(4,128)}, u32[]{:S(2)}) copy-start(s32[2048,4,128]{2,1,0:T(4,128)} %param.13) | copy-start | bytes 12582916
  9.7 0.7 copy-start.5
  10.4 0.7 copy-start.6
  17.9 9.4 %copy-start.8 = (s32[256]{0:T(256)S(1)}, s32[256]{0:T(256)}, u32[]{:S(2)}) copy-start(s32[256]{0:T(256)} %param.16) | copy-start | bytes 3076
  17.9 15.6 %copy-start.2 = (bf16[256,256]{1,0:T(8,128)(2,1)S(1)}, bf16[256,256]{1,0:T(8,128)(2,1)}, u32[]{:S(2)}) copy-start(bf16[256,256]{1,0:T(8,128)(2,1)} %ws_ref.3) | copy-start | bytes 393220
  17.9 15.6 %copy-start.3 = (bf16[256,256]{1,0:T(8,128)(2,1)S(1)}, bf16[256,256]{1,0:T(8,128)(2,1)}, u32[]{:S(2)}) copy-start(bf16[256,256]{1,0:T(8,128)(2,1)} %wn_ref.1) | copy-start | bytes 393220
  17.9 15.6 %copy-start.4 = (bf16[256,256]{1,0:T(8,128)(2,1)S(1)}, bf16[256,256]{1,0:T(8,128)(2,1)}, u32[]{:S(2)}) copy-start(bf16[256,256]{1,0:T(8,128)(2,1)} %cot_ref.1) | copy-start | bytes 393220
  17.9 15.6 %copy-start.7 = (f32[256]{0:T(256)S(1)}, f32[256]{0:T(256)}, u32[]{:S(2)}) copy-start(f32[256]{0:T(256)} %param.12) | copy-start | bytes 3076
  19.8 2.0 %collective-permute-start.3 = (bf16[1024,256]{1,0:T(8,128)(2,1)S(1)}, bf16[1024,256]{1,0:T(8,128)(2,1)S(1)}, u32[]{:S(2)}, u32[]{:S(2)}) collective-permute-start(bf16[1024,256]{1,0:T(8,128)(2,1)S(1)} %sibling_sums.1), channel_id=1, source_target_pairs={{0,1},{1,0},{2,3},{3,2},{4,5},{5,4},{6,7},{7,6},{8,9},{9,8},{10,11... | collective-permute-start | bytes 1572872 | tf_op jit(solution)/shard_map/ppermute | solution.py:38
  23.8 5.9 %collective-permute-start.4 = (bf16[256,256]{1,0:T(8,128)(2,1)S(1)}, bf16[256,256]{1,0:T(8,128)(2,1)S(1)}, u32[]{:S(2)}, u32[]{:S(2)}) collective-permute-start(bf16[256,256]{1,0:T(8,128)(2,1)S(1)} %get-tuple-element.34), channel_id=1, source_target_pairs={{0,2},{1,3},{2,0},{3,1},{4,6},{5,7},{6,4},{7,5},{8,10},{9,11},{10,... | collective-permute-start | bytes 393224 | tf_op jit(solution)/shard_map/ppermute | solution.py:38
  25.3 8.1 %collective-permute-start.5 = (bf16[256,256]{1,0:T(8,128)(2,1)S(1)}, bf16[256,256]{1,0:T(8,128)(2,1)S(1)}, u32[]{:S(2)}, u32[]{:S(2)}) collective-permute-start(bf16[256,256]{1,0:T(8,128)(2,1)S(1)} %get-tuple-element.35), channel_id=1, source_target_pairs={{0,4},{1,5},{2,6},{3,7},{4,0},{5,1},{6,2},{7,3},{8,12},{9,13},{10,... | collective-permute-start | bytes 393224 | tf_op jit(solution)/shard_map/ppermute | solution.py:38
  26.8 6.6 %collective-permute-start.6 = (bf16[256,256]{1,0:T(8,128)(2,1)S(1)}, bf16[256,256]{1,0:T(8,128)(2,1)S(1)}, u32[]{:S(2)}, u32[]{:S(2)}) collective-permute-start(bf16[256,256]{1,0:T(8,128)(2,1)S(1)} %get-tuple-element.36), channel_id=1, source_target_pairs={{0,6},{1,7},{2,4},{3,5},{4,2},{5,3},{6,0},{7,1},{8,14},{9,15},{10,... | collective-permute-start | bytes 393224 | tf_op jit(solution)/shard_map/ppermute | solution.py:38
  35.5 15.9 %collective-permute-start.17 = (f32[320,256]{1,0:T(8,128)S(1)}, f32[320,256]{1,0:T(8,128)S(1)}, u32[]{:S(2)}, u32[]{:S(2)}) collective-permute-start(f32[320,256]{1,0:T(8,128)S(1)} %get-tuple-element.48), channel_id=1, source_target_pairs={{0,1},{1,0},{2,3},{3,2},{4,5},{5,4},{6,7},{7,6},{8,9},{9,8},{10,11... | collective-permute-start | bytes 983048 | tf_op jit(solution)/shard_map/ppermute | solution.py:38
  35.6 8.6 %collective-permute-start.10 = (bf16[256,256]{1,0:T(8,128)(2,1)S(1)}, bf16[256,256]{1,0:T(8,128)(2,1)S(1)}, u32[]{:S(2)}, u32[]{:S(2)}) collective-permute-start(bf16[256,256]{1,0:T(8,128)(2,1)S(1)} %get-tuple-element.40.refs_0_), channel_id=1, source_target_pairs={{0,4},{1,5},{2,6},{3,7},{4,0},{5,1},{6,2},{7,3},{8,12},{9,13},{10,... | collective-permute-start | bytes 393224 | tf_op jit(solution)/shard_map/ppermute | solution.py:38
  37.1 7.3 %collective-permute-start.12 = (bf16[256,256]{1,0:T(8,128)(2,1)S(1)}, bf16[256,256]{1,0:T(8,128)(2,1)S(1)}, u32[]{:S(2)}, u32[]{:S(2)}) collective-permute-start(bf16[256,256]{1,0:T(8,128)(2,1)S(1)} %get-tuple-element.40.refs_0_), channel_id=1, source_target_pairs={{0,6},{1,7},{2,4},{3,5},{4,2},{5,3},{6,0},{7,1},{8,14},{9,15},{10,... | collective-permute-start | bytes 393224 | tf_op jit(solution)/shard_map/ppermute | solution.py:38
  38.3 7.2 %collective-permute-start.8 = (bf16[256,256]{1,0:T(8,128)(2,1)S(1)}, bf16[256,256]{1,0:T(8,128)(2,1)S(1)}, u32[]{:S(2)}, u32[]{:S(2)}) collective-permute-start(bf16[256,256]{1,0:T(8,128)(2,1)S(1)} %get-tuple-element.40.refs_0_), channel_id=1, source_target_pairs={{0,2},{1,3},{2,0},{3,1},{4,6},{5,7},{6,4},{7,5},{8,10},{9,11},{10,... | collective-permute-start | bytes 393224 | tf_op jit(solution)/shard_map/ppermute | solution.py:38
  39.1 8.2 %collective-permute-start.7 = (bf16[256,256]{1,0:T(8,128)(2,1)S(1)}, bf16[256,256]{1,0:T(8,128)(2,1)S(1)}, u32[]{:S(2)}, u32[]{:S(2)}) collective-permute-start(bf16[256,256]{1,0:T(8,128)(2,1)S(1)} %get-tuple-element.40.refs_0_), channel_id=1, source_target_pairs={{0,1},{1,0},{2,3},{3,2},{4,5},{5,4},{6,7},{7,6},{8,9},{9,8},{10,11... | collective-permute-start | bytes 393224 | tf_op jit(solution)/shard_map/ppermute | solution.py:38
  44.1 3.2 %collective-permute-start.11 = (bf16[256,256]{1,0:T(8,128)(2,1)S(1)}, bf16[256,256]{1,0:T(8,128)(2,1)S(1)}, u32[]{:S(2)}, u32[]{:S(2)}) collective-permute-start(bf16[256,256]{1,0:T(8,128)(2,1)S(1)} %collective-permute-done.10.refs_2_), channel_id=1, source_target_pairs={{0,1},{1,0},{2,3},{3,2},{4,5},{5,4},{6,7},{7,6},{8,9},{9,8},{10,11... | collective-permute-start | bytes 393224 | tf_op jit(solution)/shard_map/ppermute | solution.py:38
  44.4 2.9 %collective-permute-start.13 = (bf16[256,256]{1,0:T(8,128)(2,1)S(1)}, bf16[256,256]{1,0:T(8,128)(2,1)S(1)}, u32[]{:S(2)}, u32[]{:S(2)}) collective-permute-start(bf16[256,256]{1,0:T(8,128)(2,1)S(1)} %collective-permute-done.12.refs_3_), channel_id=1, source_target_pairs={{0,1},{1,0},{2,3},{3,2},{4,5},{5,4},{6,7},{7,6},{8,9},{9,8},{10,11... | collective-permute-start | bytes 393224 | tf_op jit(solution)/shard_map/ppermute | solution.py:38
  45.5 1.9 %collective-permute-start.9 = (bf16[256,256]{1,0:T(8,128)(2,1)S(1)}, bf16[256,256]{1,0:T(8,128)(2,1)S(1)}, u32[]{:S(2)}, u32[]{:S(2)}) collective-permute-start(bf16[256,256]{1,0:T(8,128)(2,1)S(1)} %collective-permute-done.8.refs_1_), channel_id=1, source_target_pairs={{0,1},{1,0},{2,3},{3,2},{4,5},{5,4},{6,7},{7,6},{8,9},{9,8},{10,11... | collective-permute-start | bytes 393224 | tf_op jit(solution)/shard_map/ppermute | solution.py:38
  49.3 20.8 %collective-permute-start.14 = (bf16[256,256]{1,0:T(8,128)(2,1)S(1)}, bf16[256,256]{1,0:T(8,128)(2,1)S(1)}, u32[]{:S(2)}, u32[]{:S(2)}) collective-permute-start(bf16[256,256]{1,0:T(8,128)(2,1)S(1)} %get-tuple-element.42), channel_id=1, source_target_pairs={{0,8},{8,0},{16,24},{24,16},{1,9},{9,1},{17,25},{25,17},{2,10},{10... | collective-permute-start | bytes 393224 | tf_op jit(solution)/shard_map/ppermute | solution.py:38
  51.4 4.6 %collective-permute-start.18 = (bf16[80,256]{1,0:T(8,128)(2,1)S(1)}, bf16[80,256]{1,0:T(8,128)(2,1)S(1)}, u32[]{:S(2)}, u32[]{:S(2)}) collective-permute-start(bf16[80,256]{1,0:T(8,128)(2,1)S(1)} %get-tuple-element.50), channel_id=1, source_target_pairs={{0,2},{1,3},{2,0},{3,1},{4,6},{5,7},{6,4},{7,5},{8,10},{9,11},{10,... | collective-permute-start | bytes 122888 | tf_op jit(solution)/shard_map/ppermute | solution.py:38
  52.7 4.0 %collective-permute-start.19 = (bf16[80,256]{1,0:T(8,128)(2,1)S(1)}, bf16[80,256]{1,0:T(8,128)(2,1)S(1)}, u32[]{:S(2)}, u32[]{:S(2)}) collective-permute-start(bf16[80,256]{1,0:T(8,128)(2,1)S(1)} %get-tuple-element.51), channel_id=1, source_target_pairs={{0,4},{1,5},{2,6},{3,7},{4,0},{5,1},{6,2},{7,3},{8,12},{9,13},{10,... | collective-permute-start | bytes 122888 | tf_op jit(solution)/shard_map/ppermute | solution.py:38
  53.5 4.9 %collective-permute-start.20 = (bf16[80,256]{1,0:T(8,128)(2,1)S(1)}, bf16[80,256]{1,0:T(8,128)(2,1)S(1)}, u32[]{:S(2)}, u32[]{:S(2)}) collective-permute-start(bf16[80,256]{1,0:T(8,128)(2,1)S(1)} %get-tuple-element.52), channel_id=1, source_target_pairs={{0,6},{1,7},{2,4},{3,5},{4,2},{5,3},{6,0},{7,1},{8,14},{9,15},{10,... | collective-permute-start | bytes 122888 | tf_op jit(solution)/shard_map/ppermute | solution.py:38
  54.9 16.6 %collective-permute-start.15 = (bf16[256,256]{1,0:T(8,128)(2,1)S(1)}, bf16[256,256]{1,0:T(8,128)(2,1)S(1)}, u32[]{:S(2)}, u32[]{:S(2)}) collective-permute-start(bf16[256,256]{1,0:T(8,128)(2,1)S(1)} %get-tuple-element.43), channel_id=1, source_target_pairs={{0,16},{8,24},{16,0},{24,8},{1,17},{9,25},{17,1},{25,9},{2,18},{10... | collective-permute-start | bytes 393224 | tf_op jit(solution)/shard_map/ppermute | solution.py:38
  58.5 6.2 %collective-permute-start.21 = (bf16[80,256]{1,0:T(8,128)(2,1)S(1)}, bf16[80,256]{1,0:T(8,128)(2,1)S(1)}, u32[]{:S(2)}, u32[]{:S(2)}) collective-permute-start(bf16[80,256]{1,0:T(8,128)(2,1)S(1)} %get-tuple-element.54), channel_id=1, source_target_pairs={{0,8},{8,0},{16,24},{24,16},{1,9},{9,1},{17,25},{25,17},{2,10},{10... | collective-permute-start | bytes 122888 | tf_op jit(solution)/shard_map/ppermute | solution.py:38
  58.6 8.9 %collective-permute-start.22 = (bf16[80,256]{1,0:T(8,128)(2,1)S(1)}, bf16[80,256]{1,0:T(8,128)(2,1)S(1)}, u32[]{:S(2)}, u32[]{:S(2)}) collective-permute-start(bf16[80,256]{1,0:T(8,128)(2,1)S(1)} %get-tuple-element.54), channel_id=1, source_target_pairs={{0,16},{8,24},{16,0},{24,8},{1,17},{9,25},{17,1},{25,9},{2,18},{10... | collective-permute-start | bytes 122888 | tf_op jit(solution)/shard_map/ppermute | solution.py:38
  61.5 6.0 %collective-permute-start.23 = (bf16[80,256]{1,0:T(8,128)(2,1)S(1)}, bf16[80,256]{1,0:T(8,128)(2,1)S(1)}, u32[]{:S(2)}, u32[]{:S(2)}) collective-permute-start(bf16[80,256]{1,0:T(8,128)(2,1)S(1)} %get-tuple-element.54), channel_id=1, source_target_pairs={{0,24},{8,16},{16,8},{24,0},{1,25},{9,17},{17,9},{25,1},{2,26},{10... | collective-permute-start | bytes 122888 | tf_op jit(solution)/shard_map/ppermute | solution.py:38
  64.7 10.6 %collective-permute-start.16 = (bf16[256,256]{1,0:T(8,128)(2,1)S(1)}, bf16[256,256]{1,0:T(8,128)(2,1)S(1)}, u32[]{:S(2)}, u32[]{:S(2)}) collective-permute-start(bf16[256,256]{1,0:T(8,128)(2,1)S(1)} %get-tuple-element.44), channel_id=1, source_target_pairs={{0,24},{8,16},{16,8},{24,0},{1,25},{9,17},{17,9},{25,1},{2,26},{10... | collective-permute-start | bytes 393224 | tf_op jit(solution)/shard_map/ppermute | solution.py:38
  68.1 4.4 %collective-permute-start.25 = (f32[64,256]{1,0:T(8,128)S(1)}, f32[64,256]{1,0:T(8,128)S(1)}, u32[]{:S(2)}, u32[]{:S(2)}) collective-permute-start(f32[64,256]{1,0:T(8,128)S(1)} %get-tuple-element.55.refs_0_), channel_id=1, source_target_pairs={{0,2},{1,3},{2,0},{3,1},{4,6},{5,7},{6,4},{7,5},{8,10},{9,11},{10,... | collective-permute-start | bytes 196616 | tf_op jit(solution)/shard_map/ppermute | solution.py:38
  69.5 4.9 %collective-permute-start.27 = (f32[64,256]{1,0:T(8,128)S(1)}, f32[64,256]{1,0:T(8,128)S(1)}, u32[]{:S(2)}, u32[]{:S(2)}) collective-permute-start(f32[64,256]{1,0:T(8,128)S(1)} %get-tuple-element.55.refs_0_), channel_id=1, source_target_pairs={{0,4},{1,5},{2,6},{3,7},{4,0},{5,1},{6,2},{7,3},{8,12},{9,13},{10,... | collective-permute-start | bytes 196616 | tf_op jit(solution)/shard_map/ppermute | solution.py:38
  70.1 5.2 %collective-permute-start.29 = (f32[64,256]{1,0:T(8,128)S(1)}, f32[64,256]{1,0:T(8,128)S(1)}, u32[]{:S(2)}, u32[]{:S(2)}) collective-permute-start(f32[64,256]{1,0:T(8,128)S(1)} %get-tuple-element.55.refs_0_), channel_id=1, source_target_pairs={{0,6},{1,7},{2,4},{3,5},{4,2},{5,3},{6,0},{7,1},{8,14},{9,15},{10,... | collective-permute-start | bytes 196616 | tf_op jit(solution)/shard_map/ppermute | solution.py:38
  71.6 4.6 %collective-permute-start.24 = (f32[64,256]{1,0:T(8,128)S(1)}, f32[64,256]{1,0:T(8,128)S(1)}, u32[]{:S(2)}, u32[]{:S(2)}) collective-permute-start(f32[64,256]{1,0:T(8,128)S(1)} %get-tuple-element.55.refs_0_), channel_id=1, source_target_pairs={{0,1},{1,0},{2,3},{3,2},{4,5},{5,4},{6,7},{7,6},{8,9},{9,8},{10,11... | collective-permute-start | bytes 196616 | tf_op jit(solution)/shard_map/ppermute | solution.py:38
  72.5 3.7 %collective-permute-start.26 = (f32[64,256]{1,0:T(8,128)S(1)}, f32[64,256]{1,0:T(8,128)S(1)}, u32[]{:S(2)}, u32[]{:S(2)}) collective-permute-start(f32[64,256]{1,0:T(8,128)S(1)} %collective-permute-done.25.refs_2_), channel_id=1, source_target_pairs={{0,1},{1,0},{2,3},{3,2},{4,5},{5,4},{6,7},{7,6},{8,9},{9,8},{10,11... | collective-permute-start | bytes 196616 | tf_op jit(solution)/shard_map/ppermute | solution.py:38
  74.4 1.8 %collective-permute-start.28 = (f32[64,256]{1,0:T(8,128)S(1)}, f32[64,256]{1,0:T(8,128)S(1)}, u32[]{:S(2)}, u32[]{:S(2)}) collective-permute-start(f32[64,256]{1,0:T(8,128)S(1)} %collective-permute-done.27.refs_4_), channel_id=1, source_target_pairs={{0,1},{1,0},{2,3},{3,2},{4,5},{5,4},{6,7},{7,6},{8,9},{9,8},{10,11... | collective-permute-start | bytes 196616 | tf_op jit(solution)/shard_map/ppermute | solution.py:38
  75.3 1.3 %collective-permute-start.30 = (f32[64,256]{1,0:T(8,128)S(1)}, f32[64,256]{1,0:T(8,128)S(1)}, u32[]{:S(2)}, u32[]{:S(2)}) collective-permute-start(f32[64,256]{1,0:T(8,128)S(1)} %collective-permute-done.29.refs_6_), channel_id=1, source_target_pairs={{0,1},{1,0},{2,3},{3,2},{4,5},{5,4},{6,7},{7,6},{8,9},{9,8},{10,11... | collective-permute-start | bytes 196616 | tf_op jit(solution)/shard_map/ppermute | solution.py:38

commit v2 on v0

v2 whole, which is shorter than its diff:
```python
import functools
import math

import jax
import jax.numpy as jnp
from jax import lax
from jax.experimental import pallas as pl
from jax.experimental.pallas import tpu as pltpu
from jax.sharding import PartitionSpec as P

BF16 = jnp.bfloat16
F32 = jnp.float32
BIAS_ROWS = 16
PIECES = 4
VMEM_LIMIT = 40 * 1024 * 1024
CONTRACT_FIRST = (((0,), (0,)), ((), ()))
CONTRACT_SECOND = (((1,), (1,)), ((), ()))
GELU_A = math.sqrt(2.0 / math.pi)
GELU_B = 0.044715


def dot(a, b, dims=(((1,), (0,)), ((), ()))):
    return lax.dot_general(a, b, dims, preferred_element_type=F32)


def params():
    return pltpu.CompilerParams(vmem_limit_bytes=VMEM_LIMIT)


def cost(flops, bytes_accessed):
    return pl.CostEstimate(flops=flops, bytes_accessed=bytes_accessed, transcendentals=0)


def whole(n):
    return [pl.BlockSpec(memory_space=pltpu.VMEM)] * n


def tree_sum(terms):
    terms = list(terms)
    while len(terms) > 1:
        terms = [a + b for a, b in zip(terms[::2], terms[1::2])]
    return terms[0]


def xor_permute(value, axis, k):
    return lax.ppermute(value, axis, [(i, i ^ k) for i in range(lax.axis_size(axis))])


def block_of(ids, p, chips):
    return (ids[0] ^ (1 - p // chips)) ^ (2 * (p % chips))


def strip_kernel(panels, blocks, tile, chips, ids_ref, live_ref, cols_ref, mask_ref, dense_ref, flip_ref):
    step = block_of(ids_ref, pl.program_id(0), chips)
    for j in range(blocks):
        i = step * blocks + j
        for s in range(panels):
            bits = mask_ref[pl.ds(j * tile * panels + s, tile, stride=panels), :].astype(F32)
            turned = bits.T
            live = live_ref[s, i] != 0
            col = cols_ref[s, i]
            for b in range(blocks):
                keep = jnp.where(live & (col == b), 1.0, 0.0).astype(F32)
                at = (s * blocks + b) * tile
                dense_ref[j * tile : (j + 1) * tile, at : at + tile] = (bits * keep).astype(BF16)
                flip_ref[at : at + tile, j * tile : (j + 1) * tile] = (turned * keep).astype(BF16)


def build_strip(ids, masks, live, cols, panels, blocks, tile, chips):
    share = blocks * tile
    width = panels * share
    rows = 2 * chips * share
    return pl.pallas_call(
        functools.partial(strip_kernel, panels, blocks, tile, chips),
        grid_spec=pltpu.PrefetchScalarGridSpec(
            num_scalar_prefetch=3,
            grid=(2 * chips,),
            in_specs=[
                pl.BlockSpec(
                    (share * panels, tile), lambda p, ids, live, cols: (block_of(ids, p, chips), 0)
                ),
            ],
            out_specs=[
                pl.BlockSpec((share, width), lambda p, ids, live, cols: (p, 0)),
                pl.BlockSpec((width, share), lambda p, ids, live, cols: (0, p)),
            ],
        ),
        out_shape=[
            jax.ShapeDtypeStruct((rows, width), BF16),
            jax.ShapeDtypeStruct((width, rows), BF16),
        ],
        compiler_params=params(),
        name="build_strip",
    )(ids, live, cols, masks)


def stack_features(ids_ref, feature_refs, held):
    share = feature_refs[0].shape[0]
    for k, ref in enumerate(feature_refs):
        at = pl.multiple_of((ids_ref[1] ^ k) * share, share)
        held[pl.ds(at, share), :] = ref[...]


def partial_sums_kernel(n, start, ids_ref, dense_ref, *refs):
    out_ref, held = refs[n], refs[n + 1]
    stack_features(ids_ref, refs[:n], held)
    rows = dense_ref[start : start + out_ref.shape[0], :]
    out_ref[...] = dot(rows, held[...]).astype(out_ref.dtype)


def partial_sums(ids, dense, features, part, dtype):
    share, width = features[0].shape
    n = len(features)
    rows = dense.shape[0] // 2
    return pl.pallas_call(
        functools.partial(partial_sums_kernel, n, part * rows),
        in_specs=[pl.BlockSpec(memory_space=pltpu.SMEM)] + whole(1 + n),
        out_specs=pl.BlockSpec(memory_space=pltpu.VMEM),
        out_shape=jax.ShapeDtypeStruct((rows, width), dtype),
        scratch_shapes=[pltpu.VMEM((n * share, width), BF16)],
        compiler_params=params(),
        name="keep_sums" if part else "away_sums",
    )(ids, dense, *features)


def chip_sums_kernel(m, keep_ref, recv_ref, own_ref, *out_refs):
    share = own_ref.shape[0]
    own_ref[...] = keep_ref[0:share, :] + recv_ref[0:share, :].astype(F32)
    for q in range(1, m):
        at = slice(q * share, (q + 1) * share)
        out_refs[q - 1][...] = (keep_ref[at, :] + recv_ref[at, :].astype(F32)).astype(BF16)


def chip_sums(keep, received, chips):
    share, width = keep.shape[0] // chips, keep.shape[1]
    block = jax.ShapeDtypeStruct((share, width), BF16)
    return pl.pallas_call(
        functools.partial(chip_sums_kernel, chips),
        in_specs=whole(2),
        out_specs=whole(chips),
        out_shape=[jax.ShapeDtypeStruct((share, width), F32)] + [block] * (chips - 1),
        compiler_params=params(),
        name="chip_sums",
    )(keep, received)


def rows_kernel(m, scale, ids_ref, own_ref, ws_ref, wn_ref, bias_ref, deg_ref, cot_ref, agg_ref, *refs):
    hidden_ref, dpre_ref, msg_ref, away_ref, keep_ref = refs[m - 1 :]
    width = own_ref.shape[1]
    agg = agg_ref[...]
    for ref in refs[: m - 1]:
        agg = agg + ref[...].astype(F32)
    deg = deg_ref[...]
    mean = (agg / deg).astype(BF16)
    v = dot(own_ref[...], ws_ref[...]) + dot(mean, wn_ref[...]) + bias_ref[...]
    t = jnp.tanh(GELU_A * (v + GELU_B * (v * v * v)))
    hidden_ref[...] = (0.5 * v * (1.0 + t)).astype(BF16)
    slope = 0.5 * (1.0 + t) + 0.5 * v * (1.0 - t * t) * (GELU_A * (1.0 + 3.0 * GELU_B * v * v))
    dpre = cot_ref[...].astype(F32) * slope
    dpre_b = dpre.astype(BF16)
    dpre_ref[...] = dpre_b
    msg_ref[...] = (dot(dpre_b, wn_ref[...], CONTRACT_SECOND) / deg).astype(BF16)
    dbias = jnp.broadcast_to(jnp.sum(dpre, axis=0, keepdims=True) * scale, (BIAS_ROWS, width))
    away_ref[width:, :] = dbias
    keep_ref[width:, :] = dbias
    first = (ids_ref[0] & 1) == 0
    mine = jnp.where(first, own_ref[...], mean)
    other = jnp.where(first, mean, own_ref[...])
    keep_ref[0:width, :] = dot(mine, dpre_b, CONTRACT_FIRST) * scale
    away_ref[0:width, :] = dot(other, dpre_b, CONTRACT_FIRST) * scale


def rows_step(ids, own, ws, wn, bias, deg, cot, agg, recvs, scale):
    share, width = own.shape
    block = jax.ShapeDtypeStruct((share, width), BF16)
    grads = jax.ShapeDtypeStruct((width + BIAS_ROWS, width), F32)
    m = len(recvs) + 1
    return pl.pallas_call(
        functools.partial(rows_kernel, m, scale),
        in_specs=[pl.BlockSpec(memory_space=pltpu.SMEM)] + whole(7 + m - 1),
        out_specs=whole(5),
        out_shape=[block, block, block, grads, grads],
        compiler_params=params(),
        name="rows_step",
    )(ids, own, ws, wn, bias, deg, cot, agg, *recvs)


def store_rounded(out_ref, total):
    rows = total.shape[0]
    tail = total[rows - BIAS_ROWS :, :]
    tail_high = tail.astype(BF16).astype(F32)
    index = lax.broadcasted_iota(jnp.int32, tail.shape, 0)
    mixed = jnp.where(index < BIAS_ROWS // 2, tail_high, tail - tail_high)
    out_ref[0 : rows - BIAS_ROWS, :] = total[0 : rows - BIAS_ROWS, :].astype(BF16)
    out_ref[rows - BIAS_ROWS :, :] = mixed.astype(BF16)


def load_sum(refs):
    rows = refs[0].shape[0]
    body = tree_sum(ref[0 : rows - BIAS_ROWS, :].astype(F32) for ref in refs)
    tail = tree_sum(ref[rows - BIAS_ROWS :, :].astype(F32) for ref in refs)
    return body, tail[0:1, :] + tail[BIAS_ROWS // 2 : BIAS_ROWS // 2 + 1, :]


def pair_grads_kernel(keep_ref, recv_ref, out_ref):
    store_rounded(out_ref, keep_ref[...] + recv_ref[...])


def pair_grads(keep, recv):
    return pl.pallas_call(
        pair_grads_kernel,
        in_specs=whole(2),
        out_specs=pl.BlockSpec(memory_space=pltpu.VMEM),
        out_shape=jax.ShapeDtypeStruct(keep.shape, BF16),
        compiler_params=params(),
        name="pair_grads",
    )(keep, recv)


def line_grads_kernel(n, *refs):
    body, line = load_sum(refs[:n])
    tail = jnp.broadcast_to(line, (BIAS_ROWS, line.shape[1]))
    store_rounded(refs[-1], jnp.concatenate([body, tail], axis=0))


def line_grads(parts, after=()):
    n = len(parts)
    return pl.pallas_call(
        functools.partial(line_grads_kernel, n),
        in_specs=whole(n) + [pl.BlockSpec(memory_space=pl.ANY)] * len(after),
        out_specs=pl.BlockSpec(memory_space=pltpu.VMEM),
        out_shape=jax.ShapeDtypeStruct(parts[0].shape, BF16),
        compiler_params=params(),
        name="line_grads",
    )(*parts, *after)


def all_grads_kernel(n, *refs):
    body, line = load_sum(refs[:n])
    rows = refs[n].shape[0]
    for i in range(PIECES):
        refs[n + i][...] = body[i * rows : (i + 1) * rows, :]
    refs[n + PIECES][...] = body
    refs[n + PIECES + 1][...] = line


def all_grads(parts):
    n = len(parts)
    rows, width = parts[0].shape
    return pl.pallas_call(
        functools.partial(all_grads_kernel, n),
        in_specs=whole(n),
        out_specs=whole(PIECES + 2),
        out_shape=[jax.ShapeDtypeStruct(((rows - BIAS_ROWS) // PIECES, width), F32)] * PIECES
        + [
            jax.ShapeDtypeStruct((rows - BIAS_ROWS, width), F32),
            jax.ShapeDtypeStruct((1, width), F32),
        ],
        compiler_params=params(),
        name="all_grads",
    )(*parts)


def place_grads_kernel(ids_ref, mine_ref, *refs):
    other_refs, (after_ref, self_ref, neigh_ref) = refs[:-3], refs[-3:]
    first = (ids_ref[0] & 1) == 0
    rows = other_refs[0].shape[0]
    for i, ref in enumerate(other_refs):
        at = slice(i * rows, (i + 1) * rows)
        self_ref[at, :] = jnp.where(first, mine_ref[at, :], ref[...])
        neigh_ref[at, :] = jnp.where(first, ref[...], mine_ref[at, :])


def place_grads(ids, mine, others, after):
    out = jax.ShapeDtypeStruct(mine.shape, F32)
    return pl.pallas_call(
        place_grads_kernel,
        in_specs=[pl.BlockSpec(memory_space=pltpu.SMEM)]
        + whole(1 + len(others))
        + [pl.BlockSpec(memory_space=pl.ANY)],
        out_specs=whole(2),
        out_shape=[out, out],
        compiler_params=params(),
        name="place_grads",
    )(ids, mine, *others, after)


def stack_messages(message_refs, held):
    share = message_refs[0].shape[0]
    for q, ref in enumerate(message_refs):
        held[q * share : (q + 1) * share, :] = ref[...]


def back_even_kernel(n, flip_ref, *refs):
    out_ref, held = refs[n], refs[n + 1]
    stack_messages(refs[:n], held)
    out_ref[...] = dot(flip_ref[:, held.shape[0] :], held[...])


def back_even(flip, messages):
    share, width = messages[0].shape
    n = len(messages)
    return pl.pallas_call(
        functools.partial(back_even_kernel, n),
        in_specs=whole(1 + n),
        out_specs=pl.BlockSpec(memory_space=pltpu.VMEM),
        out_shape=jax.ShapeDtypeStruct((flip.shape[0], width), F32),
        scratch_shapes=[pltpu.VMEM((n * share, width), BF16)],
        compiler_params=params(),
        name="back_even",
    )(flip, *messages)


def back_odd_kernel(n, ids_ref, flip_ref, prior_ref, *refs):
    own_ref, out_refs, held, total = refs[n], refs[n + 1 : -2], refs[-2], refs[-1]
    share = own_ref.shape[0]
    stack_messages(refs[:n], held)
    total[...] = prior_ref[...] + dot(flip_ref[:, 0 : held.shape[0]], held[...])
    own_ref[...] = total[pl.ds(pl.multiple_of(ids_ref[1] * share, share), share), :]
    for k, ref in enumerate(out_refs):
        at = pl.multiple_of((ids_ref[1] ^ (k + 1)) * share, share)
        ref[...] = total[pl.ds(at, share), :].astype(BF16)


def back_odd(ids, flip, prior, messages, panels):
    share, width = messages[0].shape
    n = len(messages)
    block = jax.ShapeDtypeStruct((share, width), BF16)
    return pl.pallas_call(
        functools.partial(back_odd_kernel, n),
        in_specs=[pl.BlockSpec(memory_space=pltpu.SMEM)] + whole(2 + n),
        out_specs=whole(panels),
        out_shape=[jax.ShapeDtypeStruct((share, width), F32)] + [block] * (panels - 1),
        scratch_shapes=[pltpu.VMEM((n * share, width), BF16), pltpu.VMEM(prior.shape, F32)],
        compiler_params=params(),
        name="back_odd",
    )(ids, flip, prior, *messages)


def feature_grads_kernel(n, dpre_ref, ws_ref, own_ref, *refs):
    total = own_ref[...]
    for ref in refs[:n]:
        total = total + ref[...].astype(F32)
    refs[n][...] = (total + dot(dpre_ref[...], ws_ref[...], CONTRACT_SECOND)).astype(BF16)


def feature_grads(dpre, ws, own, recvs):
    return pl.pallas_call(
        functools.partial(feature_grads_kernel, len(recvs)),
        in_specs=whole(3 + len(recvs)),
        out_specs=pl.BlockSpec(memory_space=pltpu.VMEM),
        out_shape=jax.ShapeDtypeStruct(dpre.shape, BF16),
        compiler_params=params(),
        name="feature_grads",
    )(dpre, ws, own, *recvs)


def per_device(
    features,
    self_weight,
    neigh_weight,
    out_bias,
    tile_masks,
    tile_live,
    tile_columns,
    node_degree,
    cotangent,
):
    row_devices = lax.axis_size("row")
    rep_devices = lax.axis_size("rep")
    chips = rep_devices // 2
    panel_rows, width = features.shape
    share = node_degree.shape[0]
    panels = tile_masks.shape[1]
    tile = tile_masks.shape[2]
    blocks = share // tile
    scale = 1.0 / math.sqrt(share * row_devices * rep_devices)
    rep, row = lax.axis_index("rep"), lax.axis_index("row")
    ids = jnp.stack([rep, row]).astype(jnp.int32)

    own = lax.dynamic_slice_in_dim(features, rep * share, share, 0)
    gathered = [own] + [xor_permute(own, "row", k) for k in range(1, row_devices)]
    dense, flip = build_strip(
        ids, tile_masks.reshape(panel_rows * panels, tile), tile_live.T, tile_columns.T,
        panels, blocks, tile, chips,
    )
    deg = jnp.broadcast_to(node_degree.astype(F32)[:, None], (share, width))

    away = partial_sums(ids, dense, gathered, 0, BF16)
    keep = partial_sums(ids, dense, gathered, 1, F32)
    sums = chip_sums(keep, xor_permute(away, "rep", 1), chips)
    recvs = [xor_permute(sums[q], "rep", 2 * q) for q in range(1, chips)]
    hidden_out, dpre, message, grad_away, grad_keep = rows_step(
        ids, own, self_weight, neigh_weight, out_bias[None, :], deg, cotangent, sums[0], recvs, scale
    )

    even = [message] + [xor_permute(message, "rep", 2 * q) for q in range(1, chips)]
    odd = [xor_permute(value, "rep", 1) for value in even]
    half = back_even(flip, even)
    spread = back_odd(ids, flip, half, odd, panels)
    token = spread[0]

    line = pair_grads(grad_keep, xor_permute(grad_away, "rep", 1))
    k = 1
    while k < row_devices:
        after = [token] if 2 * k == row_devices else []
        line = line_grads([line, xor_permute(line, "row", k)], after)
        k *= 2
    *pieces, mine, grad_bias = all_grads(
        [line] + [xor_permute(line, "rep", 2 * q) for q in range(1, chips)]
    )
    arrived = [xor_permute(spread[k], "row", k) for k in range(1, row_devices)]
    grad_features = feature_grads(dpre, self_weight, spread[0], arrived)
    late = xor_permute(grad_features, "rep", 1)
    others = [xor_permute(piece, "rep", 1) for piece in pieces]
    grad_self, grad_neigh = place_grads(ids, mine, others, late)
    return (hidden_out, grad_features, grad_self, grad_neigh, grad_bias[0])


def solution(mesh):
    return jax.shard_map(
        per_device,
        mesh=mesh,
        in_specs=(
            P("row", None),
            P(),
            P(),
            P(),
            P("row", "rep", None),
            P("row", "rep"),
            P("row", "rep"),
            P(("row", "rep")),
            P(("row", "rep"), None),
        ),
        out_specs=(P(("row", "rep"), None), P(("row", "rep"), None), P(), P(), P()),
        check_vma=False,
    )
```

time: 287 us -> 67.4 us (0.23)
  waiting for transfers between devices: 178 us -> 20.6 us
  blocking collectives: 56.8 us -> 0 us
  starting transfers between devices: 0.16 us -> 27.9 us
  matrix products: 16.3 us -> 0 us
  between operations: 13.9 us -> 0.86 us
  Pallas kernels: 0 us -> 12.2 us
  other arithmetic: 8.98 us -> 0.08 us
  local copies, waits for them, and re-layouts: 12 us -> 4.9 us
    psum x1 -> x0, waiting for transfers between devices: 112 us -> none  [per_device(): lax.psum((self_term, neigh_term, bias_term), ('row', 'rep'))]
    reduce_scatter x2 -> x0, waiting for transfers between devices: 42.9 us -> none  [the longest x1 42.9 us: per_device(): lax.psum_scatter(partial_sums, 'rep', scatter_dimension=0, tiled=True)]
    psum x1 -> x0, blocking collectives: 39.4 us -> none  [per_device(): lax.psum((self_term, neigh_term, bias_term), ('row', 'rep'))]
    ppermute x0 -> x28, starting transfers between devices: none -> 27.9 us  [xor_permute(): lax.ppermute(value, axis, [(i, i ^ k) for i in range(lax.axis_size(axis))])]
    all_gather x1 -> x0, waiting for transfers between devices: 23.6 us -> none  [per_device(): lax.all_gather(message, 'rep', axis=0, tiled=True)]
    ppermute x0 -> x28, waiting for transfers between devices: none -> 20.6 us  [xor_permute(): lax.ppermute(value, axis, [(i, i ^ k) for i in range(lax.axis_size(axis))])]
    all_gather x1 -> x0, blocking collectives: 17.4 us -> none  [per_device(): lax.all_gather(own, 'row', axis=0, tiled=True)]
    dot_general x8 -> x0, matrix products: 16.3 us -> none  [the longest x1 4.82 us: per_device(): jnp.dot(strip, lax.all_gather(own, 'row', axis=0, tiled=True), preferred_...]
  transfers between devices with their start and end apart: 4 -> 28, of which waited for: 3 -> 15; matrix products, arithmetic and copies ran while one was open for 1% -> 0% of each run, Pallas kernels for 0% -> 12%
where the time goes in v2:
time: 67.4 us; the launch traced here: 66.6 us
  starting transfers between devices  27.9 us (41%)
  waiting for transfers between devices  20.6 us (31%)
  Pallas kernels  12.2 us (18%)
  local copies, waits for them, and re-layouts  4.9 us (7%)
  between operations  0.86 us (1%)
    ppermute x28, starting transfers between devices, xor_permute(): lax.ppermute(value, axis, [(i, i ^ k) for i in range(lax.axis_size(axis))])  27.9 us
    ppermute x28, waiting for transfers between devices, xor_permute(): lax.ppermute(value, axis, [(i, i ^ k) for i in range(lax.axis_size(axis))])  20.6 us
    unnamed x18, local copies, waits for them, and re-layouts  4.8 us
    pallas_call x1, Pallas kernels, build_strip(): pl.pallas_call(functools.partial(strip_kernel, panels, blocks, tile, chip...  2.92 us
    pallas_call x2, Pallas kernels, partial_sums(): pl.pallas_call(functools.partial(partial_sums_kernel, n, part * rows), in...  2.57 us
    pallas_call x1, Pallas kernels, rows_step(): pl.pallas_call(functools.partial(rows_kernel, m, scale), in_specs=[pl.Blo...  1.67 us
    pallas_call x1, Pallas kernels, place_grads(): pl.pallas_call(place_grads_kernel, in_specs=[pl.BlockSpec(memory_space=pl...  1.37 us
  transfers between devices with their start and end apart: 28, of which 15 were waited for; matrix products, arithmetic and copies ran while one was open for 0% of the time, Pallas kernels for 12%

profile of v2, /device:TPU:0, one launch (start us, length us, event | category | flops | bytes accessed | tf_op | source)
XLA Modules:
  0.0 66.6 jit_solution(15561240947304167848)
XLA Ops:
  0.6 0.0 copy-start
  0.7 1.2 %copy-done = bf16[2048,256]{1,0:T(8,128)(2,1)S(1)} copy-done((bf16[2048,256]{1,0:T(8,128)(2,1)S(1)}, bf16[2048,256]{1,0:T(8,128)(2,1)}, u32[]{:S(2)}) %copy-start) | copy-done | bytes 1048600
  1.9 3.1 %collective-permute-start = (bf16[256,256]{1,0:T(8,128)(2,1)S(1)}, bf16[256,256]{1,0:T(8,128)(2,1)S(1)}, u32[]{:S(2)}, u32[]{:S(2)}) collective-permute-start(bf16[256,256]{1,0:T(8,128)(2,1)S(1)} %constant_dynamic-slice_fusion.refs_0_.own_ref), channel_id=1, source_target_pairs={{0,8},{8,0},{16,24},{24,16},{1,9},{9,1},{17,25},{25,17},{2,10},{10... | collective-permute-start | bytes 393224 | tf_op jit(solution)/shard_map/ppermute | solution.py:46
  5.0 2.6 %collective-permute-start.1 = (bf16[256,256]{1,0:T(8,128)(2,1)S(1)}, bf16[256,256]{1,0:T(8,128)(2,1)S(1)}, u32[]{:S(2)}, u32[]{:S(2)}) collective-permute-start(bf16[256,256]{1,0:T(8,128)(2,1)S(1)} %constant_dynamic-slice_fusion.refs_0_.own_ref), channel_id=1, source_target_pairs={{0,16},{8,24},{16,0},{24,8},{1,17},{9,25},{17,1},{25,9},{2,18},{10... | collective-permute-start | bytes 393224 | tf_op jit(solution)/shard_map/ppermute | solution.py:46
  7.6 0.0 collective-permute-start.2
  7.6 0.1 pad_add_fusion.ids_ref
  7.6 2.2 %copy-done.1 = s32[2048,4,128]{2,1,0:T(4,128)S(1)} copy-done((s32[2048,4,128]{2,1,0:T(4,128)S(1)}, s32[2048,4,128]{2,1,0:T(4,128)}, u32[]{:S(2)}) %copy-start.1) | copy-done | bytes 4194328
  9.8 0.7 %copy-done.5 = s32[16,4]{0,1:T(4,128)S(1)} copy-done((s32[16,4]{0,1:T(4,128)S(1)}, s32[16,4]{0,1:T(4,128)}, u32[]{:S(2)}) %copy-start.5) | copy-done | bytes 280
  10.5 0.7 %copy-done.6 = s32[16,4]{0,1:T(4,128)S(1)} copy-done((s32[16,4]{0,1:T(4,128)S(1)}, s32[16,4]{0,1:T(4,128)}, u32[]{:S(2)}) %copy-start.6) | copy-done | bytes 280
  11.2 2.9 %build_strip.1 = (bf16[2048,1024]{1,0:T(8,128)(2,1)S(1)}, bf16[1024,2048]{1,0:T(8,128)(2,1)S(1)}) custom-call(s32[2]{0:T(128)S(1)} %pad_add_fusion.ids_ref, s32[4,16]{1,0:T(4,128)S(1)} %bitcast.8, s32[4,16]{1,0:T(4,128)S(1)} %bitcast.9, s32[8192,128]{1,0:T(8,128)S(1)} %bitcast.7), custom_call_target="tpu_custom_call" | custom-call | tf_op jit(solution)/shard_map/build_strip/pallas_call | solution.py:73
  14.1 0.0 collective-permute-done.refs_1_
  14.1 3.8 %collective-permute-done.1.refs_2_ = bf16[256,256]{1,0:T(8,128)(2,1)S(1)} collective-permute-done((bf16[256,256]{1,0:T(8,128)(2,1)S(1)}, bf16[256,256]{1,0:T(8,128)(2,1)S(1)}, u32[]{:S(2)}, u32[]{:S(2)}) %collective-permute-start.1) | collective-permute-done | bytes 131104 | tf_op jit(solution)/shard_map/ppermute | solution.py:46
  17.9 1.3 %away_sums.1 = bf16[1024,256]{1,0:T(8,128)(2,1)S(1)} custom-call(s32[2]{0:T(128)S(1)} %pad_add_fusion.ids_ref, bf16[2048,1024]{1,0:T(8,128)(2,1)S(1)} %get-tuple-element.28.dense_ref, bf16[256,256]{1,0:T(8,128)(2,1)S(1)} %constant_dynamic-slice_fusion.refs_0_.own_ref, bf16[256,256]{1,0:T(8,128)(2,1)S(1)} %collective-permute-done.refs_1_, ...), custom_call_target="tpu_custom_call" | custom-call | tf_op jit(solution)/shard_map/away_sums/pallas_call | solution.py:115
  19.2 0.0 copy-start.8
  19.2 0.0 copy-start.2
  19.2 0.0 copy-start.3
  19.2 0.0 copy-start.4
  19.2 0.0 copy-start.7
  19.2 0.1 collective-permute-start.3
  19.3 1.3 %keep_sums.1.keep_ref = f32[1024,256]{1,0:T(8,128)S(1)} custom-call(s32[2]{0:T(128)S(1)} %pad_add_fusion.ids_ref, bf16[2048,1024]{1,0:T(8,128)(2,1)S(1)} %get-tuple-element.28.dense_ref, bf16[256,256]{1,0:T(8,128)(2,1)S(1)} %constant_dynamic-slice_fusion.refs_0_.own_ref, bf16[256,256]{1,0:T(8,128)(2,1)S(1)} %collective-permute-done.refs_1_, ...), custom_call_target="tpu_custom_call" | custom-call | tf_op jit(solution)/shard_map/keep_sums/pallas_call | solution.py:115
  20.6 0.6 collective-permute-done.3.recv_ref
  21.2 0.1 chip_sums.1
  21.3 1.6 %collective-permute-start.4 = (bf16[256,256]{1,0:T(8,128)(2,1)S(1)}, bf16[256,256]{1,0:T(8,128)(2,1)S(1)}, u32[]{:S(2)}, u32[]{:S(2)}) collective-permute-start(bf16[256,256]{1,0:T(8,128)(2,1)S(1)} %get-tuple-element.30), channel_id=1, source_target_pairs={{0,2},{1,3},{2,0},{3,1},{4,6},{5,7},{6,4},{7,5},{8,10},{9,11},{10,... | collective-permute-start | bytes 393224 | tf_op jit(solution)/shard_map/ppermute | solution.py:46
  22.9 1.5 %collective-permute-start.5 = (bf16[256,256]{1,0:T(8,128)(2,1)S(1)}, bf16[256,256]{1,0:T(8,128)(2,1)S(1)}, u32[]{:S(2)}, u32[]{:S(2)}) collective-permute-start(bf16[256,256]{1,0:T(8,128)(2,1)S(1)} %get-tuple-element.31), channel_id=1, source_target_pairs={{0,4},{1,5},{2,6},{3,7},{4,0},{5,1},{6,2},{7,3},{8,12},{9,13},{10,... | collective-permute-start | bytes 393224 | tf_op jit(solution)/shard_map/ppermute | solution.py:46
  24.4 0.5 collective-permute-start.6
  24.9 2.4 %collective-permute-done.4.refs_0_ = bf16[256,256]{1,0:T(8,128)(2,1)S(1)} collective-permute-done((bf16[256,256]{1,0:T(8,128)(2,1)S(1)}, bf16[256,256]{1,0:T(8,128)(2,1)S(1)}, u32[]{:S(2)}, u32[]{:S(2)}) %collective-permute-start.4) | collective-permute-done | bytes 131104 | tf_op jit(solution)/shard_map/ppermute | solution.py:46
  27.3 3.7 %collective-permute-done.5.refs_1_ = bf16[256,256]{1,0:T(8,128)(2,1)S(1)} collective-permute-done((bf16[256,256]{1,0:T(8,128)(2,1)S(1)}, bf16[256,256]{1,0:T(8,128)(2,1)S(1)}, u32[]{:S(2)}, u32[]{:S(2)}) %collective-permute-start.5) | collective-permute-done | bytes 131104 | tf_op jit(solution)/shard_map/ppermute | solution.py:46
  30.9 0.0 collective-permute-done.6.refs_2_
  30.9 0.1 broadcast_in_dim.10.deg_ref
  31.1 1.7 %rows_step.1 = (bf16[256,256]{1,0:T(8,128)(2,1)}, bf16[256,256]{1,0:T(8,128)(2,1)S(1)}, bf16[256,256]{1,0:T(8,128)(2,1)S(1)}, f32[272,256]{1,0:T(8,128)S(1)}, f32[272,256]{1,0:T(8,128)S(1)}) custom-call(s32[2]{0:T(128)S(1)} %pad_add_fusion.ids_ref, bf16[256,256]{1,0:T(8,128)(2,1)S(1)} %constant_dynamic-slice_fusion.refs_0_.own_ref, ...), custom_call_target="tpu_custom_call" | custom-call | tf_op jit(solution)/shard_map/rows_step/pallas_call | solution.py:178
  32.8 1.2 %collective-permute-start.7 = (bf16[256,256]{1,0:T(8,128)(2,1)S(1)}, bf16[256,256]{1,0:T(8,128)(2,1)S(1)}, u32[]{:S(2)}, u32[]{:S(2)}) collective-permute-start(bf16[256,256]{1,0:T(8,128)(2,1)S(1)} %get-tuple-element.36.refs_0_), channel_id=1, source_target_pairs={{0,2},{1,3},{2,0},{3,1},{4,6},{5,7},{6,4},{7,5},{8,10},{9,11},{10,... | collective-permute-start | bytes 393224 | tf_op jit(solution)/shard_map/ppermute | solution.py:46
  34.0 0.8 %collective-permute-start.8 = (bf16[256,256]{1,0:T(8,128)(2,1)S(1)}, bf16[256,256]{1,0:T(8,128)(2,1)S(1)}, u32[]{:S(2)}, u32[]{:S(2)}) collective-permute-start(bf16[256,256]{1,0:T(8,128)(2,1)S(1)} %get-tuple-element.36.refs_0_), channel_id=1, source_target_pairs={{0,4},{1,5},{2,6},{3,7},{4,0},{5,1},{6,2},{7,3},{8,12},{9,13},{10,... | collective-permute-start | bytes 393224 | tf_op jit(solution)/shard_map/ppermute | solution.py:46
  34.8 1.4 %collective-permute-start.9 = (bf16[256,256]{1,0:T(8,128)(2,1)S(1)}, bf16[256,256]{1,0:T(8,128)(2,1)S(1)}, u32[]{:S(2)}, u32[]{:S(2)}) collective-permute-start(bf16[256,256]{1,0:T(8,128)(2,1)S(1)} %get-tuple-element.36.refs_0_), channel_id=1, source_target_pairs={{0,6},{1,7},{2,4},{3,5},{4,2},{5,3},{6,0},{7,1},{8,14},{9,15},{10,... | collective-permute-start | bytes 393224 | tf_op jit(solution)/shard_map/ppermute | solution.py:46
  36.2 0.0 collective-permute-done.17.recv_ref
  36.3 2.0 %collective-permute-start.18 = (bf16[272,256]{1,0:T(8,128)(2,1)S(1)}, bf16[272,256]{1,0:T(8,128)(2,1)S(1)}, u32[]{:S(2)}, u32[]{:S(2)}) collective-permute-start(bf16[272,256]{1,0:T(8,128)(2,1)S(1)} %pair_grads.1.refs_0_), channel_id=1, source_target_pairs={{0,8},{8,0},{16,24},{24,16},{1,9},{9,1},{17,25},{25,17},{2,10},{10... | collective-permute-start | bytes 417800 | tf_op jit(solution)/shard_map/ppermute | solution.py:46
  38.3 0.0 collective-permute-start.10
  38.3 0.7 %collective-permute-done.7.refs_1_ = bf16[256,256]{1,0:T(8,128)(2,1)S(1)} collective-permute-done((bf16[256,256]{1,0:T(8,128)(2,1)S(1)}, bf16[256,256]{1,0:T(8,128)(2,1)S(1)}, u32[]{:S(2)}, u32[]{:S(2)}) %collective-permute-start.7) | collective-permute-done | bytes 131104 | tf_op jit(solution)/shard_map/ppermute | solution.py:46
  39.1 0.0 collective-permute-start.11
  39.1 1.7 %collective-permute-done.8.refs_2_ = bf16[256,256]{1,0:T(8,128)(2,1)S(1)} collective-permute-done((bf16[256,256]{1,0:T(8,128)(2,1)S(1)}, bf16[256,256]{1,0:T(8,128)(2,1)S(1)}, u32[]{:S(2)}, u32[]{:S(2)}) %collective-permute-start.8) | collective-permute-done | bytes 131104 | tf_op jit(solution)/shard_map/ppermute | solution.py:46
  40.8 1.6 %collective-permute-done.9.refs_3_ = bf16[256,256]{1,0:T(8,128)(2,1)S(1)} collective-permute-done((bf16[256,256]{1,0:T(8,128)(2,1)S(1)}, bf16[256,256]{1,0:T(8,128)(2,1)S(1)}, u32[]{:S(2)}, u32[]{:S(2)}) %collective-permute-start.9) | collective-permute-done | bytes 131104 | tf_op jit(solution)/shard_map/ppermute | solution.py:46
  42.5 3.0 %collective-permute-start.19 = (bf16[272,256]{1,0:T(8,128)(2,1)S(1)}, bf16[272,256]{1,0:T(8,128)(2,1)S(1)}, u32[]{:S(2)}, u32[]{:S(2)}) collective-permute-start(bf16[272,256]{1,0:T(8,128)(2,1)S(1)} %line_grads.2.refs_0_), channel_id=1, source_target_pairs={{0,16},{8,24},{16,0},{24,8},{1,17},{9,25},{17,1},{25,9},{2,18},{10... | collective-permute-start | bytes 417800 | tf_op jit(solution)/shard_map/ppermute | solution.py:46
  45.5 0.7 %back_even.1.prior_ref = f32[1024,256]{1,0:T(8,128)S(1)} custom-call(bf16[1024,2048]{1,0:T(8,128)(2,1)S(1)} %get-tuple-element.35.flip_ref, bf16[256,256]{1,0:T(8,128)(2,1)S(1)} %get-tuple-element.36.refs_0_, bf16[256,256]{1,0:T(8,128)(2,1)S(1)} %collective-permute-done.7.refs_1_, bf16[256,256]{1,0:T(8,128)(2,1)S(1)} %collective-permute-done.8.refs_2_, ...), custom_call_target="tpu_custom_call" | custom-call | tf_op jit(solution)/shard_map/back_even/pallas_call | solution.py:303
  46.3 1.3 %back_odd.1 = (f32[256,256]{1,0:T(8,128)S(1)}, bf16[256,256]{1,0:T(8,128)(2,1)S(1)}, bf16[256,256]{1,0:T(8,128)(2,1)S(1)}, bf16[256,256]{1,0:T(8,128)(2,1)S(1)}) custom-call(s32[2]{0:T(128)S(1)} %pad_add_fusion.ids_ref, bf16[1024,2048]{1,0:T(8,128)(2,1)S(1)} %get-tuple-element.35.flip_ref, f32[1024,256]{1,0:T(8,128)S(1)} %back_even.1.prior_ref, ...), custom_call_target="tpu_custom_call" | custom-call | tf_op jit(solution)/shard_map/back_odd/pallas_call | solution.py:329
  47.6 0.1 collective-permute-start.14
  47.7 1.9 %collective-permute-start.15 = (bf16[256,256]{1,0:T(8,128)(2,1)S(1)}, bf16[256,256]{1,0:T(8,128)(2,1)S(1)}, u32[]{:S(2)}, u32[]{:S(2)}) collective-permute-start(bf16[256,256]{1,0:T(8,128)(2,1)S(1)} %get-tuple-element.39), channel_id=1, source_target_pairs={{0,16},{8,24},{16,0},{24,8},{1,17},{9,25},{17,1},{25,9},{2,18},{10... | collective-permute-start | bytes 393224 | tf_op jit(solution)/shard_map/ppermute | solution.py:46
  49.6 2.5 %collective-permute-start.16 = (bf16[256,256]{1,0:T(8,128)(2,1)S(1)}, bf16[256,256]{1,0:T(8,128)(2,1)S(1)}, u32[]{:S(2)}, u32[]{:S(2)}) collective-permute-start(bf16[256,256]{1,0:T(8,128)(2,1)S(1)} %get-tuple-element.40), channel_id=1, source_target_pairs={{0,24},{8,16},{16,8},{24,0},{1,25},{9,17},{17,9},{25,1},{2,26},{10... | collective-permute-start | bytes 393224 | tf_op jit(solution)/shard_map/ppermute | solution.py:46
  52.0 1.1 %collective-permute-done.19.refs_1_ = bf16[272,256]{1,0:T(8,128)(2,1)S(1)} collective-permute-done((bf16[272,256]{1,0:T(8,128)(2,1)S(1)}, bf16[272,256]{1,0:T(8,128)(2,1)S(1)}, u32[]{:S(2)}, u32[]{:S(2)}) %collective-permute-start.19) | collective-permute-done | bytes 139296 | tf_op jit(solution)/shard_map/ppermute | solution.py:46
  53.2 1.3 %collective-permute-start.20 = (bf16[272,256]{1,0:T(8,128)(2,1)S(1)}, bf16[272,256]{1,0:T(8,128)(2,1)S(1)}, u32[]{:S(2)}, u32[]{:S(2)}) collective-permute-start(bf16[272,256]{1,0:T(8,128)(2,1)S(1)} %line_grads.3.refs_0_), channel_id=1, source_target_pairs={{0,2},{1,3},{2,0},{3,1},{4,6},{5,7},{6,4},{7,5},{8,10},{9,11},{10,... | collective-permute-start | bytes 417800 | tf_op jit(solution)/shard_map/ppermute | solution.py:46
  54.5 1.5 %collective-permute-start.21 = (bf16[272,256]{1,0:T(8,128)(2,1)S(1)}, bf16[272,256]{1,0:T(8,128)(2,1)S(1)}, u32[]{:S(2)}, u32[]{:S(2)}) collective-permute-start(bf16[272,256]{1,0:T(8,128)(2,1)S(1)} %line_grads.3.refs_0_), channel_id=1, source_target_pairs={{0,4},{1,5},{2,6},{3,7},{4,0},{5,1},{6,2},{7,3},{8,12},{9,13},{10,... | collective-permute-start | bytes 417800 | tf_op jit(solution)/shard_map/ppermute | solution.py:46
  56.0 0.1 collective-permute-done.14.refs_0_
  56.1 1.8 %collective-permute-start.22 = (bf16[272,256]{1,0:T(8,128)(2,1)S(1)}, bf16[272,256]{1,0:T(8,128)(2,1)S(1)}, u32[]{:S(2)}, u32[]{:S(2)}) collective-permute-start(bf16[272,256]{1,0:T(8,128)(2,1)S(1)} %line_grads.3.refs_0_), channel_id=1, source_target_pairs={{0,6},{1,7},{2,4},{3,5},{4,2},{5,3},{6,0},{7,1},{8,14},{9,15},{10,... | collective-permute-start | bytes 417800 | tf_op jit(solution)/shard_map/ppermute | solution.py:46
  57.9 3.7 %collective-permute-done.15.refs_1_ = bf16[256,256]{1,0:T(8,128)(2,1)S(1)} collective-permute-done((bf16[256,256]{1,0:T(8,128)(2,1)S(1)}, bf16[256,256]{1,0:T(8,128)(2,1)S(1)}, u32[]{:S(2)}, u32[]{:S(2)}) %collective-permute-start.15) | collective-permute-done | bytes 131104 | tf_op jit(solution)/shard_map/ppermute | solution.py:46
  61.5 0.9 %feature_grads.1 = bf16[256,256]{1,0:T(8,128)(2,1)} custom-call(bf16[256,256]{1,0:T(8,128)(2,1)S(1)} %get-tuple-element.34.dpre_ref, bf16[256,256]{1,0:T(8,128)(2,1)S(1)} %copy-done.2, f32[256,256]{1,0:T(8,128)S(1)} %get-tuple-element.37.own_ref.refs_2_, bf16[256,256]{1,0:T(8,128)(2,1)S(1)} %collective-permute-done.14.refs_0_, ...), custom_call_target="tpu_custom_call" | custom-call | tf_op jit(solution)/shard_map/feature_grads/pallas_call | solution.py:348
  62.4 0.1 collective-permute-done.21.refs_2_
  62.5 0.6 all_grads.1
  63.1 0.4 collective-permute-start.23
  63.5 0.1 collective-permute-start.24
  63.6 0.4 collective-permute-start.25
  64.0 0.1 collective-permute-start.26
  64.2 0.2 collective-permute-done.23.refs_0_
  64.4 0.4 collective-permute-done.24.refs_1_
  64.8 0.2 collective-permute-done.25.refs_2_
  64.9 0.4 collective-permute-done.26.refs_3_
  65.3 1.4 %place_grads.1 = (f32[256,256]{1,0:T(8,128)}, f32[256,256]{1,0:T(8,128)}) custom-call(s32[2]{0:T(128)S(1)} %pad_add_fusion.ids_ref, f32[256,256]{1,0:T(8,128)S(1)} %get-tuple-element.43.mine_ref, f32[64,256]{1,0:T(8,128)S(1)} %collective-permute-done.23.refs_0_, f32[64,256]{1,0:T(8,128)S(1)} %collective-permute-done.24.refs_1_, ...), custom_call_target="tpu_custom_call" | custom-call | tf_op jit(solution)/shard_map/place_grads/pallas_call | solution.py:276
  (27 shorter events, 0.2 us)
Async XLA Ops:
  0.6 1.2 %copy-start = (bf16[2048,256]{1,0:T(8,128)(2,1)S(1)}, bf16[2048,256]{1,0:T(8,128)(2,1)}, u32[]{:S(2)}) copy-start(bf16[2048,256]{1,0:T(8,128)(2,1)} %param.9) | copy-start | bytes 3145732
  1.9 12.2 %collective-permute-start = (bf16[256,256]{1,0:T(8,128)(2,1)S(1)}, bf16[256,256]{1,0:T(8,128)(2,1)S(1)}, u32[]{:S(2)}, u32[]{:S(2)}) collective-permute-start(bf16[256,256]{1,0:T(8,128)(2,1)S(1)} %constant_dynamic-slice_fusion.refs_0_.own_ref), channel_id=1, source_target_pairs={{0,8},{8,0},{16,24},{24,16},{1,9},{9,1},{17,25},{25,17},{2,10},{10... | collective-permute-start | bytes 393224 | tf_op jit(solution)/shard_map/ppermute | solution.py:46
  5.0 12.9 %collective-permute-start.1 = (bf16[256,256]{1,0:T(8,128)(2,1)S(1)}, bf16[256,256]{1,0:T(8,128)(2,1)S(1)}, u32[]{:S(2)}, u32[]{:S(2)}) collective-permute-start(bf16[256,256]{1,0:T(8,128)(2,1)S(1)} %constant_dynamic-slice_fusion.refs_0_.own_ref), channel_id=1, source_target_pairs={{0,16},{8,24},{16,0},{24,8},{1,17},{9,25},{17,1},{25,9},{2,18},{10... | collective-permute-start | bytes 393224 | tf_op jit(solution)/shard_map/ppermute | solution.py:46
  7.6 10.3 %collective-permute-start.2 = (bf16[256,256]{1,0:T(8,128)(2,1)S(1)}, bf16[256,256]{1,0:T(8,128)(2,1)S(1)}, u32[]{:S(2)}, u32[]{:S(2)}) collective-permute-start(bf16[256,256]{1,0:T(8,128)(2,1)S(1)} %constant_dynamic-slice_fusion.refs_0_.own_ref), channel_id=1, source_target_pairs={{0,24},{8,16},{16,8},{24,0},{1,25},{9,17},{17,9},{25,1},{2,26},{10... | collective-permute-start | bytes 393224 | tf_op jit(solution)/shard_map/ppermute | solution.py:46
  7.6 2.2 %copy-start.1 = (s32[2048,4,128]{2,1,0:T(4,128)S(1)}, s32[2048,4,128]{2,1,0:T(4,128)}, u32[]{:S(2)}) copy-start(s32[2048,4,128]{2,1,0:T(4,128)} %param.13) | copy-start | bytes 12582916
  9.8 0.7 %copy-start.5 = (s32[16,4]{0,1:T(4,128)S(1)}, s32[16,4]{0,1:T(4,128)}, u32[]{:S(2)}) copy-start(s32[16,4]{0,1:T(4,128)} %param.14) | copy-start | bytes 772
  10.5 0.7 %copy-start.6 = (s32[16,4]{0,1:T(4,128)S(1)}, s32[16,4]{0,1:T(4,128)}, u32[]{:S(2)}) copy-start(s32[16,4]{0,1:T(4,128)} %param.15) | copy-start | bytes 772
  19.2 5.7 %copy-start.8 = (s32[256]{0:T(256)S(1)}, s32[256]{0:T(256)}, u32[]{:S(2)}) copy-start(s32[256]{0:T(256)} %param.16) | copy-start | bytes 3076
  19.2 11.8 %copy-start.2 = (bf16[256,256]{1,0:T(8,128)(2,1)S(1)}, bf16[256,256]{1,0:T(8,128)(2,1)}, u32[]{:S(2)}) copy-start(bf16[256,256]{1,0:T(8,128)(2,1)} %ws_ref.3) | copy-start | bytes 393220
  19.2 11.8 %copy-start.3 = (bf16[256,256]{1,0:T(8,128)(2,1)S(1)}, bf16[256,256]{1,0:T(8,128)(2,1)}, u32[]{:S(2)}) copy-start(bf16[256,256]{1,0:T(8,128)(2,1)} %wn_ref.1) | copy-start | bytes 393220
  19.2 11.8 %copy-start.4 = (bf16[256,256]{1,0:T(8,128)(2,1)S(1)}, bf16[256,256]{1,0:T(8,128)(2,1)}, u32[]{:S(2)}) copy-start(bf16[256,256]{1,0:T(8,128)(2,1)} %cot_ref.1) | copy-start | bytes 393220
  19.2 11.8 %copy-start.7 = (f32[256]{0:T(256)S(1)}, f32[256]{0:T(256)}, u32[]{:S(2)}) copy-start(f32[256]{0:T(256)} %param.12) | copy-start | bytes 3076
  19.2 2.0 %collective-permute-start.3 = (bf16[1024,256]{1,0:T(8,128)(2,1)S(1)}, bf16[1024,256]{1,0:T(8,128)(2,1)S(1)}, u32[]{:S(2)}, u32[]{:S(2)}) collective-permute-start(bf16[1024,256]{1,0:T(8,128)(2,1)S(1)} %away_sums.1), channel_id=1, source_target_pairs={{0,1},{1,0},{2,3},{3,2},{4,5},{5,4},{6,7},{7,6},{8,9},{9,8},{10,11... | collective-permute-start | bytes 1572872 | tf_op jit(solution)/shard_map/ppermute | solution.py:46
  21.3 5.9 %collective-permute-start.4 = (bf16[256,256]{1,0:T(8,128)(2,1)S(1)}, bf16[256,256]{1,0:T(8,128)(2,1)S(1)}, u32[]{:S(2)}, u32[]{:S(2)}) collective-permute-start(bf16[256,256]{1,0:T(8,128)(2,1)S(1)} %get-tuple-element.30), channel_id=1, source_target_pairs={{0,2},{1,3},{2,0},{3,1},{4,6},{5,7},{6,4},{7,5},{8,10},{9,11},{10,... | collective-permute-start | bytes 393224 | tf_op jit(solution)/shard_map/ppermute | solution.py:46
  22.9 8.1 %collective-permute-start.5 = (bf16[256,256]{1,0:T(8,128)(2,1)S(1)}, bf16[256,256]{1,0:T(8,128)(2,1)S(1)}, u32[]{:S(2)}, u32[]{:S(2)}) collective-permute-start(bf16[256,256]{1,0:T(8,128)(2,1)S(1)} %get-tuple-element.31), channel_id=1, source_target_pairs={{0,4},{1,5},{2,6},{3,7},{4,0},{5,1},{6,2},{7,3},{8,12},{9,13},{10,... | collective-permute-start | bytes 393224 | tf_op jit(solution)/shard_map/ppermute | solution.py:46
  24.4 6.6 %collective-permute-start.6 = (bf16[256,256]{1,0:T(8,128)(2,1)S(1)}, bf16[256,256]{1,0:T(8,128)(2,1)S(1)}, u32[]{:S(2)}, u32[]{:S(2)}) collective-permute-start(bf16[256,256]{1,0:T(8,128)(2,1)S(1)} %get-tuple-element.32), channel_id=1, source_target_pairs={{0,6},{1,7},{2,4},{3,5},{4,2},{5,3},{6,0},{7,1},{8,14},{9,15},{10,... | collective-permute-start | bytes 393224 | tf_op jit(solution)/shard_map/ppermute | solution.py:46
  32.8 3.5 %collective-permute-start.17 = (f32[272,256]{1,0:T(8,128)S(1)}, f32[272,256]{1,0:T(8,128)S(1)}, u32[]{:S(2)}, u32[]{:S(2)}) collective-permute-start(f32[272,256]{1,0:T(8,128)S(1)} %get-tuple-element.42), channel_id=1, source_target_pairs={{0,1},{1,0},{2,3},{3,2},{4,5},{5,4},{6,7},{7,6},{8,9},{9,8},{10,11... | collective-permute-start | bytes 835592 | tf_op jit(solution)/shard_map/ppermute | solution.py:46
  32.8 6.3 %collective-permute-start.7 = (bf16[256,256]{1,0:T(8,128)(2,1)S(1)}, bf16[256,256]{1,0:T(8,128)(2,1)S(1)}, u32[]{:S(2)}, u32[]{:S(2)}) collective-permute-start(bf16[256,256]{1,0:T(8,128)(2,1)S(1)} %get-tuple-element.36.refs_0_), channel_id=1, source_target_pairs={{0,2},{1,3},{2,0},{3,1},{4,6},{5,7},{6,4},{7,5},{8,10},{9,11},{10,... | collective-permute-start | bytes 393224 | tf_op jit(solution)/shard_map/ppermute | solution.py:46
  34.0 6.8 %collective-permute-start.8 = (bf16[256,256]{1,0:T(8,128)(2,1)S(1)}, bf16[256,256]{1,0:T(8,128)(2,1)S(1)}, u32[]{:S(2)}, u32[]{:S(2)}) collective-permute-start(bf16[256,256]{1,0:T(8,128)(2,1)S(1)} %get-tuple-element.36.refs_0_), channel_id=1, source_target_pairs={{0,4},{1,5},{2,6},{3,7},{4,0},{5,1},{6,2},{7,3},{8,12},{9,13},{10,... | collective-permute-start | bytes 393224 | tf_op jit(solution)/shard_map/ppermute | solution.py:46
  34.8 7.6 %collective-permute-start.9 = (bf16[256,256]{1,0:T(8,128)(2,1)S(1)}, bf16[256,256]{1,0:T(8,128)(2,1)S(1)}, u32[]{:S(2)}, u32[]{:S(2)}) collective-permute-start(bf16[256,256]{1,0:T(8,128)(2,1)S(1)} %get-tuple-element.36.refs_0_), channel_id=1, source_target_pairs={{0,6},{1,7},{2,4},{3,5},{4,2},{5,3},{6,0},{7,1},{8,14},{9,15},{10,... | collective-permute-start | bytes 393224 | tf_op jit(solution)/shard_map/ppermute | solution.py:46
  36.3 6.2 %collective-permute-start.18 = (bf16[272,256]{1,0:T(8,128)(2,1)S(1)}, bf16[272,256]{1,0:T(8,128)(2,1)S(1)}, u32[]{:S(2)}, u32[]{:S(2)}) collective-permute-start(bf16[272,256]{1,0:T(8,128)(2,1)S(1)} %pair_grads.1.refs_0_), channel_id=1, source_target_pairs={{0,8},{8,0},{16,24},{24,16},{1,9},{9,1},{17,25},{25,17},{2,10},{10... | collective-permute-start | bytes 417800 | tf_op jit(solution)/shard_map/ppermute | solution.py:46
  38.3 7.9 %collective-permute-start.10 = (bf16[256,256]{1,0:T(8,128)(2,1)S(1)}, bf16[256,256]{1,0:T(8,128)(2,1)S(1)}, u32[]{:S(2)}, u32[]{:S(2)}) collective-permute-start(bf16[256,256]{1,0:T(8,128)(2,1)S(1)} %get-tuple-element.36.refs_0_), channel_id=1, source_target_pairs={{0,1},{1,0},{2,3},{3,2},{4,5},{5,4},{6,7},{7,6},{8,9},{9,8},{10,11... | collective-permute-start | bytes 393224 | tf_op jit(solution)/shard_map/ppermute | solution.py:46
  39.1 7.2 %collective-permute-start.11 = (bf16[256,256]{1,0:T(8,128)(2,1)S(1)}, bf16[256,256]{1,0:T(8,128)(2,1)S(1)}, u32[]{:S(2)}, u32[]{:S(2)}) collective-permute-start(bf16[256,256]{1,0:T(8,128)(2,1)S(1)} %collective-permute-done.7.refs_1_), channel_id=1, source_target_pairs={{0,1},{1,0},{2,3},{3,2},{4,5},{5,4},{6,7},{7,6},{8,9},{9,8},{10,11... | collective-permute-start | bytes 393224 | tf_op jit(solution)/shard_map/ppermute | solution.py:46
  40.8 5.5 %collective-permute-start.12 = (bf16[256,256]{1,0:T(8,128)(2,1)S(1)}, bf16[256,256]{1,0:T(8,128)(2,1)S(1)}, u32[]{:S(2)}, u32[]{:S(2)}) collective-permute-start(bf16[256,256]{1,0:T(8,128)(2,1)S(1)} %collective-permute-done.8.refs_2_), channel_id=1, source_target_pairs={{0,1},{1,0},{2,3},{3,2},{4,5},{5,4},{6,7},{7,6},{8,9},{9,8},{10,11... | collective-permute-start | bytes 393224 | tf_op jit(solution)/shard_map/ppermute | solution.py:46
  42.4 3.8 %collective-permute-start.13 = (bf16[256,256]{1,0:T(8,128)(2,1)S(1)}, bf16[256,256]{1,0:T(8,128)(2,1)S(1)}, u32[]{:S(2)}, u32[]{:S(2)}) collective-permute-start(bf16[256,256]{1,0:T(8,128)(2,1)S(1)} %collective-permute-done.9.refs_3_), channel_id=1, source_target_pairs={{0,1},{1,0},{2,3},{3,2},{4,5},{5,4},{6,7},{7,6},{8,9},{9,8},{10,11... | collective-permute-start | bytes 393224 | tf_op jit(solution)/shard_map/ppermute | solution.py:46
  42.5 10.7 %collective-permute-start.19 = (bf16[272,256]{1,0:T(8,128)(2,1)S(1)}, bf16[272,256]{1,0:T(8,128)(2,1)S(1)}, u32[]{:S(2)}, u32[]{:S(2)}) collective-permute-start(bf16[272,256]{1,0:T(8,128)(2,1)S(1)} %line_grads.2.refs_0_), channel_id=1, source_target_pairs={{0,16},{8,24},{16,0},{24,8},{1,17},{9,25},{17,1},{25,9},{2,18},{10... | collective-permute-start | bytes 417800 | tf_op jit(solution)/shard_map/ppermute | solution.py:46
  47.6 8.5 %collective-permute-start.14 = (bf16[256,256]{1,0:T(8,128)(2,1)S(1)}, bf16[256,256]{1,0:T(8,128)(2,1)S(1)}, u32[]{:S(2)}, u32[]{:S(2)}) collective-permute-start(bf16[256,256]{1,0:T(8,128)(2,1)S(1)} %get-tuple-element.38), channel_id=1, source_target_pairs={{0,8},{8,0},{16,24},{24,16},{1,9},{9,1},{17,25},{25,17},{2,10},{10... | collective-permute-start | bytes 393224 | tf_op jit(solution)/shard_map/ppermute | solution.py:46
  47.7 13.8 %collective-permute-start.15 = (bf16[256,256]{1,0:T(8,128)(2,1)S(1)}, bf16[256,256]{1,0:T(8,128)(2,1)S(1)}, u32[]{:S(2)}, u32[]{:S(2)}) collective-permute-start(bf16[256,256]{1,0:T(8,128)(2,1)S(1)} %get-tuple-element.39), channel_id=1, source_target_pairs={{0,16},{8,24},{16,0},{24,8},{1,17},{9,25},{17,1},{25,9},{2,18},{10... | collective-permute-start | bytes 393224 | tf_op jit(solution)/shard_map/ppermute | solution.py:46
  49.6 11.9 %collective-permute-start.16 = (bf16[256,256]{1,0:T(8,128)(2,1)S(1)}, bf16[256,256]{1,0:T(8,128)(2,1)S(1)}, u32[]{:S(2)}, u32[]{:S(2)}) collective-permute-start(bf16[256,256]{1,0:T(8,128)(2,1)S(1)} %get-tuple-element.40), channel_id=1, source_target_pairs={{0,24},{8,16},{16,8},{24,0},{1,25},{9,17},{17,9},{25,1},{2,26},{10... | collective-permute-start | bytes 393224 | tf_op jit(solution)/shard_map/ppermute | solution.py:46
  53.2 9.2 %collective-permute-start.20 = (bf16[272,256]{1,0:T(8,128)(2,1)S(1)}, bf16[272,256]{1,0:T(8,128)(2,1)S(1)}, u32[]{:S(2)}, u32[]{:S(2)}) collective-permute-start(bf16[272,256]{1,0:T(8,128)(2,1)S(1)} %line_grads.3.refs_0_), channel_id=1, source_target_pairs={{0,2},{1,3},{2,0},{3,1},{4,6},{5,7},{6,4},{7,5},{8,10},{9,11},{10,... | collective-permute-start | bytes 417800 | tf_op jit(solution)/shard_map/ppermute | solution.py:46
  54.5 8.0 %collective-permute-start.21 = (bf16[272,256]{1,0:T(8,128)(2,1)S(1)}, bf16[272,256]{1,0:T(8,128)(2,1)S(1)}, u32[]{:S(2)}, u32[]{:S(2)}) collective-permute-start(bf16[272,256]{1,0:T(8,128)(2,1)S(1)} %line_grads.3.refs_0_), channel_id=1, source_target_pairs={{0,4},{1,5},{2,6},{3,7},{4,0},{5,1},{6,2},{7,3},{8,12},{9,13},{10,... | collective-permute-start | bytes 417800 | tf_op jit(solution)/shard_map/ppermute | solution.py:46
  56.1 6.5 %collective-permute-start.22 = (bf16[272,256]{1,0:T(8,128)(2,1)S(1)}, bf16[272,256]{1,0:T(8,128)(2,1)S(1)}, u32[]{:S(2)}, u32[]{:S(2)}) collective-permute-start(bf16[272,256]{1,0:T(8,128)(2,1)S(1)} %line_grads.3.refs_0_), channel_id=1, source_target_pairs={{0,6},{1,7},{2,4},{3,5},{4,2},{5,3},{6,0},{7,1},{8,14},{9,15},{10,... | collective-permute-start | bytes 417800 | tf_op jit(solution)/shard_map/ppermute | solution.py:46
  62.4 1.8 %collective-permute-start.27 = (bf16[256,256]{1,0:T(8,128)(2,1)}, bf16[256,256]{1,0:T(8,128)(2,1)S(1)}, u32[]{:S(2)}, u32[]{:S(2)}) collective-permute-start(bf16[256,256]{1,0:T(8,128)(2,1)} %feature_grads.1), channel_id=1, source_target_pairs={{0,1},{1,0},{2,3},{3,2},{4,5},{5,4},{6,7},{7,6},{8,9},{9,8},{10,11... | collective-permute-start | bytes 393224 | tf_op jit(solution)/shard_map/ppermute | solution.py:46
  63.1 1.3 %collective-permute-start.23 = (f32[64,256]{1,0:T(8,128)S(1)}, f32[64,256]{1,0:T(8,128)S(1)}, u32[]{:S(2)}, u32[]{:S(2)}) collective-permute-start(f32[64,256]{1,0:T(8,128)S(1)} %get-tuple-element.44), channel_id=1, source_target_pairs={{0,1},{1,0},{2,3},{3,2},{4,5},{5,4},{6,7},{7,6},{8,9},{9,8},{10,11... | collective-permute-start | bytes 196616 | tf_op jit(solution)/shard_map/ppermute | solution.py:46
  63.5 1.3 %collective-permute-start.24 = (f32[64,256]{1,0:T(8,128)S(1)}, f32[64,256]{1,0:T(8,128)S(1)}, u32[]{:S(2)}, u32[]{:S(2)}) collective-permute-start(f32[64,256]{1,0:T(8,128)S(1)} %get-tuple-element.45), channel_id=1, source_target_pairs={{0,1},{1,0},{2,3},{3,2},{4,5},{5,4},{6,7},{7,6},{8,9},{9,8},{10,11... | collective-permute-start | bytes 196616 | tf_op jit(solution)/shard_map/ppermute | solution.py:46
  63.6 1.3 %collective-permute-start.25 = (f32[64,256]{1,0:T(8,128)S(1)}, f32[64,256]{1,0:T(8,128)S(1)}, u32[]{:S(2)}, u32[]{:S(2)}) collective-permute-start(f32[64,256]{1,0:T(8,128)S(1)} %get-tuple-element.46), channel_id=1, source_target_pairs={{0,1},{1,0},{2,3},{3,2},{4,5},{5,4},{6,7},{7,6},{8,9},{9,8},{10,11... | collective-permute-start | bytes 196616 | tf_op jit(solution)/shard_map/ppermute | solution.py:46
  64.0 1.3 %collective-permute-start.26 = (f32[64,256]{1,0:T(8,128)S(1)}, f32[64,256]{1,0:T(8,128)S(1)}, u32[]{:S(2)}, u32[]{:S(2)}) collective-permute-start(f32[64,256]{1,0:T(8,128)S(1)} %get-tuple-element.47), channel_id=1, source_target_pairs={{0,1},{1,0},{2,3},{3,2},{4,5},{5,4},{6,7},{7,6},{8,9},{9,8},{10,11... | collective-permute-start | bytes 196616 | tf_op jit(solution)/shard_map/ppermute | solution.py:46

commit v3 on v2

--- a/solution.py
+++ b/solution.py
@@ -11,7 +11,7 @@
 BF16 = jnp.bfloat16
 F32 = jnp.float32
 BIAS_ROWS = 16
-PIECES = 4
+SPACER_ROWS = 576
 VMEM_LIMIT = 40 * 1024 * 1024
 CONTRACT_FIRST = (((0,), (0,)), ((), ()))
 CONTRACT_SECOND = (((1,), (1,)), ((), ()))
@@ -101,47 +101,82 @@
         held[pl.ds(at, share), :] = ref[...]
 
 
-def partial_sums_kernel(n, start, ids_ref, dense_ref, *refs):
-    out_ref, held = refs[n], refs[n + 1]
-    stack_features(ids_ref, refs[:n], held)
+def away_sums_kernel(n, start, ids_ref, dense_ref, *refs):
+    out_ref, held_ref = refs[n:]
+    stack_features(ids_ref, refs[:n], held_ref)
     rows = dense_ref[start : start + out_ref.shape[0], :]
-    out_ref[...] = dot(rows, held[...]).astype(out_ref.dtype)
-
-
-def partial_sums(ids, dense, features, part, dtype):
+    out_ref[...] = dot(rows, held_ref[...]).astype(BF16)
+
+
+def away_far_sums(ids, dense, features, first):
     share, width = features[0].shape
     n = len(features)
-    rows = dense.shape[0] // 2
-    return pl.pallas_call(
-        functools.partial(partial_sums_kernel, n, part * rows),
+    return pl.pallas_call(
+        functools.partial(away_sums_kernel, n, first * share),
         in_specs=[pl.BlockSpec(memory_space=pltpu.SMEM)] + whole(1 + n),
+        out_specs=whole(2),
+        out_shape=[
+            jax.ShapeDtypeStruct((share, width), BF16),
+            jax.ShapeDtypeStruct((n * share, width), BF16),
+        ],
+        compiler_params=params(),
+        name="away_far",
+    )(ids, dense, *features)
+
+
+def away_near_kernel(dense_ref, held_ref, *out_refs):
+    share = out_refs[0].shape[0]
+    total = dot(dense_ref[0 : len(out_refs) * share, :], held_ref[...])
+    for q, ref in enumerate(out_refs):
+        ref[...] = total[q * share : (q + 1) * share, :].astype(BF16)
+
+
+def away_near_sums(dense, held, count, share):
+    return pl.pallas_call(
+        away_near_kernel,
+        in_specs=whole(2),
+        out_specs=whole(count),
+        out_shape=[jax.ShapeDtypeStruct((share, held.shape[1]), BF16)] * count,
+        compiler_params=params(),
+        name="away_near",
+    )(dense, held)
+
+
+def chip_sums_kernel(start, dense_ref, held_ref, *refs):
+    m = len(refs) // 2
+    share = refs[0].shape[0]
+    total = dot(dense_ref[start : start + m * share, :], held_ref[...])
+    for q in range(m):
+        part = total[q * share : (q + 1) * share, :] + refs[q][...].astype(F32)
+        refs[m + q][...] = part.astype(refs[m + q].dtype)
+
+
+def chip_sums(dense, received, held, first, dtypes, name):
+    share, width = received[0].shape
+    return pl.pallas_call(
+        functools.partial(chip_sums_kernel, first * share),
+        in_specs=whole(2 + len(received)),
+        out_specs=whole(len(received)),
+        out_shape=[jax.ShapeDtypeStruct((share, width), dtype) for dtype in dtypes],
+        compiler_params=params(),
+        name=name,
+    )(dense, held, *received)
+
+
+def add_far_kernel(own_ref, far_ref, out_ref):
+    out_ref[...] = own_ref[...] + far_ref[...].astype(F32)
+
+
+def add_far(own, far):
+    return pl.pallas_call(
+        add_far_kernel,
+        in_specs=whole(2),
         out_specs=pl.BlockSpec(memory_space=pltpu.VMEM),
-        out_shape=jax.ShapeDtypeStruct((rows, width), dtype),
-        scratch_shapes=[pltpu.VMEM((n * share, width), BF16)],
-        compiler_params=params(),
-        name="keep_sums" if part else "away_sums",
-    )(ids, dense, *features)
-
-
-def chip_sums_kernel(m, keep_ref, recv_ref, own_ref, *out_refs):
-    share = own_ref.shape[0]
-    own_ref[...] = keep_ref[0:share, :] + recv_ref[0:share, :].astype(F32)
-    for q in range(1, m):
-        at = slice(q * share, (q + 1) * share)
-        out_refs[q - 1][...] = (keep_ref[at, :] + recv_ref[at, :].astype(F32)).astype(BF16)
-
-
-def chip_sums(keep, received, chips):
-    share, width = keep.shape[0] // chips, keep.shape[1]
-    block = jax.ShapeDtypeStruct((share, width), BF16)
-    return pl.pallas_call(
-        functools.partial(chip_sums_kernel, chips),
-        in_specs=whole(2),
-        out_specs=whole(chips),
-        out_shape=[jax.ShapeDtypeStruct((share, width), F32)] + [block] * (chips - 1),
-        compiler_params=params(),
-        name="chip_sums",
-    )(keep, received)
+        out_shape=jax.ShapeDtypeStruct(own.shape, F32),
+        cost_estimate=cost(10000000, 10**6),
+        compiler_params=params(),
+        name="add_far",
+    )(own, far)
 
 
 def rows_kernel(m, scale, ids_ref, own_ref, ws_ref, wn_ref, bias_ref, deg_ref, cot_ref, agg_ref, *refs):
@@ -223,25 +258,22 @@
     store_rounded(refs[-1], jnp.concatenate([body, tail], axis=0))
 
 
-def line_grads(parts, after=()):
+def line_grads(parts):
     n = len(parts)
     return pl.pallas_call(
         functools.partial(line_grads_kernel, n),
-        in_specs=whole(n) + [pl.BlockSpec(memory_space=pl.ANY)] * len(after),
+        in_specs=whole(n),
         out_specs=pl.BlockSpec(memory_space=pltpu.VMEM),
         out_shape=jax.ShapeDtypeStruct(parts[0].shape, BF16),
         compiler_params=params(),
         name="line_grads",
-    )(*parts, *after)
+    )(*parts)
 
 
 def all_grads_kernel(n, *refs):
     body, line = load_sum(refs[:n])
-    rows = refs[n].shape[0]
-    for i in range(PIECES):
-        refs[n + i][...] = body[i * rows : (i + 1) * rows, :]
-    refs[n + PIECES][...] = body
-    refs[n + PIECES + 1][...] = line
+    refs[n][...] = body
+    refs[n + 1][...] = line
 
 
 def all_grads(parts):
@@ -250,9 +282,8 @@
     return pl.pallas_call(
         functools.partial(all_grads_kernel, n),
         in_specs=whole(n),
-        out_specs=whole(PIECES + 2),
-        out_shape=[jax.ShapeDtypeStruct(((rows - BIAS_ROWS) // PIECES, width), F32)] * PIECES
-        + [
+        out_specs=whole(2),
+        out_shape=[
             jax.ShapeDtypeStruct((rows - BIAS_ROWS, width), F32),
             jax.ShapeDtypeStruct((1, width), F32),
         ],
@@ -261,95 +292,72 @@
     )(*parts)
 
 
-def place_grads_kernel(ids_ref, mine_ref, *refs):
-    other_refs, (after_ref, self_ref, neigh_ref) = refs[:-3], refs[-3:]
+def place_grads_kernel(ids_ref, mine_ref, other_ref, line_ref, after_ref, self_ref, neigh_ref, bias_ref):
     first = (ids_ref[0] & 1) == 0
-    rows = other_refs[0].shape[0]
-    for i, ref in enumerate(other_refs):
-        at = slice(i * rows, (i + 1) * rows)
-        self_ref[at, :] = jnp.where(first, mine_ref[at, :], ref[...])
-        neigh_ref[at, :] = jnp.where(first, ref[...], mine_ref[at, :])
-
-
-def place_grads(ids, mine, others, after):
+    self_ref[...] = jnp.where(first, mine_ref[...], other_ref[...])
+    neigh_ref[...] = jnp.where(first, other_ref[...], mine_ref[...])
+    bias_ref[...] = line_ref[...]
+
+
+def place_grads(ids, mine, other, line, after):
     out = jax.ShapeDtypeStruct(mine.shape, F32)
     return pl.pallas_call(
         place_grads_kernel,
         in_specs=[pl.BlockSpec(memory_space=pltpu.SMEM)]
-        + whole(1 + len(others))
+        + whole(3)
         + [pl.BlockSpec(memory_space=pl.ANY)],
-        out_specs=whole(2),
-        out_shape=[out, out],
+        out_specs=whole(3),
+        out_shape=[out, out, jax.ShapeDtypeStruct(line.shape, F32)],
         compiler_params=params(),
         name="place_grads",
-    )(ids, mine, *others, after)
-
-
-def stack_messages(message_refs, held):
-    share = message_refs[0].shape[0]
-    for q, ref in enumerate(message_refs):
-        held[q * share : (q + 1) * share, :] = ref[...]
-
-
-def back_even_kernel(n, flip_ref, *refs):
-    out_ref, held = refs[n], refs[n + 1]
-    stack_messages(refs[:n], held)
-    out_ref[...] = dot(flip_ref[:, held.shape[0] :], held[...])
-
-
-def back_even(flip, messages):
-    share, width = messages[0].shape
-    n = len(messages)
-    return pl.pallas_call(
-        functools.partial(back_even_kernel, n),
-        in_specs=whole(1 + n),
-        out_specs=pl.BlockSpec(memory_space=pltpu.VMEM),
-        out_shape=jax.ShapeDtypeStruct((flip.shape[0], width), F32),
-        scratch_shapes=[pltpu.VMEM((n * share, width), BF16)],
-        compiler_params=params(),
-        name="back_even",
-    )(flip, *messages)
-
-
-def back_odd_kernel(n, ids_ref, flip_ref, prior_ref, *refs):
+    )(ids, mine, other, line, after)
+
+
+def back_kernel(n, ids_ref, flip_ref, *refs):
     own_ref, out_refs, held, total = refs[n], refs[n + 1 : -2], refs[-2], refs[-1]
     share = own_ref.shape[0]
-    stack_messages(refs[:n], held)
-    total[...] = prior_ref[...] + dot(flip_ref[:, 0 : held.shape[0]], held[...])
+    for q, ref in enumerate(refs[:n]):
+        held[q * share : (q + 1) * share, :] = ref[...]
+    total[...] = dot(flip_ref[...], held[...])
     own_ref[...] = total[pl.ds(pl.multiple_of(ids_ref[1] * share, share), share), :]
     for k, ref in enumerate(out_refs):
         at = pl.multiple_of((ids_ref[1] ^ (k + 1)) * share, share)
         ref[...] = total[pl.ds(at, share), :].astype(BF16)
 
 
-def back_odd(ids, flip, prior, messages, panels):
+def back_sums(ids, flip, messages, panels):
     share, width = messages[0].shape
     n = len(messages)
     block = jax.ShapeDtypeStruct((share, width), BF16)
     return pl.pallas_call(
-        functools.partial(back_odd_kernel, n),
-        in_specs=[pl.BlockSpec(memory_space=pltpu.SMEM)] + whole(2 + n),
+        functools.partial(back_kernel, n),
+        in_specs=[pl.BlockSpec(memory_space=pltpu.SMEM)] + whole(1 + n),
         out_specs=whole(panels),
         out_shape=[jax.ShapeDtypeStruct((share, width), F32)] + [block] * (panels - 1),
-        scratch_shapes=[pltpu.VMEM((n * share, width), BF16), pltpu.VMEM(prior.shape, F32)],
-        compiler_params=params(),
-        name="back_odd",
-    )(ids, flip, prior, *messages)
+        scratch_shapes=[
+            pltpu.VMEM((n * share, width), BF16),
+            pltpu.VMEM((panels * share, width), F32),
+        ],
+        compiler_params=params(),
+        name="back_sums",
+    )(ids, flip, *messages)
 
 
 def feature_grads_kernel(n, dpre_ref, ws_ref, own_ref, *refs):
     total = own_ref[...]
     for ref in refs[:n]:
         total = total + ref[...].astype(F32)
-    refs[n][...] = (total + dot(dpre_ref[...], ws_ref[...], CONTRACT_SECOND)).astype(BF16)
+    total = total + dot(dpre_ref[...], ws_ref[...], CONTRACT_SECOND)
+    refs[n][...] = total.astype(BF16)
+    refs[n + 1][...] = jnp.zeros_like(refs[n + 1])
 
 
 def feature_grads(dpre, ws, own, recvs):
     return pl.pallas_call(
         functools.partial(feature_grads_kernel, len(recvs)),
         in_specs=whole(3 + len(recvs)),
-        out_specs=pl.BlockSpec(memory_space=pltpu.VMEM),
-        out_shape=jax.ShapeDtypeStruct(dpre.shape, BF16),
+        out_specs=whole(2),
+        out_shape=[jax.ShapeDtypeStruct(dpre.shape, BF16), jax.ShapeDtypeStruct((SPACER_ROWS, dpre.shape[1]), BF16)],
         compiler_params=params(),
         name="feature_grads",
     )(dpre, ws, own, *recvs)
@@ -386,34 +394,40 @@
     )
     deg = jnp.broadcast_to(node_degree.astype(F32)[:, None], (share, width))
 
-    away = partial_sums(ids, dense, gathered, 0, BF16)
-    keep = partial_sums(ids, dense, gathered, 1, F32)
-    sums = chip_sums(keep, xor_permute(away, "rep", 1), chips)
-    recvs = [xor_permute(sums[q], "rep", 2 * q) for q in range(1, chips)]
+    last = chips - 1
+    away_far, held = away_far_sums(ids, dense, gathered, last)
+    away = away_near_sums(dense, held, last, share)
+    (far,) = chip_sums(dense, [xor_permute(away_far, "rep", 1)], held, chips + last, [BF16], "chip_far")
+    far = xor_permute(far, "rep", 2 * last)
+    sums = chip_sums(
+        dense, [xor_permute(value, "rep", 1) for value in away], held, chips,
+        [F32] + [BF16] * (last - 1), "chip_near",
+    )
+    recvs = [xor_permute(sums[q], "rep", 2 * q) for q in reversed(range(1, last))]
+    agg = add_far(sums[0], far)
     hidden_out, dpre, message, grad_away, grad_keep = rows_step(
-        ids, own, self_weight, neigh_weight, out_bias[None, :], deg, cotangent, sums[0], recvs, scale
-    )
-
-    even = [message] + [xor_permute(message, "rep", 2 * q) for q in range(1, chips)]
+        ids, own, self_weight, neigh_weight, out_bias[None, :], deg, cotangent, agg, recvs, scale
+    )
+
+    even = [xor_permute(message, "rep", 2 * q) for q in reversed(range(1, chips))]
+    even = [message] + even[::-1]
     odd = [xor_permute(value, "rep", 1) for value in even]
-    half = back_even(flip, even)
-    spread = back_odd(ids, flip, half, odd, panels)
-    token = spread[0]
+    spread = back_sums(ids, flip, odd + even, panels)
 
     line = pair_grads(grad_keep, xor_permute(grad_away, "rep", 1))
     k = 1
     while k < row_devices:
-        after = [token] if 2 * k == row_devices else []
-        line = line_grads([line, xor_permute(line, "row", k)], after)
+        line = line_grads([line, xor_permute(line, "row", k)])
         k *= 2
-    *pieces, mine, grad_bias = all_grads(
+    arrived = [xor_permute(spread[k], "row", k) for k in range(1, row_devices)]
+    grad_features, spacer = feature_grads(dpre, self_weight, spread[0], arrived)
+    late = xor_permute(spacer, "rep", 1)
+    mine, bias_line = all_grads(
         [line] + [xor_permute(line, "rep", 2 * q) for q in range(1, chips)]
     )
-    arrived = [xor_permute(spread[k], "row", k) for k in range(1, row_devices)]
-    grad_features = feature_grads(dpre, self_weight, spread[0], arrived)
-    late = xor_permute(grad_features, "rep", 1)
-    others = [xor_permute(piece, "rep", 1) for piece in pieces]
-    grad_self, grad_neigh = place_grads(ids, mine, others, late)
+    grad_self, grad_neigh, grad_bias = place_grads(
+        ids, mine, xor_permute(mine, "rep", 1), bias_line, late
+    )
     return (hidden_out, grad_features, grad_self, grad_neigh, grad_bias[0])
 
 

time: 67.4 us -> 66.1 us (0.981)
  Pallas kernels: 12.2 us -> 11.3 us
    pallas_call x5 -> x6, Pallas kernels: 4.67 us -> 4.23 us  [the longest x1 1.85 us: back_sums(): pl.pallas_call(functools.partial(back_kernel, n), in_specs=[pl.BlockSpec(...]
  transfers between devices with their start and end apart: 28 -> 28, of which waited for: 15 -> 11; matrix products, arithmetic and copies ran while one was open for 0% -> 0% of each run, Pallas kernels for 12% -> 11%
where the time goes in v3:
time: 66.1 us; the launch traced here: 65.7 us
  starting transfers between devices  28.1 us (43%)
  waiting for transfers between devices  20.4 us (31%)
  Pallas kernels  11.3 us (17%)
  local copies, waits for them, and re-layouts  4.9 us (7%)
  between operations  0.85 us (1%)
    ppermute x28, starting transfers between devices, xor_permute(): lax.ppermute(value, axis, [(i, i ^ k) for i in range(lax.axis_size(axis))])  28.1 us
    ppermute x28, waiting for transfers between devices, xor_permute(): lax.ppermute(value, axis, [(i, i ^ k) for i in range(lax.axis_size(axis))])  20.4 us
    unnamed x18, local copies, waits for them, and re-layouts  4.8 us
    pallas_call x1, Pallas kernels, build_strip(): pl.pallas_call(functools.partial(strip_kernel, panels, blocks, tile, chip...  2.92 us
    pallas_call x1, Pallas kernels, back_sums(): pl.pallas_call(functools.partial(back_kernel, n), in_specs=[pl.BlockSpec(...  1.85 us
    pallas_call x1, Pallas kernels, rows_step(): pl.pallas_call(functools.partial(rows_kernel, m, scale), in_specs=[pl.Blo...  1.67 us
    pallas_call x1, Pallas kernels, place_grads(): pl.pallas_call(place_grads_kernel, in_specs=[pl.BlockSpec(memory_space=pl...  1.38 us
  transfers between devices with their start and end apart: 28, of which 11 were waited for; matrix products, arithmetic and copies ran while one was open for 0% of the time, Pallas kernels for 11%

profile of v3, /device:TPU:0, one launch (start us, length us, event | category | flops | bytes accessed | tf_op | source)
XLA Modules:
  0.0 65.7 jit_solution(6149861227098917498)
XLA Ops:
  0.6 0.0 copy-start
  0.7 1.2 %copy-done = bf16[2048,256]{1,0:T(8,128)(2,1)S(1)} copy-done((bf16[2048,256]{1,0:T(8,128)(2,1)S(1)}, bf16[2048,256]{1,0:T(8,128)(2,1)}, u32[]{:S(2)}) %copy-start) | copy-done | bytes 1048600
  1.9 3.1 %collective-permute-start = (bf16[256,256]{1,0:T(8,128)(2,1)S(1)}, bf16[256,256]{1,0:T(8,128)(2,1)S(1)}, u32[]{:S(2)}, u32[]{:S(2)}) collective-permute-start(bf16[256,256]{1,0:T(8,128)(2,1)S(1)} %constant_dynamic-slice_fusion.refs_0_.own_ref), channel_id=1, source_target_pairs={{0,8},{8,0},{16,24},{24,16},{1,9},{9,1},{17,25},{25,17},{2,10},{10... | collective-permute-start | bytes 393224 | tf_op jit(solution)/shard_map/ppermute | solution.py:46
  5.0 2.6 %collective-permute-start.1 = (bf16[256,256]{1,0:T(8,128)(2,1)S(1)}, bf16[256,256]{1,0:T(8,128)(2,1)S(1)}, u32[]{:S(2)}, u32[]{:S(2)}) collective-permute-start(bf16[256,256]{1,0:T(8,128)(2,1)S(1)} %constant_dynamic-slice_fusion.refs_0_.own_ref), channel_id=1, source_target_pairs={{0,16},{8,24},{16,0},{24,8},{1,17},{9,25},{17,1},{25,9},{2,18},{10... | collective-permute-start | bytes 393224 | tf_op jit(solution)/shard_map/ppermute | solution.py:46
  7.6 0.0 collective-permute-start.2
  7.6 0.1 pad_add_fusion.ids_ref
  7.6 2.2 %copy-done.1 = s32[2048,4,128]{2,1,0:T(4,128)S(1)} copy-done((s32[2048,4,128]{2,1,0:T(4,128)S(1)}, s32[2048,4,128]{2,1,0:T(4,128)}, u32[]{:S(2)}) %copy-start.1) | copy-done | bytes 4194328
  9.8 0.7 %copy-done.5 = s32[16,4]{0,1:T(4,128)S(1)} copy-done((s32[16,4]{0,1:T(4,128)S(1)}, s32[16,4]{0,1:T(4,128)}, u32[]{:S(2)}) %copy-start.5) | copy-done | bytes 280
  10.5 0.7 %copy-done.6 = s32[16,4]{0,1:T(4,128)S(1)} copy-done((s32[16,4]{0,1:T(4,128)S(1)}, s32[16,4]{0,1:T(4,128)}, u32[]{:S(2)}) %copy-start.6) | copy-done | bytes 280
  11.2 2.9 %build_strip.1 = (bf16[2048,1024]{1,0:T(8,128)(2,1)S(1)}, bf16[1024,2048]{1,0:T(8,128)(2,1)S(1)}) custom-call(s32[2]{0:T(128)S(1)} %pad_add_fusion.ids_ref, s32[4,16]{1,0:T(4,128)S(1)} %bitcast.8, s32[4,16]{1,0:T(4,128)S(1)} %bitcast.9, s32[8192,128]{1,0:T(8,128)S(1)} %bitcast.7), custom_call_target="tpu_custom_call" | custom-call | tf_op jit(solution)/shard_map/build_strip/pallas_call | solution.py:73
  14.1 0.0 collective-permute-done.refs_1_
  14.1 3.8 %collective-permute-done.1.refs_2_ = bf16[256,256]{1,0:T(8,128)(2,1)S(1)} collective-permute-done((bf16[256,256]{1,0:T(8,128)(2,1)S(1)}, bf16[256,256]{1,0:T(8,128)(2,1)S(1)}, u32[]{:S(2)}, u32[]{:S(2)}) %collective-permute-start.1) | collective-permute-done | bytes 131104 | tf_op jit(solution)/shard_map/ppermute | solution.py:46
  17.9 0.0 collective-permute-done.2.refs_3_
  17.9 0.9 %away_far.1 = (bf16[256,256]{1,0:T(8,128)(2,1)S(1)}, bf16[1024,256]{1,0:T(8,128)(2,1)S(1)}) custom-call(s32[2]{0:T(128)S(1)} %pad_add_fusion.ids_ref, bf16[2048,1024]{1,0:T(8,128)(2,1)S(1)} %get-tuple-element.31.dense_ref, bf16[256,256]{1,0:T(8,128)(2,1)S(1)} %constant_dynamic-slice_fusion.refs_0_.own_ref, ...), custom_call_target="tpu_custom_call" | custom-call | tf_op jit(solution)/shard_map/away_far/pallas_call | solution.py:114
  18.8 0.1 collective-permute-start.6
  18.9 0.6 away_near.1
  19.4 0.6 collective-permute-start.3
  20.0 0.1 collective-permute-start.4
  20.1 0.4 collective-permute-start.5
  20.5 0.0 collective-permute-done.6.refs_0_
  20.5 0.3 chip_far.1
  20.8 0.0 copy-start.2
  20.9 0.0 copy-start.3
  20.9 0.0 copy-start.4
  20.9 0.0 copy-start.7
  20.9 2.5 %collective-permute-start.7 = (bf16[256,256]{1,0:T(8,128)(2,1)S(1)}, bf16[256,256]{1,0:T(8,128)(2,1)S(1)}, u32[]{:S(2)}, u32[]{:S(2)}) collective-permute-start(bf16[256,256]{1,0:T(8,128)(2,1)S(1)} %chip_far.1), channel_id=1, source_target_pairs={{0,6},{1,7},{2,4},{3,5},{4,2},{5,3},{6,0},{7,1},{8,14},{9,15},{10,... | collective-permute-start | bytes 393224 | tf_op jit(solution)/shard_map/ppermute | solution.py:46
  23.4 0.0 collective-permute-done.3.refs_0_
  23.4 0.0 collective-permute-done.4.refs_1_
  23.4 0.6 chip_near.1
  24.0 0.6 collective-permute-start.8
  24.6 0.6 collective-permute-start.9
  25.2 2.2 %collective-permute-done.7.far_ref = bf16[256,256]{1,0:T(8,128)(2,1)S(1)} collective-permute-done((bf16[256,256]{1,0:T(8,128)(2,1)S(1)}, bf16[256,256]{1,0:T(8,128)(2,1)S(1)}, u32[]{:S(2)}, u32[]{:S(2)}) %collective-permute-start.7) | collective-permute-done | bytes 131104 | tf_op jit(solution)/shard_map/ppermute | solution.py:46
  27.5 2.7 %collective-permute-done.8.refs_0_ = bf16[256,256]{1,0:T(8,128)(2,1)S(1)} collective-permute-done((bf16[256,256]{1,0:T(8,128)(2,1)S(1)}, bf16[256,256]{1,0:T(8,128)(2,1)S(1)}, u32[]{:S(2)}, u32[]{:S(2)}) %collective-permute-start.8) | collective-permute-done | bytes 131104 | tf_op jit(solution)/shard_map/ppermute | solution.py:46
  30.1 0.1 collective-permute-done.9.refs_1_
  30.2 0.1 broadcast_in_dim.10.deg_ref
  30.3 1.7 %rows_step.1 = (bf16[256,256]{1,0:T(8,128)(2,1)}, bf16[256,256]{1,0:T(8,128)(2,1)S(1)}, bf16[256,256]{1,0:T(8,128)(2,1)S(1)}, f32[272,256]{1,0:T(8,128)S(1)}, f32[272,256]{1,0:T(8,128)S(1)}) custom-call(s32[2]{0:T(128)S(1)} %pad_add_fusion.ids_ref, bf16[256,256]{1,0:T(8,128)(2,1)S(1)} %constant_dynamic-slice_fusion.refs_0_.own_ref, ...), custom_call_target="tpu_custom_call" | custom-call | tf_op jit(solution)/shard_map/rows_step/pallas_call | solution.py:213
  32.0 1.5 %collective-permute-start.11 = (bf16[256,256]{1,0:T(8,128)(2,1)S(1)}, bf16[256,256]{1,0:T(8,128)(2,1)S(1)}, u32[]{:S(2)}, u32[]{:S(2)}) collective-permute-start(bf16[256,256]{1,0:T(8,128)(2,1)S(1)} %get-tuple-element.43.refs_4_), channel_id=1, source_target_pairs={{0,2},{1,3},{2,0},{3,1},{4,6},{5,7},{6,4},{7,5},{8,10},{9,11},{10,... | collective-permute-start | bytes 393224 | tf_op jit(solution)/shard_map/ppermute | solution.py:46
  33.5 1.5 %collective-permute-start.13 = (bf16[256,256]{1,0:T(8,128)(2,1)S(1)}, bf16[256,256]{1,0:T(8,128)(2,1)S(1)}, u32[]{:S(2)}, u32[]{:S(2)}) collective-permute-start(bf16[256,256]{1,0:T(8,128)(2,1)S(1)} %get-tuple-element.43.refs_4_), channel_id=1, source_target_pairs={{0,4},{1,5},{2,6},{3,7},{4,0},{5,1},{6,2},{7,3},{8,12},{9,13},{10,... | collective-permute-start | bytes 393224 | tf_op jit(solution)/shard_map/ppermute | solution.py:46
  35.0 0.5 collective-permute-start.15
  35.5 0.0 collective-permute-done.20.recv_ref
  35.5 0.1 pair_grads.1.refs_0_
  35.6 2.0 %collective-permute-start.21 = (bf16[272,256]{1,0:T(8,128)(2,1)S(1)}, bf16[272,256]{1,0:T(8,128)(2,1)S(1)}, u32[]{:S(2)}, u32[]{:S(2)}) collective-permute-start(bf16[272,256]{1,0:T(8,128)(2,1)S(1)} %pair_grads.1.refs_0_), channel_id=1, source_target_pairs={{0,8},{8,0},{16,24},{24,16},{1,9},{9,1},{17,25},{25,17},{2,10},{10... | collective-permute-start | bytes 417800 | tf_op jit(solution)/shard_map/ppermute | solution.py:46
  37.6 0.0 collective-permute-start.10
  37.6 0.7 %collective-permute-done.11.refs_5_ = bf16[256,256]{1,0:T(8,128)(2,1)S(1)} collective-permute-done((bf16[256,256]{1,0:T(8,128)(2,1)S(1)}, bf16[256,256]{1,0:T(8,128)(2,1)S(1)}, u32[]{:S(2)}, u32[]{:S(2)}) %collective-permute-start.11) | collective-permute-done | bytes 131104 | tf_op jit(solution)/shard_map/ppermute | solution.py:46
  38.3 0.0 collective-permute-start.12
  38.3 3.6 %collective-permute-done.13.refs_6_ = bf16[256,256]{1,0:T(8,128)(2,1)S(1)} collective-permute-done((bf16[256,256]{1,0:T(8,128)(2,1)S(1)}, bf16[256,256]{1,0:T(8,128)(2,1)S(1)}, u32[]{:S(2)}, u32[]{:S(2)}) %collective-permute-start.13) | collective-permute-done | bytes 131104 | tf_op jit(solution)/shard_map/ppermute | solution.py:46
  41.9 0.5 collective-permute-start.16
  42.5 3.0 %collective-permute-start.22 = (bf16[272,256]{1,0:T(8,128)(2,1)S(1)}, bf16[272,256]{1,0:T(8,128)(2,1)S(1)}, u32[]{:S(2)}, u32[]{:S(2)}) collective-permute-start(bf16[272,256]{1,0:T(8,128)(2,1)S(1)} %line_grads.2.refs_0_), channel_id=1, source_target_pairs={{0,16},{8,24},{16,0},{24,8},{1,17},{9,25},{17,1},{25,9},{2,18},{10... | collective-permute-start | bytes 417800 | tf_op jit(solution)/shard_map/ppermute | solution.py:46
  45.6 1.9 %back_sums.1 = (f32[256,256]{1,0:T(8,128)S(1)}, bf16[256,256]{1,0:T(8,128)(2,1)S(1)}, bf16[256,256]{1,0:T(8,128)(2,1)S(1)}, bf16[256,256]{1,0:T(8,128)(2,1)S(1)}) custom-call(s32[2]{0:T(128)S(1)} %pad_add_fusion.ids_ref, bf16[1024,2048]{1,0:T(8,128)(2,1)S(1)} %get-tuple-element.42.flip_ref, bf16[256,256]{1,0:T(8,128)(2,1)S(1)} %collective-permute-done.10.refs_0_, ...), custom_call_target="tpu_custom_call" | custom-call | tf_op jit(solution)/shard_map/back_sums/pallas_call | solution.py:332
  47.4 0.1 collective-permute-start.17
  47.5 1.9 %collective-permute-start.18 = (bf16[256,256]{1,0:T(8,128)(2,1)S(1)}, bf16[256,256]{1,0:T(8,128)(2,1)S(1)}, u32[]{:S(2)}, u32[]{:S(2)}) collective-permute-start(bf16[256,256]{1,0:T(8,128)(2,1)S(1)} %get-tuple-element.46), channel_id=1, source_target_pairs={{0,16},{8,24},{16,0},{24,8},{1,17},{9,25},{17,1},{25,9},{2,18},{10... | collective-permute-start | bytes 393224 | tf_op jit(solution)/shard_map/ppermute | solution.py:46
  49.4 2.5 %collective-permute-start.19 = (bf16[256,256]{1,0:T(8,128)(2,1)S(1)}, bf16[256,256]{1,0:T(8,128)(2,1)S(1)}, u32[]{:S(2)}, u32[]{:S(2)}) collective-permute-start(bf16[256,256]{1,0:T(8,128)(2,1)S(1)} %get-tuple-element.47), channel_id=1, source_target_pairs={{0,24},{8,16},{16,8},{24,0},{1,25},{9,17},{17,9},{25,1},{2,26},{10... | collective-permute-start | bytes 393224 | tf_op jit(solution)/shard_map/ppermute | solution.py:46
  51.9 1.3 %collective-permute-done.22.refs_1_ = bf16[272,256]{1,0:T(8,128)(2,1)S(1)} collective-permute-done((bf16[272,256]{1,0:T(8,128)(2,1)S(1)}, bf16[272,256]{1,0:T(8,128)(2,1)S(1)}, u32[]{:S(2)}, u32[]{:S(2)}) %collective-permute-start.22) | collective-permute-done | bytes 139296 | tf_op jit(solution)/shard_map/ppermute | solution.py:46
  53.2 0.8 %collective-permute-start.23 = (bf16[272,256]{1,0:T(8,128)(2,1)S(1)}, bf16[272,256]{1,0:T(8,128)(2,1)S(1)}, u32[]{:S(2)}, u32[]{:S(2)}) collective-permute-start(bf16[272,256]{1,0:T(8,128)(2,1)S(1)} %line_grads.3.refs_0_), channel_id=1, source_target_pairs={{0,2},{1,3},{2,0},{3,1},{4,6},{5,7},{6,4},{7,5},{8,10},{9,11},{10,... | collective-permute-start | bytes 417800 | tf_op jit(solution)/shard_map/ppermute | solution.py:46
  53.9 1.3 %collective-permute-start.24 = (bf16[272,256]{1,0:T(8,128)(2,1)S(1)}, bf16[272,256]{1,0:T(8,128)(2,1)S(1)}, u32[]{:S(2)}, u32[]{:S(2)}) collective-permute-start(bf16[272,256]{1,0:T(8,128)(2,1)S(1)} %line_grads.3.refs_0_), channel_id=1, source_target_pairs={{0,4},{1,5},{2,6},{3,7},{4,0},{5,1},{6,2},{7,3},{8,12},{9,13},{10,... | collective-permute-start | bytes 417800 | tf_op jit(solution)/shard_map/ppermute | solution.py:46
  55.2 0.4 collective-permute-done.17.refs_0_
  55.6 1.5 %collective-permute-start.25 = (bf16[272,256]{1,0:T(8,128)(2,1)S(1)}, bf16[272,256]{1,0:T(8,128)(2,1)S(1)}, u32[]{:S(2)}, u32[]{:S(2)}) collective-permute-start(bf16[272,256]{1,0:T(8,128)(2,1)S(1)} %line_grads.3.refs_0_), channel_id=1, source_target_pairs={{0,6},{1,7},{2,4},{3,5},{4,2},{5,3},{6,0},{7,1},{8,14},{9,15},{10,... | collective-permute-start | bytes 417800 | tf_op jit(solution)/shard_map/ppermute | solution.py:46
  57.1 4.4 %collective-permute-done.18.refs_1_ = bf16[256,256]{1,0:T(8,128)(2,1)S(1)} collective-permute-done((bf16[256,256]{1,0:T(8,128)(2,1)S(1)}, bf16[256,256]{1,0:T(8,128)(2,1)S(1)}, u32[]{:S(2)}, u32[]{:S(2)}) %collective-permute-start.18) | collective-permute-done | bytes 131104 | tf_op jit(solution)/shard_map/ppermute | solution.py:46
  61.5 0.9 %feature_grads.1 = (bf16[256,256]{1,0:T(8,128)(2,1)}, bf16[576,256]{1,0:T(8,128)(2,1)S(1)}) custom-call(bf16[256,256]{1,0:T(8,128)(2,1)S(1)} %get-tuple-element.41.dpre_ref, bf16[256,256]{1,0:T(8,128)(2,1)S(1)} %copy-done.2, f32[256,256]{1,0:T(8,128)S(1)} %get-tuple-element.44.own_ref, bf16[256,256]{1,0:T(8,128)(2,1)S(1)} %collective-permute-done.17.refs_0_, ...), custom_call_target="tpu_custom_call" | custom-call | tf_op jit(solution)/shard_map/feature_grads/pallas_call | solution.py:356
  62.4 0.1 all_grads.1
  62.4 0.6 collective-permute-start.26
  63.0 0.9 %collective-permute-done.27.after_ref = bf16[576,256]{1,0:T(8,128)(2,1)S(1)} collective-permute-done((bf16[576,256]{1,0:T(8,128)(2,1)S(1)}, bf16[576,256]{1,0:T(8,128)(2,1)S(1)}, u32[]{:S(2)}, u32[]{:S(2)}) %collective-permute-start.27) | collective-permute-done | bytes 294944 | tf_op jit(solution)/shard_map/ppermute | solution.py:46
  63.9 0.4 collective-permute-done.26.other_ref
  64.3 1.4 %place_grads.1 = (f32[256,256]{1,0:T(8,128)}, f32[256,256]{1,0:T(8,128)}, f32[1,256]{1,0:T(1,128)}) custom-call(s32[2]{0:T(128)S(1)} %pad_add_fusion.ids_ref, f32[256,256]{1,0:T(8,128)S(1)} %get-tuple-element.51.mine_ref, f32[256,256]{1,0:T(8,128)S(1)} %collective-permute-done.26.other_ref, f32[1,256]{1,0:T(1,128)S(1)} %get-tuple-element.52.line_ref, ...), custom_call_target="tpu_custom_call" | custom-call | tf_op jit(solution)/shard_map/place_grads/pallas_call | solution.py:304
  (28 shorter events, 0.2 us)
Async XLA Ops:
  0.6 1.2 %copy-start = (bf16[2048,256]{1,0:T(8,128)(2,1)S(1)}, bf16[2048,256]{1,0:T(8,128)(2,1)}, u32[]{:S(2)}) copy-start(bf16[2048,256]{1,0:T(8,128)(2,1)} %param.9) | copy-start | bytes 3145732
  1.9 12.2 %collective-permute-start = (bf16[256,256]{1,0:T(8,128)(2,1)S(1)}, bf16[256,256]{1,0:T(8,128)(2,1)S(1)}, u32[]{:S(2)}, u32[]{:S(2)}) collective-permute-start(bf16[256,256]{1,0:T(8,128)(2,1)S(1)} %constant_dynamic-slice_fusion.refs_0_.own_ref), channel_id=1, source_target_pairs={{0,8},{8,0},{16,24},{24,16},{1,9},{9,1},{17,25},{25,17},{2,10},{10... | collective-permute-start | bytes 393224 | tf_op jit(solution)/shard_map/ppermute | solution.py:46
  5.0 12.9 %collective-permute-start.1 = (bf16[256,256]{1,0:T(8,128)(2,1)S(1)}, bf16[256,256]{1,0:T(8,128)(2,1)S(1)}, u32[]{:S(2)}, u32[]{:S(2)}) collective-permute-start(bf16[256,256]{1,0:T(8,128)(2,1)S(1)} %constant_dynamic-slice_fusion.refs_0_.own_ref), channel_id=1, source_target_pairs={{0,16},{8,24},{16,0},{24,8},{1,17},{9,25},{17,1},{25,9},{2,18},{10... | collective-permute-start | bytes 393224 | tf_op jit(solution)/shard_map/ppermute | solution.py:46
  7.6 10.3 %collective-permute-start.2 = (bf16[256,256]{1,0:T(8,128)(2,1)S(1)}, bf16[256,256]{1,0:T(8,128)(2,1)S(1)}, u32[]{:S(2)}, u32[]{:S(2)}) collective-permute-start(bf16[256,256]{1,0:T(8,128)(2,1)S(1)} %constant_dynamic-slice_fusion.refs_0_.own_ref), channel_id=1, source_target_pairs={{0,24},{8,16},{16,8},{24,0},{1,25},{9,17},{17,9},{25,1},{2,26},{10... | collective-permute-start | bytes 393224 | tf_op jit(solution)/shard_map/ppermute | solution.py:46
  7.6 2.2 %copy-start.1 = (s32[2048,4,128]{2,1,0:T(4,128)S(1)}, s32[2048,4,128]{2,1,0:T(4,128)}, u32[]{:S(2)}) copy-start(s32[2048,4,128]{2,1,0:T(4,128)} %param.13) | copy-start | bytes 12582916
  9.8 0.7 %copy-start.5 = (s32[16,4]{0,1:T(4,128)S(1)}, s32[16,4]{0,1:T(4,128)}, u32[]{:S(2)}) copy-start(s32[16,4]{0,1:T(4,128)} %param.14) | copy-start | bytes 772
  10.5 0.7 %copy-start.6 = (s32[16,4]{0,1:T(4,128)S(1)}, s32[16,4]{0,1:T(4,128)}, u32[]{:S(2)}) copy-start(s32[16,4]{0,1:T(4,128)} %param.15) | copy-start | bytes 772
  18.8 1.7 %collective-permute-start.6 = (bf16[256,256]{1,0:T(8,128)(2,1)S(1)}, bf16[256,256]{1,0:T(8,128)(2,1)S(1)}, u32[]{:S(2)}, u32[]{:S(2)}) collective-permute-start(bf16[256,256]{1,0:T(8,128)(2,1)S(1)} %get-tuple-element.37), channel_id=1, source_target_pairs={{0,1},{1,0},{2,3},{3,2},{4,5},{5,4},{6,7},{7,6},{8,9},{9,8},{10,11... | collective-permute-start | bytes 393224 | tf_op jit(solution)/shard_map/ppermute | solution.py:46
  19.4 4.0 %collective-permute-start.3 = (bf16[256,256]{1,0:T(8,128)(2,1)S(1)}, bf16[256,256]{1,0:T(8,128)(2,1)S(1)}, u32[]{:S(2)}, u32[]{:S(2)}) collective-permute-start(bf16[256,256]{1,0:T(8,128)(2,1)S(1)} %get-tuple-element.33), channel_id=1, source_target_pairs={{0,1},{1,0},{2,3},{3,2},{4,5},{5,4},{6,7},{7,6},{8,9},{9,8},{10,11... | collective-permute-start | bytes 393224 | tf_op jit(solution)/shard_map/ppermute | solution.py:46
  20.0 3.4 %collective-permute-start.4 = (bf16[256,256]{1,0:T(8,128)(2,1)S(1)}, bf16[256,256]{1,0:T(8,128)(2,1)S(1)}, u32[]{:S(2)}, u32[]{:S(2)}) collective-permute-start(bf16[256,256]{1,0:T(8,128)(2,1)S(1)} %get-tuple-element.34), channel_id=1, source_target_pairs={{0,1},{1,0},{2,3},{3,2},{4,5},{5,4},{6,7},{7,6},{8,9},{9,8},{10,11... | collective-permute-start | bytes 393224 | tf_op jit(solution)/shard_map/ppermute | solution.py:46
  20.1 5.1 %copy-start.8 = (s32[256]{0:T(256)S(1)}, s32[256]{0:T(256)}, u32[]{:S(2)}) copy-start(s32[256]{0:T(256)} %param.16) | copy-start | bytes 3076
  20.1 3.3 %collective-permute-start.5 = (bf16[256,256]{1,0:T(8,128)(2,1)S(1)}, bf16[256,256]{1,0:T(8,128)(2,1)S(1)}, u32[]{:S(2)}, u32[]{:S(2)}) collective-permute-start(bf16[256,256]{1,0:T(8,128)(2,1)S(1)} %get-tuple-element.35), channel_id=1, source_target_pairs={{0,1},{1,0},{2,3},{3,2},{4,5},{5,4},{6,7},{7,6},{8,9},{9,8},{10,11... | collective-permute-start | bytes 393224 | tf_op jit(solution)/shard_map/ppermute | solution.py:46
  20.8 9.5 %copy-start.2 = (bf16[256,256]{1,0:T(8,128)(2,1)S(1)}, bf16[256,256]{1,0:T(8,128)(2,1)}, u32[]{:S(2)}) copy-start(bf16[256,256]{1,0:T(8,128)(2,1)} %ws_ref.3) | copy-start | bytes 393220
  20.9 9.5 %copy-start.3 = (bf16[256,256]{1,0:T(8,128)(2,1)S(1)}, bf16[256,256]{1,0:T(8,128)(2,1)}, u32[]{:S(2)}) copy-start(bf16[256,256]{1,0:T(8,128)(2,1)} %wn_ref.1) | copy-start | bytes 393220
  20.9 9.5 %copy-start.4 = (bf16[256,256]{1,0:T(8,128)(2,1)S(1)}, bf16[256,256]{1,0:T(8,128)(2,1)}, u32[]{:S(2)}) copy-start(bf16[256,256]{1,0:T(8,128)(2,1)} %cot_ref.1) | copy-start | bytes 393220
  20.9 9.5 %copy-start.7 = (f32[256]{0:T(256)S(1)}, f32[256]{0:T(256)}, u32[]{:S(2)}) copy-start(f32[256]{0:T(256)} %param.12) | copy-start | bytes 3076
  20.9 6.5 %collective-permute-start.7 = (bf16[256,256]{1,0:T(8,128)(2,1)S(1)}, bf16[256,256]{1,0:T(8,128)(2,1)S(1)}, u32[]{:S(2)}, u32[]{:S(2)}) collective-permute-start(bf16[256,256]{1,0:T(8,128)(2,1)S(1)} %chip_far.1), channel_id=1, source_target_pairs={{0,6},{1,7},{2,4},{3,5},{4,2},{5,3},{6,0},{7,1},{8,14},{9,15},{10,... | collective-permute-start | bytes 393224 | tf_op jit(solution)/shard_map/ppermute | solution.py:46
  24.0 6.1 %collective-permute-start.8 = (bf16[256,256]{1,0:T(8,128)(2,1)S(1)}, bf16[256,256]{1,0:T(8,128)(2,1)S(1)}, u32[]{:S(2)}, u32[]{:S(2)}) collective-permute-start(bf16[256,256]{1,0:T(8,128)(2,1)S(1)} %get-tuple-element.38), channel_id=1, source_target_pairs={{0,4},{1,5},{2,6},{3,7},{4,0},{5,1},{6,2},{7,3},{8,12},{9,13},{10,... | collective-permute-start | bytes 393224 | tf_op jit(solution)/shard_map/ppermute | solution.py:46
  24.6 5.6 %collective-permute-start.9 = (bf16[256,256]{1,0:T(8,128)(2,1)S(1)}, bf16[256,256]{1,0:T(8,128)(2,1)S(1)}, u32[]{:S(2)}, u32[]{:S(2)}) collective-permute-start(bf16[256,256]{1,0:T(8,128)(2,1)S(1)} %get-tuple-element.39), channel_id=1, source_target_pairs={{0,2},{1,3},{2,0},{3,1},{4,6},{5,7},{6,4},{7,5},{8,10},{9,11},{10,... | collective-permute-start | bytes 393224 | tf_op jit(solution)/shard_map/ppermute | solution.py:46
  32.0 3.5 %collective-permute-start.20 = (f32[272,256]{1,0:T(8,128)S(1)}, f32[272,256]{1,0:T(8,128)S(1)}, u32[]{:S(2)}, u32[]{:S(2)}) collective-permute-start(f32[272,256]{1,0:T(8,128)S(1)} %get-tuple-element.50), channel_id=1, source_target_pairs={{0,1},{1,0},{2,3},{3,2},{4,5},{5,4},{6,7},{7,6},{8,9},{9,8},{10,11... | collective-permute-start | bytes 835592 | tf_op jit(solution)/shard_map/ppermute | solution.py:46
  32.0 6.3 %collective-permute-start.11 = (bf16[256,256]{1,0:T(8,128)(2,1)S(1)}, bf16[256,256]{1,0:T(8,128)(2,1)S(1)}, u32[]{:S(2)}, u32[]{:S(2)}) collective-permute-start(bf16[256,256]{1,0:T(8,128)(2,1)S(1)} %get-tuple-element.43.refs_4_), channel_id=1, source_target_pairs={{0,2},{1,3},{2,0},{3,1},{4,6},{5,7},{6,4},{7,5},{8,10},{9,11},{10,... | collective-permute-start | bytes 393224 | tf_op jit(solution)/shard_map/ppermute | solution.py:46
  33.5 8.4 %collective-permute-start.13 = (bf16[256,256]{1,0:T(8,128)(2,1)S(1)}, bf16[256,256]{1,0:T(8,128)(2,1)S(1)}, u32[]{:S(2)}, u32[]{:S(2)}) collective-permute-start(bf16[256,256]{1,0:T(8,128)(2,1)S(1)} %get-tuple-element.43.refs_4_), channel_id=1, source_target_pairs={{0,4},{1,5},{2,6},{3,7},{4,0},{5,1},{6,2},{7,3},{8,12},{9,13},{10,... | collective-permute-start | bytes 393224 | tf_op jit(solution)/shard_map/ppermute | solution.py:46
  35.0 6.9 %collective-permute-start.15 = (bf16[256,256]{1,0:T(8,128)(2,1)S(1)}, bf16[256,256]{1,0:T(8,128)(2,1)S(1)}, u32[]{:S(2)}, u32[]{:S(2)}) collective-permute-start(bf16[256,256]{1,0:T(8,128)(2,1)S(1)} %get-tuple-element.43.refs_4_), channel_id=1, source_target_pairs={{0,6},{1,7},{2,4},{3,5},{4,2},{5,3},{6,0},{7,1},{8,14},{9,15},{10,... | collective-permute-start | bytes 393224 | tf_op jit(solution)/shard_map/ppermute | solution.py:46
  35.6 6.9 %collective-permute-start.21 = (bf16[272,256]{1,0:T(8,128)(2,1)S(1)}, bf16[272,256]{1,0:T(8,128)(2,1)S(1)}, u32[]{:S(2)}, u32[]{:S(2)}) collective-permute-start(bf16[272,256]{1,0:T(8,128)(2,1)S(1)} %pair_grads.1.refs_0_), channel_id=1, source_target_pairs={{0,8},{8,0},{16,24},{24,16},{1,9},{9,1},{17,25},{25,17},{2,10},{10... | collective-permute-start | bytes 417800 | tf_op jit(solution)/shard_map/ppermute | solution.py:46
  37.6 8.0 %collective-permute-start.10 = (bf16[256,256]{1,0:T(8,128)(2,1)S(1)}, bf16[256,256]{1,0:T(8,128)(2,1)S(1)}, u32[]{:S(2)}, u32[]{:S(2)}) collective-permute-start(bf16[256,256]{1,0:T(8,128)(2,1)S(1)} %get-tuple-element.43.refs_4_), channel_id=1, source_target_pairs={{0,1},{1,0},{2,3},{3,2},{4,5},{5,4},{6,7},{7,6},{8,9},{9,8},{10,11... | collective-permute-start | bytes 393224 | tf_op jit(solution)/shard_map/ppermute | solution.py:46
  38.3 7.2 %collective-permute-start.12 = (bf16[256,256]{1,0:T(8,128)(2,1)S(1)}, bf16[256,256]{1,0:T(8,128)(2,1)S(1)}, u32[]{:S(2)}, u32[]{:S(2)}) collective-permute-start(bf16[256,256]{1,0:T(8,128)(2,1)S(1)} %collective-permute-done.11.refs_5_), channel_id=1, source_target_pairs={{0,1},{1,0},{2,3},{3,2},{4,5},{5,4},{6,7},{7,6},{8,9},{9,8},{10,11... | collective-permute-start | bytes 393224 | tf_op jit(solution)/shard_map/ppermute | solution.py:46
  41.9 3.6 %collective-permute-start.14 = (bf16[256,256]{1,0:T(8,128)(2,1)S(1)}, bf16[256,256]{1,0:T(8,128)(2,1)S(1)}, u32[]{:S(2)}, u32[]{:S(2)}) collective-permute-start(bf16[256,256]{1,0:T(8,128)(2,1)S(1)} %collective-permute-done.13.refs_6_), channel_id=1, source_target_pairs={{0,1},{1,0},{2,3},{3,2},{4,5},{5,4},{6,7},{7,6},{8,9},{9,8},{10,11... | collective-permute-start | bytes 393224 | tf_op jit(solution)/shard_map/ppermute | solution.py:46
  41.9 3.6 %collective-permute-start.16 = (bf16[256,256]{1,0:T(8,128)(2,1)S(1)}, bf16[256,256]{1,0:T(8,128)(2,1)S(1)}, u32[]{:S(2)}, u32[]{:S(2)}) collective-permute-start(bf16[256,256]{1,0:T(8,128)(2,1)S(1)} %collective-permute-done.15.refs_7_), channel_id=1, source_target_pairs={{0,1},{1,0},{2,3},{3,2},{4,5},{5,4},{6,7},{7,6},{8,9},{9,8},{10,11... | collective-permute-start | bytes 393224 | tf_op jit(solution)/shard_map/ppermute | solution.py:46
  42.5 10.6 %collective-permute-start.22 = (bf16[272,256]{1,0:T(8,128)(2,1)S(1)}, bf16[272,256]{1,0:T(8,128)(2,1)S(1)}, u32[]{:S(2)}, u32[]{:S(2)}) collective-permute-start(bf16[272,256]{1,0:T(8,128)(2,1)S(1)} %line_grads.2.refs_0_), channel_id=1, source_target_pairs={{0,16},{8,24},{16,0},{24,8},{1,17},{9,25},{17,1},{25,9},{2,18},{10... | collective-permute-start | bytes 417800 | tf_op jit(solution)/shard_map/ppermute | solution.py:46
  47.4 8.2 %collective-permute-start.17 = (bf16[256,256]{1,0:T(8,128)(2,1)S(1)}, bf16[256,256]{1,0:T(8,128)(2,1)S(1)}, u32[]{:S(2)}, u32[]{:S(2)}) collective-permute-start(bf16[256,256]{1,0:T(8,128)(2,1)S(1)} %get-tuple-element.45), channel_id=1, source_target_pairs={{0,8},{8,0},{16,24},{24,16},{1,9},{9,1},{17,25},{25,17},{2,10},{10... | collective-permute-start | bytes 393224 | tf_op jit(solution)/shard_map/ppermute | solution.py:46
  47.5 14.0 %collective-permute-start.18 = (bf16[256,256]{1,0:T(8,128)(2,1)S(1)}, bf16[256,256]{1,0:T(8,128)(2,1)S(1)}, u32[]{:S(2)}, u32[]{:S(2)}) collective-permute-start(bf16[256,256]{1,0:T(8,128)(2,1)S(1)} %get-tuple-element.46), channel_id=1, source_target_pairs={{0,16},{8,24},{16,0},{24,8},{1,17},{9,25},{17,1},{25,9},{2,18},{10... | collective-permute-start | bytes 393224 | tf_op jit(solution)/shard_map/ppermute | solution.py:46
  49.4 12.1 %collective-permute-start.19 = (bf16[256,256]{1,0:T(8,128)(2,1)S(1)}, bf16[256,256]{1,0:T(8,128)(2,1)S(1)}, u32[]{:S(2)}, u32[]{:S(2)}) collective-permute-start(bf16[256,256]{1,0:T(8,128)(2,1)S(1)} %get-tuple-element.47), channel_id=1, source_target_pairs={{0,24},{8,16},{16,8},{24,0},{1,25},{9,17},{17,9},{25,1},{2,26},{10... | collective-permute-start | bytes 393224 | tf_op jit(solution)/shard_map/ppermute | solution.py:46
  53.2 9.2 %collective-permute-start.23 = (bf16[272,256]{1,0:T(8,128)(2,1)S(1)}, bf16[272,256]{1,0:T(8,128)(2,1)S(1)}, u32[]{:S(2)}, u32[]{:S(2)}) collective-permute-start(bf16[272,256]{1,0:T(8,128)(2,1)S(1)} %line_grads.3.refs_0_), channel_id=1, source_target_pairs={{0,2},{1,3},{2,0},{3,1},{4,6},{5,7},{6,4},{7,5},{8,10},{9,11},{10,... | collective-permute-start | bytes 417800 | tf_op jit(solution)/shard_map/ppermute | solution.py:46
  53.9 8.4 %collective-permute-start.24 = (bf16[272,256]{1,0:T(8,128)(2,1)S(1)}, bf16[272,256]{1,0:T(8,128)(2,1)S(1)}, u32[]{:S(2)}, u32[]{:S(2)}) collective-permute-start(bf16[272,256]{1,0:T(8,128)(2,1)S(1)} %line_grads.3.refs_0_), channel_id=1, source_target_pairs={{0,4},{1,5},{2,6},{3,7},{4,0},{5,1},{6,2},{7,3},{8,12},{9,13},{10,... | collective-permute-start | bytes 417800 | tf_op jit(solution)/shard_map/ppermute | solution.py:46
  55.6 6.7 %collective-permute-start.25 = (bf16[272,256]{1,0:T(8,128)(2,1)S(1)}, bf16[272,256]{1,0:T(8,128)(2,1)S(1)}, u32[]{:S(2)}, u32[]{:S(2)}) collective-permute-start(bf16[272,256]{1,0:T(8,128)(2,1)S(1)} %line_grads.3.refs_0_), channel_id=1, source_target_pairs={{0,6},{1,7},{2,4},{3,5},{4,2},{5,3},{6,0},{7,1},{8,14},{9,15},{10,... | collective-permute-start | bytes 417800 | tf_op jit(solution)/shard_map/ppermute | solution.py:46
  62.3 1.6 %collective-permute-start.27 = (bf16[576,256]{1,0:T(8,128)(2,1)S(1)}, bf16[576,256]{1,0:T(8,128)(2,1)S(1)}, u32[]{:S(2)}, u32[]{:S(2)}) collective-permute-start(bf16[576,256]{1,0:T(8,128)(2,1)S(1)} %get-tuple-element.53), channel_id=1, source_target_pairs={{0,1},{1,0},{2,3},{3,2},{4,5},{5,4},{6,7},{7,6},{8,9},{9,8},{10,11... | collective-permute-start | bytes 884744 | tf_op jit(solution)/shard_map/ppermute | solution.py:46
  62.4 1.9 %collective-permute-start.26 = (f32[256,256]{1,0:T(8,128)S(1)}, f32[256,256]{1,0:T(8,128)S(1)}, u32[]{:S(2)}, u32[]{:S(2)}) collective-permute-start(f32[256,256]{1,0:T(8,128)S(1)} %get-tuple-element.51.mine_ref), channel_id=1, source_target_pairs={{0,1},{1,0},{2,3},{3,2},{4,5},{5,4},{6,7},{7,6},{8,9},{9,8},{10,11... | collective-permute-start | bytes 786440 | tf_op jit(solution)/shard_map/ppermute | solution.py:46

commit v4 on v3

--- a/solution.py
+++ b/solution.py
@@ -12,6 +12,7 @@
 F32 = jnp.float32
 BIAS_ROWS = 16
 SPACER_ROWS = 576
+FAR_ROWS = 32
 VMEM_LIMIT = 40 * 1024 * 1024
 CONTRACT_FIRST = (((0,), (0,)), ((), ()))
 CONTRACT_SECOND = (((1,), (1,)), ((), ()))
@@ -313,11 +314,29 @@
     )(ids, mine, other, line, after)
 
 
+def extend_kernel(in_ref, out_ref):
+    rows = in_ref.shape[0]
+    out_ref[0:rows, :] = in_ref[...]
+    out_ref[rows:, :] = jnp.zeros((out_ref.shape[0] - rows, out_ref.shape[1]), out_ref.dtype)
+
+
+def extend(value):
+    rows, width = value.shape
+    return pl.pallas_call(
+        extend_kernel,
+        in_specs=whole(1),
+        out_specs=pl.BlockSpec(memory_space=pltpu.VMEM),
+        out_shape=jax.ShapeDtypeStruct((rows + FAR_ROWS, width), value.dtype),
+        compiler_params=params(),
+        name="extend",
+    )(value)
+
+
 def back_kernel(n, ids_ref, flip_ref, *refs):
     own_ref, out_refs, held, total = refs[n], refs[n + 1 : -2], refs[-2], refs[-1]
     share = own_ref.shape[0]
     for q, ref in enumerate(refs[:n]):
-        held[q * share : (q + 1) * share, :] = ref[...]
+        held[q * share : (q + 1) * share, :] = ref[0:share, :]
     total[...] = dot(flip_ref[...], held[...])
     own_ref[...] = total[pl.ds(pl.multiple_of(ids_ref[1] * share, share), share), :]
     for k, ref in enumerate(out_refs):
@@ -411,14 +430,14 @@
 
     even = [xor_permute(message, "rep", 2 * q) for q in reversed(range(1, chips))]
     even = [message] + even[::-1]
-    odd = [xor_permute(value, "rep", 1) for value in even]
+    odd = [xor_permute(value, "rep", 1) for value in even[:last] + [extend(even[last])]]
     spread = back_sums(ids, flip, odd + even, panels)
 
     line = pair_grads(grad_keep, xor_permute(grad_away, "rep", 1))
-    k = 1
-    while k < row_devices:
+    k = row_devices // 2
+    while k:
         line = line_grads([line, xor_permute(line, "row", k)])
-        k *= 2
+        k //= 2
     arrived = [xor_permute(spread[k], "row", k) for k in range(1, row_devices)]
     grad_features, spacer = feature_grads(dpre, self_weight, spread[0], arrived)
     late = xor_permute(spacer, "rep", 1)

time: 66.1 us -> 65.3 us (0.988)
  waiting for transfers between devices: 20.4 us -> 19.3 us
    ppermute x28, waiting for transfers between devices: 20.4 us -> 19.3 us  [xor_permute(): lax.ppermute(value, axis, [(i, i ^ k) for i in range(lax.axis_size(axis))])]
  transfers between devices with their start and end apart: 28 -> 28, of which waited for: 11 -> 13; matrix products, arithmetic and copies ran while one was open for 0% -> 0% of each run, Pallas kernels for 11% -> 11%
where the time goes in v4:
time: 65.3 us; the launch traced here: 65 us
  starting transfers between devices  28.6 us (44%)
  waiting for transfers between devices  19.3 us (30%)
  Pallas kernels  11.3 us (17%)
  local copies, waits for them, and re-layouts  4.9 us (8%)
  between operations  0.87 us (1%)
    ppermute x28, starting transfers between devices, xor_permute(): lax.ppermute(value, axis, [(i, i ^ k) for i in range(lax.axis_size(axis))])  28.6 us
    ppermute x28, waiting for transfers between devices, xor_permute(): lax.ppermute(value, axis, [(i, i ^ k) for i in range(lax.axis_size(axis))])  19.3 us
    unnamed x18, local copies, waits for them, and re-layouts  4.8 us
    pallas_call x1, Pallas kernels, build_strip(): pl.pallas_call(functools.partial(strip_kernel, panels, blocks, tile, chip...  2.92 us
    pallas_call x1, Pallas kernels, back_sums(): pl.pallas_call(functools.partial(back_kernel, n), in_specs=[pl.BlockSpec(...  1.86 us
    pallas_call x1, Pallas kernels, rows_step(): pl.pallas_call(functools.partial(rows_kernel, m, scale), in_specs=[pl.Blo...  1.66 us
    pallas_call x1, Pallas kernels, place_grads(): pl.pallas_call(place_grads_kernel, in_specs=[pl.BlockSpec(memory_space=pl...  1.38 us
  transfers between devices with their start and end apart: 28, of which 13 were waited for; matrix products, arithmetic and copies ran while one was open for 0% of the time, Pallas kernels for 11%

profile of v4, /device:TPU:0, one launch (start us, length us, event | category | flops | bytes accessed | tf_op | source)
XLA Modules:
  0.0 65.0 jit_solution(5773196770329309591)
XLA Ops:
  0.6 0.0 copy-start
  0.7 1.2 %copy-done = bf16[2048,256]{1,0:T(8,128)(2,1)S(1)} copy-done((bf16[2048,256]{1,0:T(8,128)(2,1)S(1)}, bf16[2048,256]{1,0:T(8,128)(2,1)}, u32[]{:S(2)}) %copy-start) | copy-done | bytes 1048600
  1.9 3.1 %collective-permute-start = (bf16[256,256]{1,0:T(8,128)(2,1)S(1)}, bf16[256,256]{1,0:T(8,128)(2,1)S(1)}, u32[]{:S(2)}, u32[]{:S(2)}) collective-permute-start(bf16[256,256]{1,0:T(8,128)(2,1)S(1)} %constant_dynamic-slice_fusion.refs_0_.own_ref), channel_id=1, source_target_pairs={{0,8},{8,0},{16,24},{24,16},{1,9},{9,1},{17,25},{25,17},{2,10},{10... | collective-permute-start | bytes 393224 | tf_op jit(solution)/shard_map/ppermute | solution.py:47
  5.0 2.6 %collective-permute-start.1 = (bf16[256,256]{1,0:T(8,128)(2,1)S(1)}, bf16[256,256]{1,0:T(8,128)(2,1)S(1)}, u32[]{:S(2)}, u32[]{:S(2)}) collective-permute-start(bf16[256,256]{1,0:T(8,128)(2,1)S(1)} %constant_dynamic-slice_fusion.refs_0_.own_ref), channel_id=1, source_target_pairs={{0,16},{8,24},{16,0},{24,8},{1,17},{9,25},{17,1},{25,9},{2,18},{10... | collective-permute-start | bytes 393224 | tf_op jit(solution)/shard_map/ppermute | solution.py:47
  7.6 0.0 collective-permute-start.2
  7.6 0.1 pad_add_fusion.ids_ref
  7.6 2.2 %copy-done.1 = s32[2048,4,128]{2,1,0:T(4,128)S(1)} copy-done((s32[2048,4,128]{2,1,0:T(4,128)S(1)}, s32[2048,4,128]{2,1,0:T(4,128)}, u32[]{:S(2)}) %copy-start.1) | copy-done | bytes 4194328
  9.8 0.7 %copy-done.5 = s32[16,4]{0,1:T(4,128)S(1)} copy-done((s32[16,4]{0,1:T(4,128)S(1)}, s32[16,4]{0,1:T(4,128)}, u32[]{:S(2)}) %copy-start.5) | copy-done | bytes 280
  10.5 0.7 %copy-done.6 = s32[16,4]{0,1:T(4,128)S(1)} copy-done((s32[16,4]{0,1:T(4,128)S(1)}, s32[16,4]{0,1:T(4,128)}, u32[]{:S(2)}) %copy-start.6) | copy-done | bytes 280
  11.2 2.9 %build_strip.1 = (bf16[2048,1024]{1,0:T(8,128)(2,1)S(1)}, bf16[1024,2048]{1,0:T(8,128)(2,1)S(1)}) custom-call(s32[2]{0:T(128)S(1)} %pad_add_fusion.ids_ref, s32[4,16]{1,0:T(4,128)S(1)} %bitcast.8, s32[4,16]{1,0:T(4,128)S(1)} %bitcast.9, s32[8192,128]{1,0:T(8,128)S(1)} %bitcast.7), custom_call_target="tpu_custom_call" | custom-call | tf_op jit(solution)/shard_map/build_strip/pallas_call | solution.py:74
  14.1 0.0 collective-permute-done.refs_1_
  14.1 3.8 %collective-permute-done.1.refs_2_ = bf16[256,256]{1,0:T(8,128)(2,1)S(1)} collective-permute-done((bf16[256,256]{1,0:T(8,128)(2,1)S(1)}, bf16[256,256]{1,0:T(8,128)(2,1)S(1)}, u32[]{:S(2)}, u32[]{:S(2)}) %collective-permute-start.1) | collective-permute-done | bytes 131104 | tf_op jit(solution)/shard_map/ppermute | solution.py:47
  17.9 0.9 %away_far.1 = (bf16[256,256]{1,0:T(8,128)(2,1)S(1)}, bf16[1024,256]{1,0:T(8,128)(2,1)S(1)}) custom-call(s32[2]{0:T(128)S(1)} %pad_add_fusion.ids_ref, bf16[2048,1024]{1,0:T(8,128)(2,1)S(1)} %get-tuple-element.31.dense_ref, bf16[256,256]{1,0:T(8,128)(2,1)S(1)} %constant_dynamic-slice_fusion.refs_0_.own_ref, ...), custom_call_target="tpu_custom_call" | custom-call | tf_op jit(solution)/shard_map/away_far/pallas_call | solution.py:115
  18.8 0.1 collective-permute-start.6
  18.9 0.6 away_near.1
  19.4 0.6 collective-permute-start.3
  20.0 0.1 collective-permute-start.4
  20.1 0.4 collective-permute-start.5
  20.5 0.3 chip_far.1
  20.8 0.0 copy-start.2
  20.9 0.0 copy-start.3
  20.9 0.0 copy-start.4
  20.9 0.0 copy-start.7
  20.9 2.5 %collective-permute-start.7 = (bf16[256,256]{1,0:T(8,128)(2,1)S(1)}, bf16[256,256]{1,0:T(8,128)(2,1)S(1)}, u32[]{:S(2)}, u32[]{:S(2)}) collective-permute-start(bf16[256,256]{1,0:T(8,128)(2,1)S(1)} %chip_far.1), channel_id=1, source_target_pairs={{0,6},{1,7},{2,4},{3,5},{4,2},{5,3},{6,0},{7,1},{8,14},{9,15},{10,... | collective-permute-start | bytes 393224 | tf_op jit(solution)/shard_map/ppermute | solution.py:47
  23.4 0.0 collective-permute-done.3.refs_0_
  23.4 0.0 collective-permute-done.4.refs_1_
  23.4 0.0 collective-permute-done.5.refs_2_
  23.4 0.6 chip_near.1
  24.0 0.6 collective-permute-start.8
  24.6 0.6 collective-permute-start.9
  25.2 2.2 %collective-permute-done.7.far_ref = bf16[256,256]{1,0:T(8,128)(2,1)S(1)} collective-permute-done((bf16[256,256]{1,0:T(8,128)(2,1)S(1)}, bf16[256,256]{1,0:T(8,128)(2,1)S(1)}, u32[]{:S(2)}, u32[]{:S(2)}) %collective-permute-start.7) | collective-permute-done | bytes 131104 | tf_op jit(solution)/shard_map/ppermute | solution.py:47
  27.5 2.7 %collective-permute-done.8.refs_0_ = bf16[256,256]{1,0:T(8,128)(2,1)S(1)} collective-permute-done((bf16[256,256]{1,0:T(8,128)(2,1)S(1)}, bf16[256,256]{1,0:T(8,128)(2,1)S(1)}, u32[]{:S(2)}, u32[]{:S(2)}) %collective-permute-start.8) | collective-permute-done | bytes 131104 | tf_op jit(solution)/shard_map/ppermute | solution.py:47
  30.1 0.1 collective-permute-done.9.refs_1_
  30.2 0.1 broadcast_in_dim.10.deg_ref
  30.3 1.7 %rows_step.1 = (bf16[256,256]{1,0:T(8,128)(2,1)}, bf16[256,256]{1,0:T(8,128)(2,1)S(1)}, bf16[256,256]{1,0:T(8,128)(2,1)S(1)}, f32[272,256]{1,0:T(8,128)S(1)}, f32[272,256]{1,0:T(8,128)S(1)}) custom-call(s32[2]{0:T(128)S(1)} %pad_add_fusion.ids_ref, bf16[256,256]{1,0:T(8,128)(2,1)S(1)} %constant_dynamic-slice_fusion.refs_0_.own_ref, ...), custom_call_target="tpu_custom_call" | custom-call | tf_op jit(solution)/shard_map/rows_step/pallas_call | solution.py:214
  32.0 2.4 %collective-permute-start.15 = (bf16[256,256]{1,0:T(8,128)(2,1)S(1)}, bf16[256,256]{1,0:T(8,128)(2,1)S(1)}, u32[]{:S(2)}, u32[]{:S(2)}) collective-permute-start(bf16[256,256]{1,0:T(8,128)(2,1)S(1)} %get-tuple-element.43.refs_4_), channel_id=1, source_target_pairs={{0,6},{1,7},{2,4},{3,5},{4,2},{5,3},{6,0},{7,1},{8,14},{9,15},{10,... | collective-permute-start | bytes 393224 | tf_op jit(solution)/shard_map/ppermute | solution.py:47
  34.5 0.5 collective-permute-start.11
  35.0 0.5 collective-permute-start.13
  35.5 0.1 pair_grads.1.refs_0_
  35.6 3.0 %collective-permute-start.21 = (bf16[272,256]{1,0:T(8,128)(2,1)S(1)}, bf16[272,256]{1,0:T(8,128)(2,1)S(1)}, u32[]{:S(2)}, u32[]{:S(2)}) collective-permute-start(bf16[272,256]{1,0:T(8,128)(2,1)S(1)} %pair_grads.1.refs_0_), channel_id=1, source_target_pairs={{0,16},{8,24},{16,0},{24,8},{1,17},{9,25},{17,1},{25,9},{2,18},{10... | collective-permute-start | bytes 417800 | tf_op jit(solution)/shard_map/ppermute | solution.py:47
  38.6 0.6 collective-permute-done.15.in_ref.refs_7_
  39.2 0.1 collective-permute-start.16
  39.3 0.5 collective-permute-start.10
  39.8 1.9 %collective-permute-done.11.refs_5_ = bf16[256,256]{1,0:T(8,128)(2,1)S(1)} collective-permute-done((bf16[256,256]{1,0:T(8,128)(2,1)S(1)}, bf16[256,256]{1,0:T(8,128)(2,1)S(1)}, u32[]{:S(2)}, u32[]{:S(2)}) %collective-permute-start.11) | collective-permute-done | bytes 131104 | tf_op jit(solution)/shard_map/ppermute | solution.py:47
  41.7 0.5 collective-permute-start.14
  42.2 2.9 %collective-permute-done.21.refs_1_ = bf16[272,256]{1,0:T(8,128)(2,1)S(1)} collective-permute-done((bf16[272,256]{1,0:T(8,128)(2,1)S(1)}, bf16[272,256]{1,0:T(8,128)(2,1)S(1)}, u32[]{:S(2)}, u32[]{:S(2)}) %collective-permute-start.21) | collective-permute-done | bytes 139296 | tf_op jit(solution)/shard_map/ppermute | solution.py:47
  45.1 0.1 collective-permute-start.22
  45.2 1.9 %back_sums.1 = (f32[256,256]{1,0:T(8,128)S(1)}, bf16[256,256]{1,0:T(8,128)(2,1)S(1)}, bf16[256,256]{1,0:T(8,128)(2,1)S(1)}, bf16[256,256]{1,0:T(8,128)(2,1)S(1)}) custom-call(s32[2]{0:T(128)S(1)} %pad_add_fusion.ids_ref, bf16[1024,2048]{1,0:T(8,128)(2,1)S(1)} %get-tuple-element.42.flip_ref, bf16[256,256]{1,0:T(8,128)(2,1)S(1)} %collective-permute-done.10.refs_0_, ...), custom_call_target="tpu_custom_call" | custom-call | tf_op jit(solution)/shard_map/back_sums/pallas_call | solution.py:351
  47.1 2.1 %collective-permute-start.17 = (bf16[256,256]{1,0:T(8,128)(2,1)S(1)}, bf16[256,256]{1,0:T(8,128)(2,1)S(1)}, u32[]{:S(2)}, u32[]{:S(2)}) collective-permute-start(bf16[256,256]{1,0:T(8,128)(2,1)S(1)} %get-tuple-element.45), channel_id=1, source_target_pairs={{0,8},{8,0},{16,24},{24,16},{1,9},{9,1},{17,25},{25,17},{2,10},{10... | collective-permute-start | bytes 393224 | tf_op jit(solution)/shard_map/ppermute | solution.py:47
  49.2 0.6 collective-permute-start.18
  49.7 1.9 %collective-permute-start.19 = (bf16[256,256]{1,0:T(8,128)(2,1)S(1)}, bf16[256,256]{1,0:T(8,128)(2,1)S(1)}, u32[]{:S(2)}, u32[]{:S(2)}) collective-permute-start(bf16[256,256]{1,0:T(8,128)(2,1)S(1)} %get-tuple-element.47), channel_id=1, source_target_pairs={{0,24},{8,16},{16,8},{24,0},{1,25},{9,17},{17,9},{25,1},{2,26},{10... | collective-permute-start | bytes 393224 | tf_op jit(solution)/shard_map/ppermute | solution.py:47
  51.6 0.8 %collective-permute-done.22.refs_1_ = bf16[272,256]{1,0:T(8,128)(2,1)S(1)} collective-permute-done((bf16[272,256]{1,0:T(8,128)(2,1)S(1)}, bf16[272,256]{1,0:T(8,128)(2,1)S(1)}, u32[]{:S(2)}, u32[]{:S(2)}) %collective-permute-start.22) | collective-permute-done | bytes 139296 | tf_op jit(solution)/shard_map/ppermute | solution.py:47
  52.4 1.6 %collective-permute-start.23 = (bf16[272,256]{1,0:T(8,128)(2,1)S(1)}, bf16[272,256]{1,0:T(8,128)(2,1)S(1)}, u32[]{:S(2)}, u32[]{:S(2)}) collective-permute-start(bf16[272,256]{1,0:T(8,128)(2,1)S(1)} %line_grads.3.refs_0_), channel_id=1, source_target_pairs={{0,2},{1,3},{2,0},{3,1},{4,6},{5,7},{6,4},{7,5},{8,10},{9,11},{10,... | collective-permute-start | bytes 417800 | tf_op jit(solution)/shard_map/ppermute | solution.py:47
  54.0 1.3 %collective-permute-start.24 = (bf16[272,256]{1,0:T(8,128)(2,1)S(1)}, bf16[272,256]{1,0:T(8,128)(2,1)S(1)}, u32[]{:S(2)}, u32[]{:S(2)}) collective-permute-start(bf16[272,256]{1,0:T(8,128)(2,1)S(1)} %line_grads.3.refs_0_), channel_id=1, source_target_pairs={{0,4},{1,5},{2,6},{3,7},{4,0},{5,1},{6,2},{7,3},{8,12},{9,13},{10,... | collective-permute-start | bytes 417800 | tf_op jit(solution)/shard_map/ppermute | solution.py:47
  55.3 0.7 %collective-permute-done.17.refs_0_ = bf16[256,256]{1,0:T(8,128)(2,1)S(1)} collective-permute-done((bf16[256,256]{1,0:T(8,128)(2,1)S(1)}, bf16[256,256]{1,0:T(8,128)(2,1)S(1)}, u32[]{:S(2)}, u32[]{:S(2)}) %collective-permute-start.17) | collective-permute-done | bytes 131104 | tf_op jit(solution)/shard_map/ppermute | solution.py:47
  56.0 2.7 %collective-permute-start.25 = (bf16[272,256]{1,0:T(8,128)(2,1)S(1)}, bf16[272,256]{1,0:T(8,128)(2,1)S(1)}, u32[]{:S(2)}, u32[]{:S(2)}) collective-permute-start(bf16[272,256]{1,0:T(8,128)(2,1)S(1)} %line_grads.3.refs_0_), channel_id=1, source_target_pairs={{0,6},{1,7},{2,4},{3,5},{4,2},{5,3},{6,0},{7,1},{8,14},{9,15},{10,... | collective-permute-start | bytes 417800 | tf_op jit(solution)/shard_map/ppermute | solution.py:47
  58.7 2.1 %collective-permute-done.18.refs_1_ = bf16[256,256]{1,0:T(8,128)(2,1)S(1)} collective-permute-done((bf16[256,256]{1,0:T(8,128)(2,1)S(1)}, bf16[256,256]{1,0:T(8,128)(2,1)S(1)}, u32[]{:S(2)}, u32[]{:S(2)}) %collective-permute-start.18) | collective-permute-done | bytes 131104 | tf_op jit(solution)/shard_map/ppermute | solution.py:47
  60.8 0.9 %feature_grads.1 = (bf16[256,256]{1,0:T(8,128)(2,1)}, bf16[576,256]{1,0:T(8,128)(2,1)S(1)}) custom-call(bf16[256,256]{1,0:T(8,128)(2,1)S(1)} %get-tuple-element.41.dpre_ref, bf16[256,256]{1,0:T(8,128)(2,1)S(1)} %copy-done.2, f32[256,256]{1,0:T(8,128)S(1)} %get-tuple-element.44.own_ref, bf16[256,256]{1,0:T(8,128)(2,1)S(1)} %collective-permute-done.17.refs_0_, ...), custom_call_target="tpu_custom_call" | custom-call | tf_op jit(solution)/shard_map/feature_grads/pallas_call | solution.py:375
  61.7 0.2 collective-permute-done.25.refs_3_
  61.9 0.1 all_grads.1
  62.0 0.3 collective-permute-start.26
  62.4 0.9 %collective-permute-done.27.after_ref = bf16[576,256]{1,0:T(8,128)(2,1)S(1)} collective-permute-done((bf16[576,256]{1,0:T(8,128)(2,1)S(1)}, bf16[576,256]{1,0:T(8,128)(2,1)S(1)}, u32[]{:S(2)}, u32[]{:S(2)}) %collective-permute-start.27) | collective-permute-done | bytes 294944 | tf_op jit(solution)/shard_map/ppermute | solution.py:47
  63.3 0.4 collective-permute-done.26.other_ref
  63.6 1.4 %place_grads.1 = (f32[256,256]{1,0:T(8,128)}, f32[256,256]{1,0:T(8,128)}, f32[1,256]{1,0:T(1,128)}) custom-call(s32[2]{0:T(128)S(1)} %pad_add_fusion.ids_ref, f32[256,256]{1,0:T(8,128)S(1)} %get-tuple-element.51.mine_ref, f32[256,256]{1,0:T(8,128)S(1)} %collective-permute-done.26.other_ref, f32[1,256]{1,0:T(1,128)S(1)} %get-tuple-element.52.line_ref, ...), custom_call_target="tpu_custom_call" | custom-call | tf_op jit(solution)/shard_map/place_grads/pallas_call | solution.py:305
  (29 shorter events, 0.2 us)
Async XLA Ops:
  0.6 1.2 %copy-start = (bf16[2048,256]{1,0:T(8,128)(2,1)S(1)}, bf16[2048,256]{1,0:T(8,128)(2,1)}, u32[]{:S(2)}) copy-start(bf16[2048,256]{1,0:T(8,128)(2,1)} %param.9) | copy-start | bytes 3145732
  1.9 12.2 %collective-permute-start = (bf16[256,256]{1,0:T(8,128)(2,1)S(1)}, bf16[256,256]{1,0:T(8,128)(2,1)S(1)}, u32[]{:S(2)}, u32[]{:S(2)}) collective-permute-start(bf16[256,256]{1,0:T(8,128)(2,1)S(1)} %constant_dynamic-slice_fusion.refs_0_.own_ref), channel_id=1, source_target_pairs={{0,8},{8,0},{16,24},{24,16},{1,9},{9,1},{17,25},{25,17},{2,10},{10... | collective-permute-start | bytes 393224 | tf_op jit(solution)/shard_map/ppermute | solution.py:47
  5.0 12.9 %collective-permute-start.1 = (bf16[256,256]{1,0:T(8,128)(2,1)S(1)}, bf16[256,256]{1,0:T(8,128)(2,1)S(1)}, u32[]{:S(2)}, u32[]{:S(2)}) collective-permute-start(bf16[256,256]{1,0:T(8,128)(2,1)S(1)} %constant_dynamic-slice_fusion.refs_0_.own_ref), channel_id=1, source_target_pairs={{0,16},{8,24},{16,0},{24,8},{1,17},{9,25},{17,1},{25,9},{2,18},{10... | collective-permute-start | bytes 393224 | tf_op jit(solution)/shard_map/ppermute | solution.py:47
  7.6 10.3 %collective-permute-start.2 = (bf16[256,256]{1,0:T(8,128)(2,1)S(1)}, bf16[256,256]{1,0:T(8,128)(2,1)S(1)}, u32[]{:S(2)}, u32[]{:S(2)}) collective-permute-start(bf16[256,256]{1,0:T(8,128)(2,1)S(1)} %constant_dynamic-slice_fusion.refs_0_.own_ref), channel_id=1, source_target_pairs={{0,24},{8,16},{16,8},{24,0},{1,25},{9,17},{17,9},{25,1},{2,26},{10... | collective-permute-start | bytes 393224 | tf_op jit(solution)/shard_map/ppermute | solution.py:47
  7.6 2.2 %copy-start.1 = (s32[2048,4,128]{2,1,0:T(4,128)S(1)}, s32[2048,4,128]{2,1,0:T(4,128)}, u32[]{:S(2)}) copy-start(s32[2048,4,128]{2,1,0:T(4,128)} %param.13) | copy-start | bytes 12582916
  9.8 0.7 %copy-start.5 = (s32[16,4]{0,1:T(4,128)S(1)}, s32[16,4]{0,1:T(4,128)}, u32[]{:S(2)}) copy-start(s32[16,4]{0,1:T(4,128)} %param.14) | copy-start | bytes 772
  10.5 0.7 %copy-start.6 = (s32[16,4]{0,1:T(4,128)S(1)}, s32[16,4]{0,1:T(4,128)}, u32[]{:S(2)}) copy-start(s32[16,4]{0,1:T(4,128)} %param.15) | copy-start | bytes 772
  18.8 1.7 %collective-permute-start.6 = (bf16[256,256]{1,0:T(8,128)(2,1)S(1)}, bf16[256,256]{1,0:T(8,128)(2,1)S(1)}, u32[]{:S(2)}, u32[]{:S(2)}) collective-permute-start(bf16[256,256]{1,0:T(8,128)(2,1)S(1)} %get-tuple-element.37), channel_id=1, source_target_pairs={{0,1},{1,0},{2,3},{3,2},{4,5},{5,4},{6,7},{7,6},{8,9},{9,8},{10,11... | collective-permute-start | bytes 393224 | tf_op jit(solution)/shard_map/ppermute | solution.py:47
  19.4 4.0 %collective-permute-start.3 = (bf16[256,256]{1,0:T(8,128)(2,1)S(1)}, bf16[256,256]{1,0:T(8,128)(2,1)S(1)}, u32[]{:S(2)}, u32[]{:S(2)}) collective-permute-start(bf16[256,256]{1,0:T(8,128)(2,1)S(1)} %get-tuple-element.33), channel_id=1, source_target_pairs={{0,1},{1,0},{2,3},{3,2},{4,5},{5,4},{6,7},{7,6},{8,9},{9,8},{10,11... | collective-permute-start | bytes 393224 | tf_op jit(solution)/shard_map/ppermute | solution.py:47
  20.0 3.4 %collective-permute-start.4 = (bf16[256,256]{1,0:T(8,128)(2,1)S(1)}, bf16[256,256]{1,0:T(8,128)(2,1)S(1)}, u32[]{:S(2)}, u32[]{:S(2)}) collective-permute-start(bf16[256,256]{1,0:T(8,128)(2,1)S(1)} %get-tuple-element.34), channel_id=1, source_target_pairs={{0,1},{1,0},{2,3},{3,2},{4,5},{5,4},{6,7},{7,6},{8,9},{9,8},{10,11... | collective-permute-start | bytes 393224 | tf_op jit(solution)/shard_map/ppermute | solution.py:47
  20.1 5.1 %copy-start.8 = (s32[256]{0:T(256)S(1)}, s32[256]{0:T(256)}, u32[]{:S(2)}) copy-start(s32[256]{0:T(256)} %param.16) | copy-start | bytes 3076
  20.1 3.3 %collective-permute-start.5 = (bf16[256,256]{1,0:T(8,128)(2,1)S(1)}, bf16[256,256]{1,0:T(8,128)(2,1)S(1)}, u32[]{:S(2)}, u32[]{:S(2)}) collective-permute-start(bf16[256,256]{1,0:T(8,128)(2,1)S(1)} %get-tuple-element.35), channel_id=1, source_target_pairs={{0,1},{1,0},{2,3},{3,2},{4,5},{5,4},{6,7},{7,6},{8,9},{9,8},{10,11... | collective-permute-start | bytes 393224 | tf_op jit(solution)/shard_map/ppermute | solution.py:47
  20.8 9.5 %copy-start.2 = (bf16[256,256]{1,0:T(8,128)(2,1)S(1)}, bf16[256,256]{1,0:T(8,128)(2,1)}, u32[]{:S(2)}) copy-start(bf16[256,256]{1,0:T(8,128)(2,1)} %ws_ref.3) | copy-start | bytes 393220
  20.9 9.5 %copy-start.3 = (bf16[256,256]{1,0:T(8,128)(2,1)S(1)}, bf16[256,256]{1,0:T(8,128)(2,1)}, u32[]{:S(2)}) copy-start(bf16[256,256]{1,0:T(8,128)(2,1)} %wn_ref.1) | copy-start | bytes 393220
  20.9 9.5 %copy-start.4 = (bf16[256,256]{1,0:T(8,128)(2,1)S(1)}, bf16[256,256]{1,0:T(8,128)(2,1)}, u32[]{:S(2)}) copy-start(bf16[256,256]{1,0:T(8,128)(2,1)} %cot_ref.1) | copy-start | bytes 393220
  20.9 9.5 %copy-start.7 = (f32[256]{0:T(256)S(1)}, f32[256]{0:T(256)}, u32[]{:S(2)}) copy-start(f32[256]{0:T(256)} %param.12) | copy-start | bytes 3076
  20.9 6.5 %collective-permute-start.7 = (bf16[256,256]{1,0:T(8,128)(2,1)S(1)}, bf16[256,256]{1,0:T(8,128)(2,1)S(1)}, u32[]{:S(2)}, u32[]{:S(2)}) collective-permute-start(bf16[256,256]{1,0:T(8,128)(2,1)S(1)} %chip_far.1), channel_id=1, source_target_pairs={{0,6},{1,7},{2,4},{3,5},{4,2},{5,3},{6,0},{7,1},{8,14},{9,15},{10,... | collective-permute-start | bytes 393224 | tf_op jit(solution)/shard_map/ppermute | solution.py:47
  24.0 6.1 %collective-permute-start.8 = (bf16[256,256]{1,0:T(8,128)(2,1)S(1)}, bf16[256,256]{1,0:T(8,128)(2,1)S(1)}, u32[]{:S(2)}, u32[]{:S(2)}) collective-permute-start(bf16[256,256]{1,0:T(8,128)(2,1)S(1)} %get-tuple-element.38), channel_id=1, source_target_pairs={{0,4},{1,5},{2,6},{3,7},{4,0},{5,1},{6,2},{7,3},{8,12},{9,13},{10,... | collective-permute-start | bytes 393224 | tf_op jit(solution)/shard_map/ppermute | solution.py:47
  24.6 5.6 %collective-permute-start.9 = (bf16[256,256]{1,0:T(8,128)(2,1)S(1)}, bf16[256,256]{1,0:T(8,128)(2,1)S(1)}, u32[]{:S(2)}, u32[]{:S(2)}) collective-permute-start(bf16[256,256]{1,0:T(8,128)(2,1)S(1)} %get-tuple-element.39), channel_id=1, source_target_pairs={{0,2},{1,3},{2,0},{3,1},{4,6},{5,7},{6,4},{7,5},{8,10},{9,11},{10,... | collective-permute-start | bytes 393224 | tf_op jit(solution)/shard_map/ppermute | solution.py:47
  32.0 3.5 %collective-permute-start.20 = (f32[272,256]{1,0:T(8,128)S(1)}, f32[272,256]{1,0:T(8,128)S(1)}, u32[]{:S(2)}, u32[]{:S(2)}) collective-permute-start(f32[272,256]{1,0:T(8,128)S(1)} %get-tuple-element.50), channel_id=1, source_target_pairs={{0,1},{1,0},{2,3},{3,2},{4,5},{5,4},{6,7},{7,6},{8,9},{9,8},{10,11... | collective-permute-start | bytes 835592 | tf_op jit(solution)/shard_map/ppermute | solution.py:47
  32.0 7.2 %collective-permute-start.15 = (bf16[256,256]{1,0:T(8,128)(2,1)S(1)}, bf16[256,256]{1,0:T(8,128)(2,1)S(1)}, u32[]{:S(2)}, u32[]{:S(2)}) collective-permute-start(bf16[256,256]{1,0:T(8,128)(2,1)S(1)} %get-tuple-element.43.refs_4_), channel_id=1, source_target_pairs={{0,6},{1,7},{2,4},{3,5},{4,2},{5,3},{6,0},{7,1},{8,14},{9,15},{10,... | collective-permute-start | bytes 393224 | tf_op jit(solution)/shard_map/ppermute | solution.py:47
  34.5 7.2 %collective-permute-start.11 = (bf16[256,256]{1,0:T(8,128)(2,1)S(1)}, bf16[256,256]{1,0:T(8,128)(2,1)S(1)}, u32[]{:S(2)}, u32[]{:S(2)}) collective-permute-start(bf16[256,256]{1,0:T(8,128)(2,1)S(1)} %get-tuple-element.43.refs_4_), channel_id=1, source_target_pairs={{0,2},{1,3},{2,0},{3,1},{4,6},{5,7},{6,4},{7,5},{8,10},{9,11},{10,... | collective-permute-start | bytes 393224 | tf_op jit(solution)/shard_map/ppermute | solution.py:47
  35.0 6.7 %collective-permute-start.13 = (bf16[256,256]{1,0:T(8,128)(2,1)S(1)}, bf16[256,256]{1,0:T(8,128)(2,1)S(1)}, u32[]{:S(2)}, u32[]{:S(2)}) collective-permute-start(bf16[256,256]{1,0:T(8,128)(2,1)S(1)} %get-tuple-element.43.refs_4_), channel_id=1, source_target_pairs={{0,4},{1,5},{2,6},{3,7},{4,0},{5,1},{6,2},{7,3},{8,12},{9,13},{10,... | collective-permute-start | bytes 393224 | tf_op jit(solution)/shard_map/ppermute | solution.py:47
  35.6 9.5 %collective-permute-start.21 = (bf16[272,256]{1,0:T(8,128)(2,1)S(1)}, bf16[272,256]{1,0:T(8,128)(2,1)S(1)}, u32[]{:S(2)}, u32[]{:S(2)}) collective-permute-start(bf16[272,256]{1,0:T(8,128)(2,1)S(1)} %pair_grads.1.refs_0_), channel_id=1, source_target_pairs={{0,16},{8,24},{16,0},{24,8},{1,17},{9,25},{17,1},{25,9},{2,18},{10... | collective-permute-start | bytes 417800 | tf_op jit(solution)/shard_map/ppermute | solution.py:47
  39.2 6.0 %collective-permute-start.16 = (bf16[288,256]{1,0:T(8,128)(2,1)S(1)}, bf16[288,256]{1,0:T(8,128)(2,1)S(1)}, u32[]{:S(2)}, u32[]{:S(2)}) collective-permute-start(bf16[288,256]{1,0:T(8,128)(2,1)S(1)} %extend.1), channel_id=1, source_target_pairs={{0,1},{1,0},{2,3},{3,2},{4,5},{5,4},{6,7},{7,6},{8,9},{9,8},{10,11... | collective-permute-start | bytes 442376 | tf_op jit(solution)/shard_map/ppermute | solution.py:47
  39.3 5.9 %collective-permute-start.10 = (bf16[256,256]{1,0:T(8,128)(2,1)S(1)}, bf16[256,256]{1,0:T(8,128)(2,1)S(1)}, u32[]{:S(2)}, u32[]{:S(2)}) collective-permute-start(bf16[256,256]{1,0:T(8,128)(2,1)S(1)} %get-tuple-element.43.refs_4_), channel_id=1, source_target_pairs={{0,1},{1,0},{2,3},{3,2},{4,5},{5,4},{6,7},{7,6},{8,9},{9,8},{10,11... | collective-permute-start | bytes 393224 | tf_op jit(solution)/shard_map/ppermute | solution.py:47
  41.7 3.5 %collective-permute-start.12 = (bf16[256,256]{1,0:T(8,128)(2,1)S(1)}, bf16[256,256]{1,0:T(8,128)(2,1)S(1)}, u32[]{:S(2)}, u32[]{:S(2)}) collective-permute-start(bf16[256,256]{1,0:T(8,128)(2,1)S(1)} %collective-permute-done.11.refs_5_), channel_id=1, source_target_pairs={{0,1},{1,0},{2,3},{3,2},{4,5},{5,4},{6,7},{7,6},{8,9},{9,8},{10,11... | collective-permute-start | bytes 393224 | tf_op jit(solution)/shard_map/ppermute | solution.py:47
  41.7 3.5 %collective-permute-start.14 = (bf16[256,256]{1,0:T(8,128)(2,1)S(1)}, bf16[256,256]{1,0:T(8,128)(2,1)S(1)}, u32[]{:S(2)}, u32[]{:S(2)}) collective-permute-start(bf16[256,256]{1,0:T(8,128)(2,1)S(1)} %collective-permute-done.13.refs_6_), channel_id=1, source_target_pairs={{0,1},{1,0},{2,3},{3,2},{4,5},{5,4},{6,7},{7,6},{8,9},{9,8},{10,11... | collective-permute-start | bytes 393224 | tf_op jit(solution)/shard_map/ppermute | solution.py:47
  45.1 7.3 %collective-permute-start.22 = (bf16[272,256]{1,0:T(8,128)(2,1)S(1)}, bf16[272,256]{1,0:T(8,128)(2,1)S(1)}, u32[]{:S(2)}, u32[]{:S(2)}) collective-permute-start(bf16[272,256]{1,0:T(8,128)(2,1)S(1)} %line_grads.2.refs_0_), channel_id=1, source_target_pairs={{0,8},{8,0},{16,24},{24,16},{1,9},{9,1},{17,25},{25,17},{2,10},{10... | collective-permute-start | bytes 417800 | tf_op jit(solution)/shard_map/ppermute | solution.py:47
  47.1 8.9 %collective-permute-start.17 = (bf16[256,256]{1,0:T(8,128)(2,1)S(1)}, bf16[256,256]{1,0:T(8,128)(2,1)S(1)}, u32[]{:S(2)}, u32[]{:S(2)}) collective-permute-start(bf16[256,256]{1,0:T(8,128)(2,1)S(1)} %get-tuple-element.45), channel_id=1, source_target_pairs={{0,8},{8,0},{16,24},{24,16},{1,9},{9,1},{17,25},{25,17},{2,10},{10... | collective-permute-start | bytes 393224 | tf_op jit(solution)/shard_map/ppermute | solution.py:47
  49.2 11.6 %collective-permute-start.18 = (bf16[256,256]{1,0:T(8,128)(2,1)S(1)}, bf16[256,256]{1,0:T(8,128)(2,1)S(1)}, u32[]{:S(2)}, u32[]{:S(2)}) collective-permute-start(bf16[256,256]{1,0:T(8,128)(2,1)S(1)} %get-tuple-element.46), channel_id=1, source_target_pairs={{0,16},{8,24},{16,0},{24,8},{1,17},{9,25},{17,1},{25,9},{2,18},{10... | collective-permute-start | bytes 393224 | tf_op jit(solution)/shard_map/ppermute | solution.py:47
  49.7 11.1 %collective-permute-start.19 = (bf16[256,256]{1,0:T(8,128)(2,1)S(1)}, bf16[256,256]{1,0:T(8,128)(2,1)S(1)}, u32[]{:S(2)}, u32[]{:S(2)}) collective-permute-start(bf16[256,256]{1,0:T(8,128)(2,1)S(1)} %get-tuple-element.47), channel_id=1, source_target_pairs={{0,24},{8,16},{16,8},{24,0},{1,25},{9,17},{17,9},{25,1},{2,26},{10... | collective-permute-start | bytes 393224 | tf_op jit(solution)/shard_map/ppermute | solution.py:47
  52.4 9.2 %collective-permute-start.23 = (bf16[272,256]{1,0:T(8,128)(2,1)S(1)}, bf16[272,256]{1,0:T(8,128)(2,1)S(1)}, u32[]{:S(2)}, u32[]{:S(2)}) collective-permute-start(bf16[272,256]{1,0:T(8,128)(2,1)S(1)} %line_grads.3.refs_0_), channel_id=1, source_target_pairs={{0,2},{1,3},{2,0},{3,1},{4,6},{5,7},{6,4},{7,5},{8,10},{9,11},{10,... | collective-permute-start | bytes 417800 | tf_op jit(solution)/shard_map/ppermute | solution.py:47
  54.0 7.7 %collective-permute-start.24 = (bf16[272,256]{1,0:T(8,128)(2,1)S(1)}, bf16[272,256]{1,0:T(8,128)(2,1)S(1)}, u32[]{:S(2)}, u32[]{:S(2)}) collective-permute-start(bf16[272,256]{1,0:T(8,128)(2,1)S(1)} %line_grads.3.refs_0_), channel_id=1, source_target_pairs={{0,4},{1,5},{2,6},{3,7},{4,0},{5,1},{6,2},{7,3},{8,12},{9,13},{10,... | collective-permute-start | bytes 417800 | tf_op jit(solution)/shard_map/ppermute | solution.py:47
  56.0 6.0 %collective-permute-start.25 = (bf16[272,256]{1,0:T(8,128)(2,1)S(1)}, bf16[272,256]{1,0:T(8,128)(2,1)S(1)}, u32[]{:S(2)}, u32[]{:S(2)}) collective-permute-start(bf16[272,256]{1,0:T(8,128)(2,1)S(1)} %line_grads.3.refs_0_), channel_id=1, source_target_pairs={{0,6},{1,7},{2,4},{3,5},{4,2},{5,3},{6,0},{7,1},{8,14},{9,15},{10,... | collective-permute-start | bytes 417800 | tf_op jit(solution)/shard_map/ppermute | solution.py:47
  61.7 1.6 %collective-permute-start.27 = (bf16[576,256]{1,0:T(8,128)(2,1)S(1)}, bf16[576,256]{1,0:T(8,128)(2,1)S(1)}, u32[]{:S(2)}, u32[]{:S(2)}) collective-permute-start(bf16[576,256]{1,0:T(8,128)(2,1)S(1)} %get-tuple-element.53), channel_id=1, source_target_pairs={{0,1},{1,0},{2,3},{3,2},{4,5},{5,4},{6,7},{7,6},{8,9},{9,8},{10,11... | collective-permute-start | bytes 884744 | tf_op jit(solution)/shard_map/ppermute | solution.py:47
  62.0 1.6 %collective-permute-start.26 = (f32[256,256]{1,0:T(8,128)S(1)}, f32[256,256]{1,0:T(8,128)S(1)}, u32[]{:S(2)}, u32[]{:S(2)}) collective-permute-start(f32[256,256]{1,0:T(8,128)S(1)} %get-tuple-element.51.mine_ref), channel_id=1, source_target_pairs={{0,1},{1,0},{2,3},{3,2},{4,5},{5,4},{6,7},{7,6},{8,9},{9,8},{10,11... | collective-permute-start | bytes 786440 | tf_op jit(solution)/shard_map/ppermute | solution.py:47

commit v5 on v4

--- a/solution.py
+++ b/solution.py
@@ -11,7 +11,7 @@
 BF16 = jnp.bfloat16
 F32 = jnp.float32
 BIAS_ROWS = 16
-SPACER_ROWS = 576
+SPACER_ROWS = 304
 FAR_ROWS = 32
 VMEM_LIMIT = 40 * 1024 * 1024
 CONTRACT_FIRST = (((0,), (0,)), ((), ()))
@@ -273,45 +273,50 @@
 
 def all_grads_kernel(n, *refs):
     body, line = load_sum(refs[:n])
-    refs[n][...] = body
-    refs[n + 1][...] = line
+    half = body.shape[0] // 2
+    refs[n][...] = body[:half, :]
+    refs[n + 1][...] = body[half:, :]
+    refs[n + 2][...] = line
 
 
 def all_grads(parts):
     n = len(parts)
     rows, width = parts[0].shape
+    half = jax.ShapeDtypeStruct(((rows - BIAS_ROWS) // 2, width), F32)
     return pl.pallas_call(
         functools.partial(all_grads_kernel, n),
         in_specs=whole(n),
-        out_specs=whole(2),
-        out_shape=[
-            jax.ShapeDtypeStruct((rows - BIAS_ROWS, width), F32),
-            jax.ShapeDtypeStruct((1, width), F32),
-        ],
+        out_specs=whole(3),
+        out_shape=[half, half, jax.ShapeDtypeStruct((1, width), F32)],
         compiler_params=params(),
         name="all_grads",
     )(*parts)
 
 
-def place_grads_kernel(ids_ref, mine_ref, other_ref, line_ref, after_ref, self_ref, neigh_ref, bias_ref):
+def place_grads_kernel(ids_ref, *refs):
+    mine_refs, other_refs, (line_ref, after_ref, self_ref, neigh_ref, bias_ref) = refs[:2], refs[2:4], refs[4:]
     first = (ids_ref[0] & 1) == 0
-    self_ref[...] = jnp.where(first, mine_ref[...], other_ref[...])
-    neigh_ref[...] = jnp.where(first, other_ref[...], mine_ref[...])
+    half = refs[0].shape[0]
+    for k, (mine_ref, other_ref) in enumerate(zip(mine_refs, other_refs)):
+        at = slice(k * half, (k + 1) * half)
+        self_ref[at, :] = jnp.where(first, mine_ref[...], other_ref[...])
+        neigh_ref[at, :] = jnp.where(first, other_ref[...], mine_ref[...])
     bias_ref[...] = line_ref[...]
 
 
 def place_grads(ids, mine, other, line, after):
-    out = jax.ShapeDtypeStruct(mine.shape, F32)
+    rows, width = mine[0].shape
+    out = jax.ShapeDtypeStruct((2 * rows, width), F32)
     return pl.pallas_call(
         place_grads_kernel,
         in_specs=[pl.BlockSpec(memory_space=pltpu.SMEM)]
-        + whole(3)
+        + whole(5)
         + [pl.BlockSpec(memory_space=pl.ANY)],
         out_specs=whole(3),
         out_shape=[out, out, jax.ShapeDtypeStruct(line.shape, F32)],
         compiler_params=params(),
         name="place_grads",
-    )(ids, mine, other, line, after)
+    )(ids, *mine, *other, line, after)
 
 
 def extend_kernel(in_ref, out_ref):
@@ -441,12 +446,11 @@
     arrived = [xor_permute(spread[k], "row", k) for k in range(1, row_devices)]
     grad_features, spacer = feature_grads(dpre, self_weight, spread[0], arrived)
     late = xor_permute(spacer, "rep", 1)
-    mine, bias_line = all_grads(
+    *mine, bias_line = all_grads(
         [line] + [xor_permute(line, "rep", 2 * q) for q in range(1, chips)]
     )
-    grad_self, grad_neigh, grad_bias = place_grads(
-        ids, mine, xor_permute(mine, "rep", 1), bias_line, late
-    )
+    other = [xor_permute(value, "rep", 1) for value in mine]
+    grad_self, grad_neigh, grad_bias = place_grads(ids, mine, other, bias_line, late)
     return (hidden_out, grad_features, grad_self, grad_neigh, grad_bias[0])
 
 

time: 65.3 us -> 65.3 us (level)
    ppermute x28 -> x29, starting transfers between devices: 28.6 us -> 28.9 us  [xor_permute(): lax.ppermute(value, axis, [(i, i ^ k) for i in range(lax.axis_size(axis))])]
    ppermute x28 -> x29, waiting for transfers between devices: 19.3 us -> 19.1 us  [xor_permute(): lax.ppermute(value, axis, [(i, i ^ k) for i in range(lax.axis_size(axis))])]
  transfers between devices with their start and end apart: 28 -> 29, of which waited for: 13 -> 14; matrix products, arithmetic and copies ran while one was open for 0% -> 0% of each run, Pallas kernels for 11% -> 11%
where the time goes in v5:
time: 65.3 us; the launch traced here: 65.1 us
  starting transfers between devices  28.9 us (44%)
  waiting for transfers between devices  19.1 us (29%)
  Pallas kernels  11.3 us (17%)
  local copies, waits for them, and re-layouts  4.9 us (8%)
  between operations  0.87 us (1%)
    ppermute x29, starting transfers between devices, xor_permute(): lax.ppermute(value, axis, [(i, i ^ k) for i in range(lax.axis_size(axis))])  28.9 us
    ppermute x29, waiting for transfers between devices, xor_permute(): lax.ppermute(value, axis, [(i, i ^ k) for i in range(lax.axis_size(axis))])  19.1 us
    unnamed x18, local copies, waits for them, and re-layouts  4.8 us
    pallas_call x1, Pallas kernels, build_strip(): pl.pallas_call(functools.partial(strip_kernel, panels, blocks, tile, chip...  2.92 us
    pallas_call x1, Pallas kernels, back_sums(): pl.pallas_call(functools.partial(back_kernel, n), in_specs=[pl.BlockSpec(...  1.86 us
    pallas_call x1, Pallas kernels, rows_step(): pl.pallas_call(functools.partial(rows_kernel, m, scale), in_specs=[pl.Blo...  1.67 us
    pallas_call x1, Pallas kernels, place_grads(): pl.pallas_call(place_grads_kernel, in_specs=[pl.BlockSpec(memory_space=pl...  1.38 us
  transfers between devices with their start and end apart: 29, of which 14 were waited for; matrix products, arithmetic and copies ran while one was open for 0% of the time, Pallas kernels for 11%

profile of v5, /device:TPU:0, one launch (start us, length us, event | category | flops | bytes accessed | tf_op | source)
XLA Modules:
  0.0 65.1 jit_solution(15799048670658315306)
XLA Ops:
  0.6 0.0 copy-start
  0.7 1.2 %copy-done = bf16[2048,256]{1,0:T(8,128)(2,1)S(1)} copy-done((bf16[2048,256]{1,0:T(8,128)(2,1)S(1)}, bf16[2048,256]{1,0:T(8,128)(2,1)}, u32[]{:S(2)}) %copy-start) | copy-done | bytes 1048600
  1.9 3.1 %collective-permute-start = (bf16[256,256]{1,0:T(8,128)(2,1)S(1)}, bf16[256,256]{1,0:T(8,128)(2,1)S(1)}, u32[]{:S(2)}, u32[]{:S(2)}) collective-permute-start(bf16[256,256]{1,0:T(8,128)(2,1)S(1)} %constant_dynamic-slice_fusion.refs_0_.own_ref), channel_id=1, source_target_pairs={{0,8},{8,0},{16,24},{24,16},{1,9},{9,1},{17,25},{25,17},{2,10},{10... | collective-permute-start | bytes 393224 | tf_op jit(solution)/shard_map/ppermute | solution.py:47
  5.0 2.6 %collective-permute-start.1 = (bf16[256,256]{1,0:T(8,128)(2,1)S(1)}, bf16[256,256]{1,0:T(8,128)(2,1)S(1)}, u32[]{:S(2)}, u32[]{:S(2)}) collective-permute-start(bf16[256,256]{1,0:T(8,128)(2,1)S(1)} %constant_dynamic-slice_fusion.refs_0_.own_ref), channel_id=1, source_target_pairs={{0,16},{8,24},{16,0},{24,8},{1,17},{9,25},{17,1},{25,9},{2,18},{10... | collective-permute-start | bytes 393224 | tf_op jit(solution)/shard_map/ppermute | solution.py:47
  7.6 0.0 collective-permute-start.2
  7.6 0.1 pad_add_fusion.ids_ref
  7.6 2.2 %copy-done.1 = s32[2048,4,128]{2,1,0:T(4,128)S(1)} copy-done((s32[2048,4,128]{2,1,0:T(4,128)S(1)}, s32[2048,4,128]{2,1,0:T(4,128)}, u32[]{:S(2)}) %copy-start.1) | copy-done | bytes 4194328
  9.8 0.7 %copy-done.5 = s32[16,4]{0,1:T(4,128)S(1)} copy-done((s32[16,4]{0,1:T(4,128)S(1)}, s32[16,4]{0,1:T(4,128)}, u32[]{:S(2)}) %copy-start.5) | copy-done | bytes 280
  10.5 0.7 %copy-done.6 = s32[16,4]{0,1:T(4,128)S(1)} copy-done((s32[16,4]{0,1:T(4,128)S(1)}, s32[16,4]{0,1:T(4,128)}, u32[]{:S(2)}) %copy-start.6) | copy-done | bytes 280
  11.2 2.9 %build_strip.1 = (bf16[2048,1024]{1,0:T(8,128)(2,1)S(1)}, bf16[1024,2048]{1,0:T(8,128)(2,1)S(1)}) custom-call(s32[2]{0:T(128)S(1)} %pad_add_fusion.ids_ref, s32[4,16]{1,0:T(4,128)S(1)} %bitcast.8, s32[4,16]{1,0:T(4,128)S(1)} %bitcast.9, s32[8192,128]{1,0:T(8,128)S(1)} %bitcast.7), custom_call_target="tpu_custom_call" | custom-call | tf_op jit(solution)/shard_map/build_strip/pallas_call | solution.py:74
  14.1 3.8 %collective-permute-done.1.refs_2_ = bf16[256,256]{1,0:T(8,128)(2,1)S(1)} collective-permute-done((bf16[256,256]{1,0:T(8,128)(2,1)S(1)}, bf16[256,256]{1,0:T(8,128)(2,1)S(1)}, u32[]{:S(2)}, u32[]{:S(2)}) %collective-permute-start.1) | collective-permute-done | bytes 131104 | tf_op jit(solution)/shard_map/ppermute | solution.py:47
  17.9 0.0 collective-permute-done.2.refs_3_
  17.9 0.9 %away_far.1 = (bf16[256,256]{1,0:T(8,128)(2,1)S(1)}, bf16[1024,256]{1,0:T(8,128)(2,1)S(1)}) custom-call(s32[2]{0:T(128)S(1)} %pad_add_fusion.ids_ref, bf16[2048,1024]{1,0:T(8,128)(2,1)S(1)} %get-tuple-element.32.dense_ref, bf16[256,256]{1,0:T(8,128)(2,1)S(1)} %constant_dynamic-slice_fusion.refs_0_.own_ref, ...), custom_call_target="tpu_custom_call" | custom-call | tf_op jit(solution)/shard_map/away_far/pallas_call | solution.py:115
  18.8 0.1 collective-permute-start.6
  18.9 0.6 away_near.1
  19.4 0.6 collective-permute-start.3
  20.0 0.1 collective-permute-start.4
  20.1 0.4 collective-permute-start.5
  20.5 0.0 collective-permute-done.6.refs_0_
  20.5 0.3 chip_far.1
  20.8 0.0 copy-start.2
  20.9 0.0 copy-start.3
  20.9 0.0 copy-start.4
  20.9 0.0 copy-start.7
  20.9 2.5 %collective-permute-start.7 = (bf16[256,256]{1,0:T(8,128)(2,1)S(1)}, bf16[256,256]{1,0:T(8,128)(2,1)S(1)}, u32[]{:S(2)}, u32[]{:S(2)}) collective-permute-start(bf16[256,256]{1,0:T(8,128)(2,1)S(1)} %chip_far.1), channel_id=1, source_target_pairs={{0,6},{1,7},{2,4},{3,5},{4,2},{5,3},{6,0},{7,1},{8,14},{9,15},{10,... | collective-permute-start | bytes 393224 | tf_op jit(solution)/shard_map/ppermute | solution.py:47
  23.4 0.6 chip_near.1
  24.0 0.6 collective-permute-start.8
  24.6 0.6 collective-permute-start.9
  25.2 2.2 %collective-permute-done.7.far_ref = bf16[256,256]{1,0:T(8,128)(2,1)S(1)} collective-permute-done((bf16[256,256]{1,0:T(8,128)(2,1)S(1)}, bf16[256,256]{1,0:T(8,128)(2,1)S(1)}, u32[]{:S(2)}, u32[]{:S(2)}) %collective-permute-start.7) | collective-permute-done | bytes 131104 | tf_op jit(solution)/shard_map/ppermute | solution.py:47
  27.5 2.7 %collective-permute-done.8.refs_0_ = bf16[256,256]{1,0:T(8,128)(2,1)S(1)} collective-permute-done((bf16[256,256]{1,0:T(8,128)(2,1)S(1)}, bf16[256,256]{1,0:T(8,128)(2,1)S(1)}, u32[]{:S(2)}, u32[]{:S(2)}) %collective-permute-start.8) | collective-permute-done | bytes 131104 | tf_op jit(solution)/shard_map/ppermute | solution.py:47
  30.1 0.1 collective-permute-done.9.refs_1_
  30.2 0.1 broadcast_in_dim.10.deg_ref
  30.3 1.7 %rows_step.1 = (bf16[256,256]{1,0:T(8,128)(2,1)}, bf16[256,256]{1,0:T(8,128)(2,1)S(1)}, bf16[256,256]{1,0:T(8,128)(2,1)S(1)}, f32[272,256]{1,0:T(8,128)S(1)}, f32[272,256]{1,0:T(8,128)S(1)}) custom-call(s32[2]{0:T(128)S(1)} %pad_add_fusion.ids_ref, bf16[256,256]{1,0:T(8,128)(2,1)S(1)} %constant_dynamic-slice_fusion.refs_0_.own_ref, ...), custom_call_target="tpu_custom_call" | custom-call | tf_op jit(solution)/shard_map/rows_step/pallas_call | solution.py:214
  32.0 2.4 %collective-permute-start.15 = (bf16[256,256]{1,0:T(8,128)(2,1)S(1)}, bf16[256,256]{1,0:T(8,128)(2,1)S(1)}, u32[]{:S(2)}, u32[]{:S(2)}) collective-permute-start(bf16[256,256]{1,0:T(8,128)(2,1)S(1)} %get-tuple-element.44.refs_4_), channel_id=1, source_target_pairs={{0,6},{1,7},{2,4},{3,5},{4,2},{5,3},{6,0},{7,1},{8,14},{9,15},{10,... | collective-permute-start | bytes 393224 | tf_op jit(solution)/shard_map/ppermute | solution.py:47
  34.5 0.5 collective-permute-start.11
  35.0 0.5 collective-permute-start.13
  35.5 0.1 pair_grads.1.refs_0_
  35.6 3.0 %collective-permute-start.21 = (bf16[272,256]{1,0:T(8,128)(2,1)S(1)}, bf16[272,256]{1,0:T(8,128)(2,1)S(1)}, u32[]{:S(2)}, u32[]{:S(2)}) collective-permute-start(bf16[272,256]{1,0:T(8,128)(2,1)S(1)} %pair_grads.1.refs_0_), channel_id=1, source_target_pairs={{0,16},{8,24},{16,0},{24,8},{1,17},{9,25},{17,1},{25,9},{2,18},{10... | collective-permute-start | bytes 417800 | tf_op jit(solution)/shard_map/ppermute | solution.py:47
  38.6 0.6 collective-permute-done.15.in_ref.refs_7_
  39.2 0.1 collective-permute-start.16
  39.3 0.5 collective-permute-start.10
  39.8 1.9 %collective-permute-done.11.refs_5_ = bf16[256,256]{1,0:T(8,128)(2,1)S(1)} collective-permute-done((bf16[256,256]{1,0:T(8,128)(2,1)S(1)}, bf16[256,256]{1,0:T(8,128)(2,1)S(1)}, u32[]{:S(2)}, u32[]{:S(2)}) %collective-permute-start.11) | collective-permute-done | bytes 131104 | tf_op jit(solution)/shard_map/ppermute | solution.py:47
  41.7 0.5 collective-permute-start.14
  42.2 2.9 %collective-permute-done.21.refs_1_ = bf16[272,256]{1,0:T(8,128)(2,1)S(1)} collective-permute-done((bf16[272,256]{1,0:T(8,128)(2,1)S(1)}, bf16[272,256]{1,0:T(8,128)(2,1)S(1)}, u32[]{:S(2)}, u32[]{:S(2)}) %collective-permute-start.21) | collective-permute-done | bytes 139296 | tf_op jit(solution)/shard_map/ppermute | solution.py:47
  45.1 0.1 collective-permute-start.22
  45.2 1.9 %back_sums.1 = (f32[256,256]{1,0:T(8,128)S(1)}, bf16[256,256]{1,0:T(8,128)(2,1)S(1)}, bf16[256,256]{1,0:T(8,128)(2,1)S(1)}, bf16[256,256]{1,0:T(8,128)(2,1)S(1)}) custom-call(s32[2]{0:T(128)S(1)} %pad_add_fusion.ids_ref, bf16[1024,2048]{1,0:T(8,128)(2,1)S(1)} %get-tuple-element.43.flip_ref, bf16[256,256]{1,0:T(8,128)(2,1)S(1)} %collective-permute-done.10.refs_0_, ...), custom_call_target="tpu_custom_call" | custom-call | tf_op jit(solution)/shard_map/back_sums/pallas_call | solution.py:356
  47.1 2.1 %collective-permute-start.17 = (bf16[256,256]{1,0:T(8,128)(2,1)S(1)}, bf16[256,256]{1,0:T(8,128)(2,1)S(1)}, u32[]{:S(2)}, u32[]{:S(2)}) collective-permute-start(bf16[256,256]{1,0:T(8,128)(2,1)S(1)} %get-tuple-element.46), channel_id=1, source_target_pairs={{0,8},{8,0},{16,24},{24,16},{1,9},{9,1},{17,25},{25,17},{2,10},{10... | collective-permute-start | bytes 393224 | tf_op jit(solution)/shard_map/ppermute | solution.py:47
  49.2 0.6 collective-permute-start.18
  49.7 1.9 %collective-permute-start.19 = (bf16[256,256]{1,0:T(8,128)(2,1)S(1)}, bf16[256,256]{1,0:T(8,128)(2,1)S(1)}, u32[]{:S(2)}, u32[]{:S(2)}) collective-permute-start(bf16[256,256]{1,0:T(8,128)(2,1)S(1)} %get-tuple-element.48), channel_id=1, source_target_pairs={{0,24},{8,16},{16,8},{24,0},{1,25},{9,17},{17,9},{25,1},{2,26},{10... | collective-permute-start | bytes 393224 | tf_op jit(solution)/shard_map/ppermute | solution.py:47
  51.6 0.8 %collective-permute-done.22.refs_1_ = bf16[272,256]{1,0:T(8,128)(2,1)S(1)} collective-permute-done((bf16[272,256]{1,0:T(8,128)(2,1)S(1)}, bf16[272,256]{1,0:T(8,128)(2,1)S(1)}, u32[]{:S(2)}, u32[]{:S(2)}) %collective-permute-start.22) | collective-permute-done | bytes 139296 | tf_op jit(solution)/shard_map/ppermute | solution.py:47
  52.5 1.6 %collective-permute-start.23 = (bf16[272,256]{1,0:T(8,128)(2,1)S(1)}, bf16[272,256]{1,0:T(8,128)(2,1)S(1)}, u32[]{:S(2)}, u32[]{:S(2)}) collective-permute-start(bf16[272,256]{1,0:T(8,128)(2,1)S(1)} %line_grads.3.refs_0_), channel_id=1, source_target_pairs={{0,2},{1,3},{2,0},{3,1},{4,6},{5,7},{6,4},{7,5},{8,10},{9,11},{10,... | collective-permute-start | bytes 417800 | tf_op jit(solution)/shard_map/ppermute | solution.py:47
  54.0 1.3 %collective-permute-start.24 = (bf16[272,256]{1,0:T(8,128)(2,1)S(1)}, bf16[272,256]{1,0:T(8,128)(2,1)S(1)}, u32[]{:S(2)}, u32[]{:S(2)}) collective-permute-start(bf16[272,256]{1,0:T(8,128)(2,1)S(1)} %line_grads.3.refs_0_), channel_id=1, source_target_pairs={{0,4},{1,5},{2,6},{3,7},{4,0},{5,1},{6,2},{7,3},{8,12},{9,13},{10,... | collective-permute-start | bytes 417800 | tf_op jit(solution)/shard_map/ppermute | solution.py:47
  55.3 0.7 %collective-permute-done.17.refs_0_ = bf16[256,256]{1,0:T(8,128)(2,1)S(1)} collective-permute-done((bf16[256,256]{1,0:T(8,128)(2,1)S(1)}, bf16[256,256]{1,0:T(8,128)(2,1)S(1)}, u32[]{:S(2)}, u32[]{:S(2)}) %collective-permute-start.17) | collective-permute-done | bytes 131104 | tf_op jit(solution)/shard_map/ppermute | solution.py:47
  56.0 2.7 %collective-permute-start.25 = (bf16[272,256]{1,0:T(8,128)(2,1)S(1)}, bf16[272,256]{1,0:T(8,128)(2,1)S(1)}, u32[]{:S(2)}, u32[]{:S(2)}) collective-permute-start(bf16[272,256]{1,0:T(8,128)(2,1)S(1)} %line_grads.3.refs_0_), channel_id=1, source_target_pairs={{0,6},{1,7},{2,4},{3,5},{4,2},{5,3},{6,0},{7,1},{8,14},{9,15},{10,... | collective-permute-start | bytes 417800 | tf_op jit(solution)/shard_map/ppermute | solution.py:47
  58.7 2.1 %collective-permute-done.18.refs_1_ = bf16[256,256]{1,0:T(8,128)(2,1)S(1)} collective-permute-done((bf16[256,256]{1,0:T(8,128)(2,1)S(1)}, bf16[256,256]{1,0:T(8,128)(2,1)S(1)}, u32[]{:S(2)}, u32[]{:S(2)}) %collective-permute-start.18) | collective-permute-done | bytes 131104 | tf_op jit(solution)/shard_map/ppermute | solution.py:47
  60.8 0.9 %feature_grads.1 = (bf16[256,256]{1,0:T(8,128)(2,1)}, bf16[304,256]{1,0:T(8,128)(2,1)S(1)}) custom-call(bf16[256,256]{1,0:T(8,128)(2,1)S(1)} %get-tuple-element.42.dpre_ref, bf16[256,256]{1,0:T(8,128)(2,1)S(1)} %copy-done.2, f32[256,256]{1,0:T(8,128)S(1)} %get-tuple-element.45.own_ref, bf16[256,256]{1,0:T(8,128)(2,1)S(1)} %collective-permute-done.17.refs_0_, ...), custom_call_target="tpu_custom_call" | custom-call | tf_op jit(solution)/shard_map/feature_grads/pallas_call | solution.py:380
  61.7 0.2 collective-permute-done.25.refs_3_
  61.9 0.1 all_grads.1
  62.0 0.4 collective-permute-start.26
  62.4 0.2 collective-permute-start.27
  62.6 0.5 collective-permute-done.28.refs_5_
  63.1 0.3 collective-permute-done.26.refs_2_
  63.4 0.3 collective-permute-done.27.refs_3_
  63.7 1.4 %place_grads.1 = (f32[256,256]{1,0:T(8,128)}, f32[256,256]{1,0:T(8,128)}, f32[1,256]{1,0:T(1,128)}) custom-call(s32[2]{0:T(128)S(1)} %pad_add_fusion.ids_ref, f32[128,256]{1,0:T(8,128)S(1)} %get-tuple-element.52.refs_0_, f32[128,256]{1,0:T(8,128)S(1)} %get-tuple-element.53.refs_1_, f32[128,256]{1,0:T(8,128)S(1)} %collective-permute-done.26.refs_2_, ...), custom_call_target="tpu_custom_call" | custom-call | tf_op jit(solution)/shard_map/place_grads/pallas_call | solution.py:310
  (31 shorter events, 0.2 us)
Async XLA Ops:
  0.6 1.2 %copy-start = (bf16[2048,256]{1,0:T(8,128)(2,1)S(1)}, bf16[2048,256]{1,0:T(8,128)(2,1)}, u32[]{:S(2)}) copy-start(bf16[2048,256]{1,0:T(8,128)(2,1)} %param.9) | copy-start | bytes 3145732
  1.9 12.2 %collective-permute-start = (bf16[256,256]{1,0:T(8,128)(2,1)S(1)}, bf16[256,256]{1,0:T(8,128)(2,1)S(1)}, u32[]{:S(2)}, u32[]{:S(2)}) collective-permute-start(bf16[256,256]{1,0:T(8,128)(2,1)S(1)} %constant_dynamic-slice_fusion.refs_0_.own_ref), channel_id=1, source_target_pairs={{0,8},{8,0},{16,24},{24,16},{1,9},{9,1},{17,25},{25,17},{2,10},{10... | collective-permute-start | bytes 393224 | tf_op jit(solution)/shard_map/ppermute | solution.py:47
  5.0 12.9 %collective-permute-start.1 = (bf16[256,256]{1,0:T(8,128)(2,1)S(1)}, bf16[256,256]{1,0:T(8,128)(2,1)S(1)}, u32[]{:S(2)}, u32[]{:S(2)}) collective-permute-start(bf16[256,256]{1,0:T(8,128)(2,1)S(1)} %constant_dynamic-slice_fusion.refs_0_.own_ref), channel_id=1, source_target_pairs={{0,16},{8,24},{16,0},{24,8},{1,17},{9,25},{17,1},{25,9},{2,18},{10... | collective-permute-start | bytes 393224 | tf_op jit(solution)/shard_map/ppermute | solution.py:47
  7.6 10.3 %collective-permute-start.2 = (bf16[256,256]{1,0:T(8,128)(2,1)S(1)}, bf16[256,256]{1,0:T(8,128)(2,1)S(1)}, u32[]{:S(2)}, u32[]{:S(2)}) collective-permute-start(bf16[256,256]{1,0:T(8,128)(2,1)S(1)} %constant_dynamic-slice_fusion.refs_0_.own_ref), channel_id=1, source_target_pairs={{0,24},{8,16},{16,8},{24,0},{1,25},{9,17},{17,9},{25,1},{2,26},{10... | collective-permute-start | bytes 393224 | tf_op jit(solution)/shard_map/ppermute | solution.py:47
  7.6 2.2 %copy-start.1 = (s32[2048,4,128]{2,1,0:T(4,128)S(1)}, s32[2048,4,128]{2,1,0:T(4,128)}, u32[]{:S(2)}) copy-start(s32[2048,4,128]{2,1,0:T(4,128)} %param.13) | copy-start | bytes 12582916
  9.8 0.7 %copy-start.5 = (s32[16,4]{0,1:T(4,128)S(1)}, s32[16,4]{0,1:T(4,128)}, u32[]{:S(2)}) copy-start(s32[16,4]{0,1:T(4,128)} %param.14) | copy-start | bytes 772
  10.5 0.7 %copy-start.6 = (s32[16,4]{0,1:T(4,128)S(1)}, s32[16,4]{0,1:T(4,128)}, u32[]{:S(2)}) copy-start(s32[16,4]{0,1:T(4,128)} %param.15) | copy-start | bytes 772
  18.8 1.7 %collective-permute-start.6 = (bf16[256,256]{1,0:T(8,128)(2,1)S(1)}, bf16[256,256]{1,0:T(8,128)(2,1)S(1)}, u32[]{:S(2)}, u32[]{:S(2)}) collective-permute-start(bf16[256,256]{1,0:T(8,128)(2,1)S(1)} %get-tuple-element.38), channel_id=1, source_target_pairs={{0,1},{1,0},{2,3},{3,2},{4,5},{5,4},{6,7},{7,6},{8,9},{9,8},{10,11... | collective-permute-start | bytes 393224 | tf_op jit(solution)/shard_map/ppermute | solution.py:47
  19.4 4.0 %collective-permute-start.3 = (bf16[256,256]{1,0:T(8,128)(2,1)S(1)}, bf16[256,256]{1,0:T(8,128)(2,1)S(1)}, u32[]{:S(2)}, u32[]{:S(2)}) collective-permute-start(bf16[256,256]{1,0:T(8,128)(2,1)S(1)} %get-tuple-element.34), channel_id=1, source_target_pairs={{0,1},{1,0},{2,3},{3,2},{4,5},{5,4},{6,7},{7,6},{8,9},{9,8},{10,11... | collective-permute-start | bytes 393224 | tf_op jit(solution)/shard_map/ppermute | solution.py:47
  20.0 3.4 %collective-permute-start.4 = (bf16[256,256]{1,0:T(8,128)(2,1)S(1)}, bf16[256,256]{1,0:T(8,128)(2,1)S(1)}, u32[]{:S(2)}, u32[]{:S(2)}) collective-permute-start(bf16[256,256]{1,0:T(8,128)(2,1)S(1)} %get-tuple-element.35), channel_id=1, source_target_pairs={{0,1},{1,0},{2,3},{3,2},{4,5},{5,4},{6,7},{7,6},{8,9},{9,8},{10,11... | collective-permute-start | bytes 393224 | tf_op jit(solution)/shard_map/ppermute | solution.py:47
  20.1 5.1 %copy-start.8 = (s32[256]{0:T(256)S(1)}, s32[256]{0:T(256)}, u32[]{:S(2)}) copy-start(s32[256]{0:T(256)} %param.16) | copy-start | bytes 3076
  20.1 3.3 %collective-permute-start.5 = (bf16[256,256]{1,0:T(8,128)(2,1)S(1)}, bf16[256,256]{1,0:T(8,128)(2,1)S(1)}, u32[]{:S(2)}, u32[]{:S(2)}) collective-permute-start(bf16[256,256]{1,0:T(8,128)(2,1)S(1)} %get-tuple-element.36), channel_id=1, source_target_pairs={{0,1},{1,0},{2,3},{3,2},{4,5},{5,4},{6,7},{7,6},{8,9},{9,8},{10,11... | collective-permute-start | bytes 393224 | tf_op jit(solution)/shard_map/ppermute | solution.py:47
  20.8 9.5 %copy-start.2 = (bf16[256,256]{1,0:T(8,128)(2,1)S(1)}, bf16[256,256]{1,0:T(8,128)(2,1)}, u32[]{:S(2)}) copy-start(bf16[256,256]{1,0:T(8,128)(2,1)} %ws_ref.3) | copy-start | bytes 393220
  20.9 9.5 %copy-start.3 = (bf16[256,256]{1,0:T(8,128)(2,1)S(1)}, bf16[256,256]{1,0:T(8,128)(2,1)}, u32[]{:S(2)}) copy-start(bf16[256,256]{1,0:T(8,128)(2,1)} %wn_ref.1) | copy-start | bytes 393220
  20.9 9.5 %copy-start.4 = (bf16[256,256]{1,0:T(8,128)(2,1)S(1)}, bf16[256,256]{1,0:T(8,128)(2,1)}, u32[]{:S(2)}) copy-start(bf16[256,256]{1,0:T(8,128)(2,1)} %cot_ref.1) | copy-start | bytes 393220
  20.9 9.5 %copy-start.7 = (f32[256]{0:T(256)S(1)}, f32[256]{0:T(256)}, u32[]{:S(2)}) copy-start(f32[256]{0:T(256)} %param.12) | copy-start | bytes 3076
  20.9 6.5 %collective-permute-start.7 = (bf16[256,256]{1,0:T(8,128)(2,1)S(1)}, bf16[256,256]{1,0:T(8,128)(2,1)S(1)}, u32[]{:S(2)}, u32[]{:S(2)}) collective-permute-start(bf16[256,256]{1,0:T(8,128)(2,1)S(1)} %chip_far.1), channel_id=1, source_target_pairs={{0,6},{1,7},{2,4},{3,5},{4,2},{5,3},{6,0},{7,1},{8,14},{9,15},{10,... | collective-permute-start | bytes 393224 | tf_op jit(solution)/shard_map/ppermute | solution.py:47
  24.0 6.1 %collective-permute-start.8 = (bf16[256,256]{1,0:T(8,128)(2,1)S(1)}, bf16[256,256]{1,0:T(8,128)(2,1)S(1)}, u32[]{:S(2)}, u32[]{:S(2)}) collective-permute-start(bf16[256,256]{1,0:T(8,128)(2,1)S(1)} %get-tuple-element.39), channel_id=1, source_target_pairs={{0,4},{1,5},{2,6},{3,7},{4,0},{5,1},{6,2},{7,3},{8,12},{9,13},{10,... | collective-permute-start | bytes 393224 | tf_op jit(solution)/shard_map/ppermute | solution.py:47
  24.6 5.6 %collective-permute-start.9 = (bf16[256,256]{1,0:T(8,128)(2,1)S(1)}, bf16[256,256]{1,0:T(8,128)(2,1)S(1)}, u32[]{:S(2)}, u32[]{:S(2)}) collective-permute-start(bf16[256,256]{1,0:T(8,128)(2,1)S(1)} %get-tuple-element.40), channel_id=1, source_target_pairs={{0,2},{1,3},{2,0},{3,1},{4,6},{5,7},{6,4},{7,5},{8,10},{9,11},{10,... | collective-permute-start | bytes 393224 | tf_op jit(solution)/shard_map/ppermute | solution.py:47
  32.0 3.5 %collective-permute-start.20 = (f32[272,256]{1,0:T(8,128)S(1)}, f32[272,256]{1,0:T(8,128)S(1)}, u32[]{:S(2)}, u32[]{:S(2)}) collective-permute-start(f32[272,256]{1,0:T(8,128)S(1)} %get-tuple-element.51), channel_id=1, source_target_pairs={{0,1},{1,0},{2,3},{3,2},{4,5},{5,4},{6,7},{7,6},{8,9},{9,8},{10,11... | collective-permute-start | bytes 835592 | tf_op jit(solution)/shard_map/ppermute | solution.py:47
  32.0 7.2 %collective-permute-start.15 = (bf16[256,256]{1,0:T(8,128)(2,1)S(1)}, bf16[256,256]{1,0:T(8,128)(2,1)S(1)}, u32[]{:S(2)}, u32[]{:S(2)}) collective-permute-start(bf16[256,256]{1,0:T(8,128)(2,1)S(1)} %get-tuple-element.44.refs_4_), channel_id=1, source_target_pairs={{0,6},{1,7},{2,4},{3,5},{4,2},{5,3},{6,0},{7,1},{8,14},{9,15},{10,... | collective-permute-start | bytes 393224 | tf_op jit(solution)/shard_map/ppermute | solution.py:47
  34.5 7.2 %collective-permute-start.11 = (bf16[256,256]{1,0:T(8,128)(2,1)S(1)}, bf16[256,256]{1,0:T(8,128)(2,1)S(1)}, u32[]{:S(2)}, u32[]{:S(2)}) collective-permute-start(bf16[256,256]{1,0:T(8,128)(2,1)S(1)} %get-tuple-element.44.refs_4_), channel_id=1, source_target_pairs={{0,2},{1,3},{2,0},{3,1},{4,6},{5,7},{6,4},{7,5},{8,10},{9,11},{10,... | collective-permute-start | bytes 393224 | tf_op jit(solution)/shard_map/ppermute | solution.py:47
  35.0 6.7 %collective-permute-start.13 = (bf16[256,256]{1,0:T(8,128)(2,1)S(1)}, bf16[256,256]{1,0:T(8,128)(2,1)S(1)}, u32[]{:S(2)}, u32[]{:S(2)}) collective-permute-start(bf16[256,256]{1,0:T(8,128)(2,1)S(1)} %get-tuple-element.44.refs_4_), channel_id=1, source_target_pairs={{0,4},{1,5},{2,6},{3,7},{4,0},{5,1},{6,2},{7,3},{8,12},{9,13},{10,... | collective-permute-start | bytes 393224 | tf_op jit(solution)/shard_map/ppermute | solution.py:47
  35.6 9.5 %collective-permute-start.21 = (bf16[272,256]{1,0:T(8,128)(2,1)S(1)}, bf16[272,256]{1,0:T(8,128)(2,1)S(1)}, u32[]{:S(2)}, u32[]{:S(2)}) collective-permute-start(bf16[272,256]{1,0:T(8,128)(2,1)S(1)} %pair_grads.1.refs_0_), channel_id=1, source_target_pairs={{0,16},{8,24},{16,0},{24,8},{1,17},{9,25},{17,1},{25,9},{2,18},{10... | collective-permute-start | bytes 417800 | tf_op jit(solution)/shard_map/ppermute | solution.py:47
  39.2 6.0 %collective-permute-start.16 = (bf16[288,256]{1,0:T(8,128)(2,1)S(1)}, bf16[288,256]{1,0:T(8,128)(2,1)S(1)}, u32[]{:S(2)}, u32[]{:S(2)}) collective-permute-start(bf16[288,256]{1,0:T(8,128)(2,1)S(1)} %extend.1), channel_id=1, source_target_pairs={{0,1},{1,0},{2,3},{3,2},{4,5},{5,4},{6,7},{7,6},{8,9},{9,8},{10,11... | collective-permute-start | bytes 442376 | tf_op jit(solution)/shard_map/ppermute | solution.py:47
  39.3 5.9 %collective-permute-start.10 = (bf16[256,256]{1,0:T(8,128)(2,1)S(1)}, bf16[256,256]{1,0:T(8,128)(2,1)S(1)}, u32[]{:S(2)}, u32[]{:S(2)}) collective-permute-start(bf16[256,256]{1,0:T(8,128)(2,1)S(1)} %get-tuple-element.44.refs_4_), channel_id=1, source_target_pairs={{0,1},{1,0},{2,3},{3,2},{4,5},{5,4},{6,7},{7,6},{8,9},{9,8},{10,11... | collective-permute-start | bytes 393224 | tf_op jit(solution)/shard_map/ppermute | solution.py:47
  41.7 3.5 %collective-permute-start.12 = (bf16[256,256]{1,0:T(8,128)(2,1)S(1)}, bf16[256,256]{1,0:T(8,128)(2,1)S(1)}, u32[]{:S(2)}, u32[]{:S(2)}) collective-permute-start(bf16[256,256]{1,0:T(8,128)(2,1)S(1)} %collective-permute-done.11.refs_5_), channel_id=1, source_target_pairs={{0,1},{1,0},{2,3},{3,2},{4,5},{5,4},{6,7},{7,6},{8,9},{9,8},{10,11... | collective-permute-start | bytes 393224 | tf_op jit(solution)/shard_map/ppermute | solution.py:47
  41.7 3.5 %collective-permute-start.14 = (bf16[256,256]{1,0:T(8,128)(2,1)S(1)}, bf16[256,256]{1,0:T(8,128)(2,1)S(1)}, u32[]{:S(2)}, u32[]{:S(2)}) collective-permute-start(bf16[256,256]{1,0:T(8,128)(2,1)S(1)} %collective-permute-done.13.refs_6_), channel_id=1, source_target_pairs={{0,1},{1,0},{2,3},{3,2},{4,5},{5,4},{6,7},{7,6},{8,9},{9,8},{10,11... | collective-permute-start | bytes 393224 | tf_op jit(solution)/shard_map/ppermute | solution.py:47
  45.1 7.3 %collective-permute-start.22 = (bf16[272,256]{1,0:T(8,128)(2,1)S(1)}, bf16[272,256]{1,0:T(8,128)(2,1)S(1)}, u32[]{:S(2)}, u32[]{:S(2)}) collective-permute-start(bf16[272,256]{1,0:T(8,128)(2,1)S(1)} %line_grads.2.refs_0_), channel_id=1, source_target_pairs={{0,8},{8,0},{16,24},{24,16},{1,9},{9,1},{17,25},{25,17},{2,10},{10... | collective-permute-start | bytes 417800 | tf_op jit(solution)/shard_map/ppermute | solution.py:47
  47.1 8.9 %collective-permute-start.17 = (bf16[256,256]{1,0:T(8,128)(2,1)S(1)}, bf16[256,256]{1,0:T(8,128)(2,1)S(1)}, u32[]{:S(2)}, u32[]{:S(2)}) collective-permute-start(bf16[256,256]{1,0:T(8,128)(2,1)S(1)} %get-tuple-element.46), channel_id=1, source_target_pairs={{0,8},{8,0},{16,24},{24,16},{1,9},{9,1},{17,25},{25,17},{2,10},{10... | collective-permute-start | bytes 393224 | tf_op jit(solution)/shard_map/ppermute | solution.py:47
  49.2 11.6 %collective-permute-start.18 = (bf16[256,256]{1,0:T(8,128)(2,1)S(1)}, bf16[256,256]{1,0:T(8,128)(2,1)S(1)}, u32[]{:S(2)}, u32[]{:S(2)}) collective-permute-start(bf16[256,256]{1,0:T(8,128)(2,1)S(1)} %get-tuple-element.47), channel_id=1, source_target_pairs={{0,16},{8,24},{16,0},{24,8},{1,17},{9,25},{17,1},{25,9},{2,18},{10... | collective-permute-start | bytes 393224 | tf_op jit(solution)/shard_map/ppermute | solution.py:47
  49.7 11.1 %collective-permute-start.19 = (bf16[256,256]{1,0:T(8,128)(2,1)S(1)}, bf16[256,256]{1,0:T(8,128)(2,1)S(1)}, u32[]{:S(2)}, u32[]{:S(2)}) collective-permute-start(bf16[256,256]{1,0:T(8,128)(2,1)S(1)} %get-tuple-element.48), channel_id=1, source_target_pairs={{0,24},{8,16},{16,8},{24,0},{1,25},{9,17},{17,9},{25,1},{2,26},{10... | collective-permute-start | bytes 393224 | tf_op jit(solution)/shard_map/ppermute | solution.py:47
  52.5 9.2 %collective-permute-start.23 = (bf16[272,256]{1,0:T(8,128)(2,1)S(1)}, bf16[272,256]{1,0:T(8,128)(2,1)S(1)}, u32[]{:S(2)}, u32[]{:S(2)}) collective-permute-start(bf16[272,256]{1,0:T(8,128)(2,1)S(1)} %line_grads.3.refs_0_), channel_id=1, source_target_pairs={{0,2},{1,3},{2,0},{3,1},{4,6},{5,7},{6,4},{7,5},{8,10},{9,11},{10,... | collective-permute-start | bytes 417800 | tf_op jit(solution)/shard_map/ppermute | solution.py:47
  54.0 7.7 %collective-permute-start.24 = (bf16[272,256]{1,0:T(8,128)(2,1)S(1)}, bf16[272,256]{1,0:T(8,128)(2,1)S(1)}, u32[]{:S(2)}, u32[]{:S(2)}) collective-permute-start(bf16[272,256]{1,0:T(8,128)(2,1)S(1)} %line_grads.3.refs_0_), channel_id=1, source_target_pairs={{0,4},{1,5},{2,6},{3,7},{4,0},{5,1},{6,2},{7,3},{8,12},{9,13},{10,... | collective-permute-start | bytes 417800 | tf_op jit(solution)/shard_map/ppermute | solution.py:47
  56.0 6.0 %collective-permute-start.25 = (bf16[272,256]{1,0:T(8,128)(2,1)S(1)}, bf16[272,256]{1,0:T(8,128)(2,1)S(1)}, u32[]{:S(2)}, u32[]{:S(2)}) collective-permute-start(bf16[272,256]{1,0:T(8,128)(2,1)S(1)} %line_grads.3.refs_0_), channel_id=1, source_target_pairs={{0,6},{1,7},{2,4},{3,5},{4,2},{5,3},{6,0},{7,1},{8,14},{9,15},{10,... | collective-permute-start | bytes 417800 | tf_op jit(solution)/shard_map/ppermute | solution.py:47
  61.7 1.4 %collective-permute-start.28 = (bf16[304,256]{1,0:T(8,128)(2,1)S(1)}, bf16[304,256]{1,0:T(8,128)(2,1)S(1)}, u32[]{:S(2)}, u32[]{:S(2)}) collective-permute-start(bf16[304,256]{1,0:T(8,128)(2,1)S(1)} %get-tuple-element.55), channel_id=1, source_target_pairs={{0,1},{1,0},{2,3},{3,2},{4,5},{5,4},{6,7},{7,6},{8,9},{9,8},{10,11... | collective-permute-start | bytes 466952 | tf_op jit(solution)/shard_map/ppermute | solution.py:47
  62.0 1.4 %collective-permute-start.26 = (f32[128,256]{1,0:T(8,128)S(1)}, f32[128,256]{1,0:T(8,128)S(1)}, u32[]{:S(2)}, u32[]{:S(2)}) collective-permute-start(f32[128,256]{1,0:T(8,128)S(1)} %get-tuple-element.52.refs_0_), channel_id=1, source_target_pairs={{0,1},{1,0},{2,3},{3,2},{4,5},{5,4},{6,7},{7,6},{8,9},{9,8},{10,11... | collective-permute-start | bytes 393224 | tf_op jit(solution)/shard_map/ppermute | solution.py:47
  62.4 1.3 %collective-permute-start.27 = (f32[128,256]{1,0:T(8,128)S(1)}, f32[128,256]{1,0:T(8,128)S(1)}, u32[]{:S(2)}, u32[]{:S(2)}) collective-permute-start(f32[128,256]{1,0:T(8,128)S(1)} %get-tuple-element.53.refs_1_), channel_id=1, source_target_pairs={{0,1},{1,0},{2,3},{3,2},{4,5},{5,4},{6,7},{7,6},{8,9},{9,8},{10,11... | collective-permute-start | bytes 393224 | tf_op jit(solution)/shard_map/ppermute | solution.py:47
